TPU v7x, 128 devices: a whole 4x4x4 slice. The times are simulated.
128 devices in a mesh: dp: 32 (over z, x, y_hi), mp: 4 (over y_lo, core).
Axes of the slice: x: 4, y: 4 (y_hi: 2, y_lo: 2; y = y_hi * 2 + y_lo), z: 4, core: 2. Of those that a mesh axis runs over, the one named last changes fastest.
Arguments:
- image_pool: bfloat16 [32768, 1152], P(('dp', 'mp')), may hold values from -6 to 6
- text_pool: bfloat16 [32768, 1152], P(('dp', 'mp')), may hold values from -6 to 6
- image_head: bfloat16 [1152, 1152], P(None, 'mp'), may hold values from -0.1875 to 0.1875
- text_head: bfloat16 [1152, 1152], P(None, 'mp'), may hold values from -0.1875 to 0.1875
- logit_scale: float32 [1], replicated, may hold values from 8 to 12
- logit_bias: float32 [1], replicated, may hold values from -1.5 to -0.5
Outputs:
- grad_image: bfloat16 [32768, 1152], P(('dp', 'mp'))
- grad_text: bfloat16 [32768, 1152], P(('dp', 'mp'))
- grad_image_head: float32 [1152, 1152], P(None, 'mp')
- grad_text_head: float32 [1152, 1152], P(None, 'mp')
All inputs are finite; a program needn't handle non-finite values.
Results may differ from a plain program's by a relative error of at most 0.008.
Values may be sent and summed in bfloat16 or wider, within the bound.
No kernel may reach another device: no remote copies, remote signals or barrier semaphores. Data moves between devices by JAX's collectives and lax.ppermute only.
A program may use at most 128 MiB of HBM per device.

v0:
```python
import jax
import jax.numpy as jnp
from jax import lax
from jax.sharding import PartitionSpec as P

WIN = 4


def shifted(block, axis, distance):
    devices = range(lax.axis_size(axis))
    route = [((i - distance) % len(devices), i) for i in devices]
    return lax.ppermute(block, axis, route)


def embed(pooled, head):
    raw = jnp.dot(pooled, head, preferred_element_type=jnp.float32)
    inverse = lax.rsqrt(jnp.sum(raw * raw, axis=1, keepdims=True) + 1e-06)
    return (raw * inverse, inverse)


def unembed(grads, unit, inverse):
    inner = jnp.sum(unit * grads, axis=1, keepdims=True)
    return ((grads - unit * inner) * inverse).astype(jnp.bfloat16)


def contract_rows(left, right):
    return lax.dot_general(
        left, right, (((0,), (0,)), ((), ())), preferred_element_type=jnp.float32
    )


def contract_cols(left, right):
    return lax.dot_general(
        left, right, (((1,), (1,)), ((), ())), preferred_element_type=jnp.float32
    )


def body(image_pool, text_pool, image_head, text_head, logit_scale, logit_bias):
    image_full, text_full = (
        lax.all_gather(image_head, "mp", axis=1, tiled=True),
        lax.all_gather(text_head, "mp", axis=1, tiled=True),
    )
    image_unit, image_inv = embed(image_pool, image_full)
    text_unit, text_inv = embed(text_pool, text_full)
    image_emb = image_unit.astype(jnp.bfloat16)
    text_share = text_unit.astype(jnp.bfloat16)
    scale = logit_scale[0]
    bias = logit_bias[0]
    rows = image_pool.shape[0]
    block = rows * lax.axis_size("mp")
    weight_c = 1.0 / (WIN * block)
    member = lax.axis_index("mp")
    row_ids = lax.broadcasted_iota(jnp.int32, (rows, block), 0) + member * rows
    col_ids = lax.broadcasted_iota(jnp.int32, (rows, block), 1)
    labels = (row_ids == col_ids).astype(jnp.float32)
    grad_x = jnp.zeros((rows, image_pool.shape[1]), jnp.float32)
    carried = None
    text_block = None
    text_block = lax.all_gather(text_share, "mp", axis=0, tiled=True)
    for step in range(WIN):
        if step > 0:
            text_block = shifted(text_block, "dp", 1)
        score = scale * contract_cols(image_emb, text_block) + bias
        target = labels if step == 0 else jnp.zeros_like(labels)
        tile = (weight_c * (jax.nn.sigmoid(score) - target)).astype(jnp.bfloat16)
        grad_x = grad_x + scale * jnp.dot(tile, text_block, preferred_element_type=jnp.float32)
        partial_grad = scale * contract_rows(tile, image_emb)
        if step == 0:
            carried = partial_grad
        else:
            carried = shifted(carried, "dp", 1) + partial_grad
    carried = shifted(carried, "dp", -(WIN - 1))
    grad_y = lax.psum_scatter(carried, "mp", scatter_dimension=0, tiled=True)
    raw_image = unembed(grad_x, image_unit, image_inv)
    raw_text = unembed(grad_y, text_unit, text_inv)
    grad_image = contract_cols(raw_image, image_full).astype(jnp.bfloat16)
    grad_text = contract_cols(raw_text, text_full).astype(jnp.bfloat16)
    columns = image_head.shape[1]
    image_part = contract_rows(image_pool, raw_image)
    text_part = contract_rows(text_pool, raw_text)
    image_sum, text_sum = lax.psum((image_part, text_part), ("dp", "mp"))
    grad_image_head = lax.dynamic_slice_in_dim(image_sum, member * columns, columns, 1)
    grad_text_head = lax.dynamic_slice_in_dim(text_sum, member * columns, columns, 1)
    return (grad_image, grad_text, grad_image_head, grad_text_head)


def solution(mesh):
    in_specs = (
        P(("dp", "mp"), None),
        P(("dp", "mp"), None),
        P(None, "mp"),
        P(None, "mp"),
        P(),
        P(),
    )
    out_specs = (P(("dp", "mp"), None), P(("dp", "mp"), None), P(None, "mp"), P(None, "mp"))
    return jax.shard_map(body, mesh=mesh, in_specs=in_specs, out_specs=out_specs, check_vma=False)
```

profile of v0, /device:TPU:1, one launch (start us, length us, event | category | flops | bytes accessed | tf_op | source)
XLA Modules:
  0.0 940.2 jit_solution(6054623781068578863)
XLA Ops:
  8.7 38.4 %all-gather.6.cloned.1.call-done = bf16[1152,1152]{0,1:T(8,128)(2,1)} async-done(((bf16[1152,288]{0,1:T(8,128)(2,1)}), bf16[1152,1152]{0,1:T(8,128)(2,1)}) %all-gather.6.cloned.1.call-update) | async-done | bytes 2654224 | tf_op jit(solution)/shard_map/all_gather | solution.py:41
  47.1 3.1 multiply_reduce_fusion.2
  50.2 1.0 multiply_convert_fusion.2
  52.5 30.9 %all-gather.4.cloned.1.call-done = bf16[1152,1152]{0,1:T(8,128)(2,1)} async-done(((bf16[1152,288]{0,1:T(8,128)(2,1)}), bf16[1152,1152]{0,1:T(8,128)(2,1)}) %all-gather.4.cloned.1.call-update) | async-done | bytes 2654224 | tf_op jit(solution)/shard_map/all_gather | solution.py:40
  83.4 2.9 multiply_reduce_fusion.3
  86.4 31.4 %all-gather.8.cloned.1.call-done = bf16[1024,1152]{1,0:T(8,128)(2,1)} async-done(((bf16[256,1152]{1,0:T(8,128)(2,1)}), bf16[1024,1152]{1,0:T(8,128)(2,1)}) %all-gather.8.cloned.1.call-update) | async-done | bytes 2359312 | tf_op jit(solution)/shard_map/all_gather | solution.py:59
  117.8 2.7 fusion.27
  120.6 0.9 convolution_multiply_fusion.3
  121.5 2.5 collective-permute-start.3
  124.0 1.4 collective-permute-start
  125.4 155.8 %collective-permute-done = bf16[1024,1152]{1,0:T(8,128)(2,1)S(1)} collective-permute-done((bf16[1024,1152]{1,0:T(8,128)(2,1)S(1)}, bf16[1024,1152]{1,0:T(8,128)(2,1)S(1)}, u32[]{:S(2)}, u32[]{:S(2)}) %collective-permute-start) | collective-permute-done | bytes 2359328 | tf_op jit(solution)/shard_map/ppermute | solution.py:12
  281.2 1.0 fusion.28
  282.2 0.9 fusion
  283.8 158.3 %collective-permute-done.1 = bf16[1024,1152]{1,0:T(8,128)(2,1)S(1)} collective-permute-done((bf16[1024,1152]{1,0:T(8,128)(2,1)S(1)}, bf16[1024,1152]{1,0:T(8,128)(2,1)S(1)}, u32[]{:S(2)}, u32[]{:S(2)}) %collective-permute-start.1) | collective-permute-done | bytes 2359328 | tf_op jit(solution)/shard_map/ppermute | solution.py:12
  442.1 1.0 fusion.29
  443.1 0.9 convolution_multiply_fusion.1
  444.6 157.8 %collective-permute-done.2 = bf16[1024,1152]{1,0:T(8,128)(2,1)S(1)} collective-permute-done((bf16[1024,1152]{1,0:T(8,128)(2,1)S(1)}, bf16[1024,1152]{1,0:T(8,128)(2,1)S(1)}, u32[]{:S(2)}, u32[]{:S(2)}) %collective-permute-start.2) | collective-permute-done | bytes 2359328 | tf_op jit(solution)/shard_map/ppermute | solution.py:12
  602.4 1.0 fusion.30
  603.8 0.9 convolution_multiply_fusion
  605.5 103.2 %collective-permute-done.6 = f32[1024,1152]{1,0:T(8,128)} collective-permute-done((f32[1024,1152]{1,0:T(8,128)S(1)}, f32[1024,1152]{1,0:T(8,128)}, u32[]{:S(2)}, u32[]{:S(2)}) %collective-permute-start.6) | collective-permute-done | bytes 4718624 | tf_op jit(solution)/shard_map/ppermute | solution.py:12
  708.7 1.0 copy-done.7
  709.7 2.7 fusion.31
  714.2 0.9 convolution_add_fusion.1
  716.1 1.0 multiply_reduce_fusion.1
  717.3 3.3 convolution_bitcast_fusion.1
  720.7 38.1 %reduce-scatter.2.cloned.1.call-done = f32[256,1152]{1,0:T(8,128)} async-done(((f32[1024,1152]{1,0:T(8,128)}), f32[256,1152]{1,0:T(8,128)}) %reduce-scatter.2.cloned.1.call-update) | async-done | bytes 1179664 | tf_op jit(solution)/shard_map/reduce_scatter | solution.py:73
  758.7 1.6 multiply_reduce_fusion
  760.7 3.3 convolution_bitcast_fusion
  764.0 3.7 convolution_convert_fusion.1
  767.7 1.8 convolution_convert_fusion
  769.5 160.7 %all-reduce.3.cloned.1.call-done = (f32[1152,1152]{0,1:T(8,128)}, f32[1152,1152]{0,1:T(8,128)}) async-done(((f32[1152,1152]{0,1:T(8,128)}, f32[1152,1152]{0,1:T(8,128)}), (f32[1152,1152]{0,1:T(8,128)}, f32[1152,1152]{0,1:T(8,128)})) %all-reduce.3.cloned.1.call-update) | async-done | bytes 10616848 | tf_op jit(solution)/shard_map/psum | solution.py:81
  930.2 3.4 constant_dynamic-slice_fusion
  (64 shorter events, 7.6 us)
Async XLA Ops:
  7.2 76.2 %copy-start = (bf16[256,1152]{1,0:T(8,128)(2,1)S(1)}, bf16[256,1152]{1,0:T(8,128)(2,1)}, u32[]{:S(2)}) copy-start(bf16[256,1152]{1,0:T(8,128)(2,1)} %param.6) | copy-start | bytes 1769476
  7.2 39.9 %all-gather.6.cloned.1.call-start = ((), (), s32[]{:S(2)}) async-start(), calls=%async_computation.2 | async-start | bytes 3317760 | tf_op jit(solution)/shard_map/all_gather | solution.py:41
  7.9 75.5 %all-gather.4.cloned.1.call-start = ((), (), s32[]{:S(2)}) async-start(), calls=%async_computation.1 | async-start | bytes 3317760 | tf_op jit(solution)/shard_map/all_gather | solution.py:40
  8.7 109.1 %all-gather.8.cloned.1.call-start = ((), (), s32[]{:S(2)}) async-start(), calls=%async_computation.3 | async-start | bytes 2949120 | tf_op jit(solution)/shard_map/all_gather | solution.py:59
  51.1 707.6 %reduce-scatter.2.cloned.1.call-start = ((), (), s32[]{:S(2)}) async-start(), calls=%async_computation.4 | async-start | bytes 5898240 | tf_op jit(solution)/shard_map/reduce_scatter | solution.py:73
  120.5 0.9 copy-start.6
  120.5 3.4 copy-start.10
  121.5 160.8 %collective-permute-start.3 = (f32[1024,1152]{1,0:T(8,128)S(1)}, f32[1024,1152]{1,0:T(8,128)S(1)}, u32[]{:S(2)}, u32[]{:S(2)}) collective-permute-start(f32[1024,1152]{1,0:T(8,128)S(1)} %convolution_multiply_fusion.3), channel_id=1, source_target_pairs={{124,0},{0,4},{4,8},{8,12},{12,16},{16,20},{20,24},{24,28},{28,32}... | collective-permute-start | bytes 14155784 | tf_op jit(solution)/shard_map/ppermute | solution.py:12
  124.0 157.3 %collective-permute-start = (bf16[1024,1152]{1,0:T(8,128)(2,1)S(1)}, bf16[1024,1152]{1,0:T(8,128)(2,1)S(1)}, u32[]{:S(2)}, u32[]{:S(2)}) collective-permute-start(bf16[1024,1152]{1,0:T(8,128)(2,1)S(1)} %copy-done.10), channel_id=1, source_target_pairs={{124,0},{0,4},{4,8},{8,12},{12,16},{16,20},{20,24},{24,28},{28,32}... | collective-permute-start | bytes 7077896 | tf_op jit(solution)/shard_map/ppermute | solution.py:12
  281.2 2.0 copy-start.11
  282.2 0.9 copy-start.15
  283.2 160.8 %collective-permute-start.4 = (f32[1024,1152]{1,0:T(8,128)S(1)}, f32[1024,1152]{1,0:T(8,128)S(1)}, u32[]{:S(2)}, u32[]{:S(2)}) collective-permute-start(f32[1024,1152]{1,0:T(8,128)S(1)} %fusion), channel_id=1, source_target_pairs={{124,0},{0,4},{4,8},{8,12},{12,16},{16,20},{20,24},{24,28},{28,32}... | collective-permute-start | bytes 14155784 | tf_op jit(solution)/shard_map/ppermute | solution.py:12
  283.3 158.8 %collective-permute-start.1 = (bf16[1024,1152]{1,0:T(8,128)(2,1)S(1)}, bf16[1024,1152]{1,0:T(8,128)(2,1)S(1)}, u32[]{:S(2)}, u32[]{:S(2)}) collective-permute-start(bf16[1024,1152]{1,0:T(8,128)(2,1)S(1)} %collective-permute-done), channel_id=1, source_target_pairs={{124,0},{0,4},{4,8},{8,12},{12,16},{16,20},{20,24},{24,28},{28,32}... | collective-permute-start | bytes 7077896 | tf_op jit(solution)/shard_map/ppermute | solution.py:12
  442.1 2.5 copy-start.13
  443.0 0.9 copy-start.2
  444.5 160.3 %collective-permute-start.5 = (f32[1024,1152]{1,0:T(8,128)S(1)}, f32[1024,1152]{1,0:T(8,128)S(1)}, u32[]{:S(2)}, u32[]{:S(2)}) collective-permute-start(f32[1024,1152]{1,0:T(8,128)S(1)} %add.98), channel_id=1, source_target_pairs={{124,0},{0,4},{4,8},{8,12},{12,16},{16,20},{20,24},{24,28},{28,32}... | collective-permute-start | bytes 14155784 | tf_op jit(solution)/shard_map/ppermute | solution.py:12
  444.5 157.9 %collective-permute-start.2 = (bf16[1024,1152]{1,0:T(8,128)(2,1)S(1)}, bf16[1024,1152]{1,0:T(8,128)(2,1)S(1)}, u32[]{:S(2)}, u32[]{:S(2)}) collective-permute-start(bf16[1024,1152]{1,0:T(8,128)(2,1)S(1)} %collective-permute-done.1), channel_id=1, source_target_pairs={{124,0},{0,4},{4,8},{8,12},{12,16},{16,20},{20,24},{24,28},{28,32}... | collective-permute-start | bytes 7077896 | tf_op jit(solution)/shard_map/ppermute | solution.py:12
  602.4 1.4 copy-start.8
  603.8 0.9 copy-start.4
  605.2 103.4 %collective-permute-start.6 = (f32[1024,1152]{1,0:T(8,128)S(1)}, f32[1024,1152]{1,0:T(8,128)}, u32[]{:S(2)}, u32[]{:S(2)}) collective-permute-start(f32[1024,1152]{1,0:T(8,128)S(1)} %add.99), channel_id=1, source_target_pairs={{12,0},{16,4},{20,8},{24,12},{28,16},{32,20},{36,24},{40,28},{44,3... | collective-permute-start | bytes 14155784 | tf_op jit(solution)/shard_map/ppermute | solution.py:12
  708.6 1.0 copy-start.7
  708.7 221.6 %all-reduce.3.cloned.1.call-start = ((), (), s32[]{:S(2)}) async-start(), calls=%async_computation.5 | async-start | bytes 21233664 | tf_op jit(solution)/shard_map/psum | solution.py:81
  709.7 2.7 copy-start.12
  709.7 2.7 copy-start.16
  712.4 1.0 copy-start.3
  712.4 1.8 copy-start.14
  714.2 1.0 copy-start.5
  714.2 1.8 copy-start.9
  720.7 40.0 %copy-start.17 = (bf16[256,1152]{1,0:T(8,128)(2,1)S(1)}, bf16[256,1152]{1,0:T(8,128)(2,1)}, u32[]{:S(2)}) copy-start(bf16[256,1152]{1,0:T(8,128)(2,1)} %param.7) | copy-start | bytes 1769476
  758.7 1.6 copy-start.1
  764.0 3.7 copy-start.18
Sparse Core Ops, SparseCore 0:
  9.7 37.3 all-gather.5
  48.7 34.5 all-gather.3
  85.6 32.1 all-gather.7
  708.8 49.8 reduce-scatter.1
  764.1 166.1 all-reduce.2
where the time goes:
time: 941 us; the launch traced here: 940 us
  waiting for transfers between devices  876 us (93%)
  matrix products  32.7 us (3%)
  between operations  15.4 us (2%)
    ppermute x7, waiting for transfers between devices, shifted(): return lax.ppermute(block, axis, route)  575 us
    psum x1, waiting for transfers between devices, body(): image_sum, text_sum = lax.psum((image_part, text_part), ('dp', 'mp'))  161 us
    all_gather x1, waiting for transfers between devices, body(): lax.all_gather(text_head, 'mp', axis=1, tiled=True)  38.4 us
    reduce_scatter x1, waiting for transfers between devices, body(): grad_y = lax.psum_scatter(carried, 'mp', scatter_dimension=0, tiled=True)  38.1 us
    all_gather x1, waiting for transfers between devices, body(): text_block = lax.all_gather(text_share, 'mp', axis=0, tiled=True)  31.4 us
    all_gather x1, waiting for transfers between devices, body(): lax.all_gather(image_head, 'mp', axis=1, tiled=True)  30.9 us
  transfers between devices with their start and end apart: 12, of which 9 were waited for; matrix products, arithmetic and copies ran while one was open for 3% of the time, Pallas kernels for 0%

commit v1 on v0

v1 whole, which is shorter than its diff:
```python
import jax
import jax.numpy as jnp
from jax import lax
from jax.sharding import Mesh, PartitionSpec as P

WIN = 4
AXES = ("z", "x", "yh", "yl", "core")
SIZES = (4, 4, 2, 2, 2)
BF = jnp.bfloat16
F32 = jnp.float32


def flat(z, x, y, core):
    return (((z % 4) * 4 + x % 4) * 4 + y % 4) * 2 + core


def moved(block, route):
    pairs = []
    for z in range(4):
        for x in range(4):
            for y in range(4):
                for core in range(2):
                    place = route(z, x, y, core)
                    if place is not None:
                        pairs.append((flat(z, x, y, core), flat(*place)))
    return lax.ppermute(block, AXES, pairs)


def hop(dz=0, dx=0, dy=0, swap=0):
    return lambda z, x, y, core: (z + dz, x + dx, y + dy, core ^ swap)


def collect(step, parity=None, direct=False):
    def route(z, x, y, core):
        role = core ^ 1 if direct else core
        if role:
            z, x, y = 3 - z, 3 - x, 3 - y
        column, odd, half = z * 4 + x, y // 2, y % 2
        if parity is not None and odd != parity:
            return None
        if step == "half":
            half = 1 - half
        elif step == "column":
            column = (column + 1) % 16
        elif step == "cross":
            odd, half = 1 - odd, 1 - half
        z, x, y = column // 4, column % 4, odd * 2 + half
        if role:
            z, x, y = 3 - z, 3 - x, 3 - y
        return (z, x, y, role)

    return route


def dot_nt(left, right):
    return lax.dot_general(
        left, right, (((1,), (1,)), ((), ())), preferred_element_type=F32
    )


def dot_nn(left, right):
    return jnp.dot(left, right, preferred_element_type=F32)


def body(image_pool, text_pool, image_head, text_head, logit_scale, logit_bias):
    core = lax.axis_index("core")
    half = lax.axis_index("yl")
    odd = lax.axis_index("yh")
    plane = lax.axis_index("z")
    first = core == 0
    scale = logit_scale[0]
    bias = logit_bias[0]
    rows, width = image_pool.shape
    columns = image_head.shape[1]
    weight_c = 1.0 / (WIN * 4 * rows)

    head_own = jnp.where(first, image_head, text_head).T
    head_other = jnp.where(first, text_head, image_head).T
    pool_own = jnp.where(first, image_pool, text_pool)
    pool_other = jnp.where(first, text_pool, image_pool)
    head_up = moved(head_own, hop(dy=1))
    head_down = moved(head_other, hop(dy=-1, swap=1))
    head_mate = moved(head_other, hop(swap=1))
    pool_mate = moved(pool_other, hop(swap=1))
    pool = jnp.concatenate([pool_own, pool_mate], axis=0)
    head = jnp.zeros((4 * columns, width), BF)
    far = 1 - half
    for part, place in (
        (head_own, 2 * half + core),
        (head_mate, 2 * half + 1 - core),
        (head_up, 2 * far + core),
        (head_down, 2 * far + 1 - core),
    ):
        head = lax.dynamic_update_slice(head, part, (place * columns, 0))

    raw = dot_nt(pool, head)
    inverse = lax.rsqrt(jnp.sum(raw * raw, axis=1, keepdims=True) + 1e-06)
    unit = raw * inverse
    emb = unit.astype(BF)

    pool_z1 = moved(pool, hop(dz=1))
    pool_z3 = moved(pool, hop(dz=-1))

    count = 2 * rows
    ids = lax.broadcasted_iota(jnp.int32, (count, count), 0)
    jds = lax.broadcasted_iota(jnp.int32, (count, count), 1)
    label = (ids == (jds + rows) % count).astype(F32)

    def term(other, target=0.0):
        score = scale * dot_nt(emb, other) + bias
        tile = (weight_c * (jax.nn.sigmoid(score) - target)).astype(BF)
        return dot_nn(tile, other)

    b0n = moved(emb, collect("same", direct=True))
    b2n = moved(emb, collect("column", direct=True))
    c1a = moved(emb, collect("cross", parity=0, direct=True))
    b0f = moved(emb, collect("half", direct=True))
    grad = term(b0n, label)
    grad = grad + term(b2n)
    c1b = moved(b2n, collect("cross", parity=1))
    x3o = moved(c1a, collect("column", parity=1))
    b2f = moved(b0f, collect("column"))
    c2a = moved(b0f, collect("cross", parity=0))
    grad = grad + term(b0f)
    is_odd = jnp.where(first, odd, 1 - odd) == 1
    b1f = jnp.where(is_odd, c1a, c1b)
    x3e = moved(c1b, collect("column", parity=0))
    grad = grad + term(b1f)
    c2b = moved(b2f, collect("cross", parity=1))
    grad = grad + term(b2f)
    b3f = jnp.where(is_odd, x3o, x3e)
    b3n = moved(b3f, collect("half"))
    grad = grad + term(b3f)
    b1n = jnp.where(is_odd, c2a, c2b)
    grad = grad + term(b1n)
    pool_late, b3f = lax.optimization_barrier((pool, b3f))
    pool_z2 = moved(pool_late, hop(dz=2))
    grad = scale * (grad + term(b3n))

    inner = jnp.sum(unit * grad, axis=1, keepdims=True)
    raw_grad = ((grad - unit * inner) * inverse).astype(BF)

    piece = columns // 4
    turned = raw_grad.T.reshape(4, 4, piece, count)

    def slice_of(place):
        return lax.dynamic_index_in_dim(turned, place % 4, 1, False).reshape(columns, count)

    part1 = moved(slice_of(plane + 1), hop(dz=1))
    part3 = moved(slice_of(plane + 3), hop(dz=-1))
    part2 = moved(slice_of(plane + 2), hop(dz=2))
    grad_pool = dot_nn(raw_grad, head).astype(BF)
    pool_back = moved(grad_pool[rows:], hop(swap=1))
    grad_image = jnp.where(first, grad_pool[:rows], pool_back)
    grad_text = jnp.where(first, pool_back, grad_pool[:rows])
    total = dot_nn(slice_of(plane), pool) + dot_nn(part1, pool_z1)
    total = total + dot_nn(part3, pool_z3) + dot_nn(part2, pool_z2)
    total = total.reshape(4, piece, width)

    def shard_for(yh, yl):
        return lax.dynamic_index_in_dim(total, 2 * yl + yh, 0, False)

    up_h = jnp.where(half == 1, 1 - odd, odd)
    down_h = jnp.where(half == 0, 1 - odd, odd)
    got = [
        moved(shard_for(up_h, 1 - half).astype(BF), hop(dy=1)),
        moved(shard_for(down_h, 1 - half).astype(BF), hop(dy=-1)),
        moved(shard_for(1 - odd, half).astype(BF), hop(dy=2)),
    ]
    mine = shard_for(odd, half)
    for part in got:
        mine = mine + part.astype(F32)
    narrow = mine.astype(BF)
    for part in [moved(narrow, hop(dx=1)), moved(narrow, hop(dx=-1)), moved(narrow, hop(dx=2))]:
        mine = mine + part.astype(F32)
    narrow = mine.astype(BF)
    across = moved(narrow, hop(dy=2))
    low = jnp.where(odd == 0, narrow, across)
    high = jnp.where(odd == 0, across, narrow)
    pair = jnp.stack([low, high])
    ring = [pair, moved(pair, hop(dz=-1)), moved(pair, hop(dz=2)), moved(pair, hop(dz=1))]
    ring = jnp.stack(ring + ring, axis=1)
    ring = lax.dynamic_slice_in_dim(ring, 4 - plane, 4, 1)
    ring = ring.reshape(2, columns, width)
    keep = lax.dynamic_index_in_dim(ring, core, 0, False)
    give = lax.dynamic_index_in_dim(ring, 1 - core, 0, False)
    back = moved(give, hop(swap=1))
    head_image = jnp.where(first, keep, back).astype(F32).T
    head_text = jnp.where(first, back, keep).astype(F32).T
    return (grad_image, grad_text, head_image, head_text)


def solution(mesh):
    fine = Mesh(mesh.devices.reshape(SIZES), AXES)
    rows = P(AXES, None)
    cols = P(None, ("yl", "core"))
    return jax.shard_map(
        body,
        mesh=fine,
        in_specs=(rows, rows, cols, cols, P(), P()),
        out_specs=(rows, rows, cols, cols),
        check_vma=False,
    )
```

time: 941 us -> 230 us (0.24)
  waiting for transfers between devices: 876 us -> 86 us
  starting transfers between devices: 5.15 us -> 57.7 us
  matrix products: 32.7 us -> 59.3 us
  between operations: 15.4 us -> 2.28 us
  other arithmetic: 4.23 us -> 14.1 us
    ppermute x7 -> x33, waiting for transfers between devices: 575 us -> 86 us  [moved(): return lax.ppermute(block, AXES, pairs)]
    psum x1 -> x0, waiting for transfers between devices: 161 us -> none  [body(): image_sum, text_sum = lax.psum((image_part, text_part), ('dp', 'mp'))]
    all_gather x3 -> x0, waiting for transfers between devices: 101 us -> none  [the longest x1 38.4 us: body(): lax.all_gather(text_head, 'mp', axis=1, tiled=True)]
    ppermute x7 -> x33, starting transfers between devices: 4.95 us -> 57.7 us  [moved(): return lax.ppermute(block, AXES, pairs)]
    reduce_scatter x1 -> x0, waiting for transfers between devices: 38.1 us -> none  [body(): grad_y = lax.psum_scatter(carried, 'mp', scatter_dimension=0, tiled=True)]
    dot_general x18 -> x14, matrix products: 32.7 us -> 59.3 us  [the longest x13 55.4 us: dot_nn(): return jnp.dot(left, right, preferred_element_type=F32)]
  transfers between devices with their start and end apart: 12 -> 33, of which waited for: 9 -> 15; matrix products, arithmetic and copies ran while one was open for 3% -> 30% of each run, Pallas kernels for 0% -> 0%
where the time goes in v1:
time: 230 us; the launch traced here: 229 us
  waiting for transfers between devices  86 us (37%)
  matrix products  59.3 us (26%)
  starting transfers between devices  57.7 us (25%)
  other arithmetic  14.1 us (6%)
  local copies, waits for them, and re-layouts  9.36 us (4%)
    ppermute x33, waiting for transfers between devices, moved(): return lax.ppermute(block, AXES, pairs)  86 us
    ppermute x33, starting transfers between devices, moved(): return lax.ppermute(block, AXES, pairs)  57.7 us
    dot_general x13, matrix products, dot_nn(): return jnp.dot(left, right, preferred_element_type=F32)  55.4 us
  transfers between devices with their start and end apart: 33, of which 15 were waited for; matrix products, arithmetic and copies ran while one was open for 30% of the time, Pallas kernels for 0%

profile of v1, /device:TPU:1, one launch (start us, length us, event | category | flops | bytes accessed | tf_op | source)
XLA Modules:
  0.0 228.8 jit_solution(1480957650445593980)
XLA Ops:
  4.1 2.7 %collective-permute-start.3 = (bf16[288,1152]{1,0:T(8,128)(2,1)}, bf16[288,1152]{1,0:T(8,128)(2,1)S(1)}, u32[]{:S(2)}, u32[]{:S(2)}) collective-permute-start(bf16[288,1152]{1,0:T(8,128)(2,1)} %select_bitcast_fusion), channel_id=1, source_target_pairs={{0,7},{1,6},{2,1},{3,0},{4,3},{5,2},{6,5},{7,4},{8,15},{9,14},{10,... | collective-permute-start | bytes 1990664 | tf_op jit(solution)/shard_map/ppermute | solution.py:26
  13.0 15.0 %collective-permute-done.2 = bf16[288,1152]{1,0:T(8,128)(2,1)S(1)} collective-permute-done((bf16[288,1152]{1,0:T(8,128)(2,1)}, bf16[288,1152]{1,0:T(8,128)(2,1)S(1)}, u32[]{:S(2)}, u32[]{:S(2)}) %collective-permute-start.2) | collective-permute-done | bytes 663584 | tf_op jit(solution)/shard_map/ppermute | solution.py:26
  29.8 3.9 %multiply_reduce_fusion.1 = (f32[512]{0:T(512)S(1)}, f32[512,1152]{1,0:T(8,128)S(1)}) fusion(bf16[1152,1152]{1,0:T(8,128)(2,1)} %constant_dynamic-update-slice_fusion, bf16[256,1152]{1,0:T(8,128)(2,1)S(1)} %collective-permute-done, bf16[256,1152]{1,0:T(8,128)(2,1)S(1)} %get-tuple-element.19), kind=kOutput, calls=%fused_computation.14 | convolution fusion | flops 1362492928 | bytes 6195200 | tf_op jit(solution)/shard_map/dot_general | solution.py:56
  37.5 2.9 %collective-permute-start.6 = (bf16[512,1152]{1,0:T(8,128)(2,1)}, bf16[512,1152]{1,0:T(8,128)(2,1)}, u32[]{:S(2)}, u32[]{:S(2)}) collective-permute-start(bf16[512,1152]{1,0:T(8,128)(2,1)} %multiply_convert_fusion.1), channel_id=1, source_target_pairs={{0,3},{1,2},{2,1},{3,0},{4,7},{5,6},{6,5},{7,4},{8,11},{9,10},{10,... | collective-permute-start | bytes 3538952 | tf_op jit(solution)/shard_map/ppermute | solution.py:26
  42.5 9.4 %collective-permute-done.5 = bf16[512,1152]{1,0:T(8,128)(2,1)} collective-permute-done((bf16[512,1152]{1,0:T(8,128)(2,1)}, bf16[512,1152]{1,0:T(8,128)(2,1)}, u32[]{:S(2)}, u32[]{:S(2)}) %collective-permute-start.5) | collective-permute-done | bytes 1179680 | tf_op jit(solution)/shard_map/ppermute | solution.py:26
  55.6 2.8 %collective-permute-start.4 = (bf16[512,1152]{1,0:T(8,128)(2,1)}, bf16[512,1152]{1,0:T(8,128)(2,1)}, u32[]{:S(2)}, u32[]{:S(2)}) collective-permute-start(bf16[512,1152]{1,0:T(8,128)(2,1)} %multiply_convert_fusion.1), channel_id=1, source_target_pairs={{0,1},{1,0},{2,3},{3,2},{4,5},{5,4},{6,7},{7,6},{8,9},{9,8},{10,11... | collective-permute-start | bytes 3538952 | tf_op jit(solution)/shard_map/ppermute | solution.py:26
  59.9 5.6 %collective-permute-done.6 = bf16[512,1152]{1,0:T(8,128)(2,1)} collective-permute-done((bf16[512,1152]{1,0:T(8,128)(2,1)}, bf16[512,1152]{1,0:T(8,128)(2,1)}, u32[]{:S(2)}, u32[]{:S(2)}) %collective-permute-start.6) | collective-permute-done | bytes 1179680 | tf_op jit(solution)/shard_map/ppermute | solution.py:26
  65.5 3.9 %collective-permute-start.9 = (bf16[512,1152]{1,0:T(8,128)(2,1)}, bf16[512,1152]{1,0:T(8,128)(2,1)}, u32[]{:S(2)}, u32[]{:S(2)}) collective-permute-start(bf16[512,1152]{1,0:T(8,128)(2,1)} %collective-permute-done.6), channel_id=1, source_target_pairs={{0,8},{1,121},{2,10},{3,123},{4,12},{5,125},{6,14},{7,127},{8,16},... | collective-permute-start | bytes 3538952 | tf_op jit(solution)/shard_map/ppermute | solution.py:26
  69.4 3.6 %collective-permute-start.10 = (bf16[512,1152]{1,0:T(8,128)(2,1)}, bf16[512,1152]{1,0:T(8,128)(2,1)S(1)}, u32[]{:S(2)}, u32[]{:S(2)}) collective-permute-start(bf16[512,1152]{1,0:T(8,128)(2,1)} %collective-permute-done.7), channel_id=1, source_target_pairs={{1,121},{3,123},{4,12},{6,14},{9,1},{11,3},{12,20},{14,22},{17,9},... | collective-permute-start | bytes 3538952 | tf_op jit(solution)/shard_map/ppermute | solution.py:26
  73.0 5.1 %fusion.68 = f32[512,1152]{1,0:T(8,128)} fusion(bf16[512,1152]{1,0:T(8,128)(2,1)} %collective-permute-done.5, bf16[512,1152]{1,0:T(8,128)(2,1)} %multiply_convert_fusion.1, f32[]{:T(128)} %bitcast.114, f32[]{:T(128)} %bitcast.106), kind=kOutput, calls=%fused_computation.87 | convolution fusion | flops 1209794560 | bytes 4718600 | tf_op jit(solution)/shard_map/dot_general | solution.py:62
  79.8 5.1 %fusion.67 = f32[512,1152]{1,0:T(8,128)} fusion(bf16[512,1152]{1,0:T(8,128)(2,1)} %collective-permute-done.6, bf16[512,1152]{1,0:T(8,128)(2,1)} %multiply_convert_fusion.1, f32[]{:T(128)} %bitcast.113, f32[]{:T(128)} %bitcast.105), kind=kOutput, calls=%fused_computation.86 | convolution fusion | flops 1209794560 | bytes 4718600 | tf_op jit(solution)/shard_map/dot_general | solution.py:62
  85.0 6.6 %fusion = f32[512,1152]{1,0:T(8,128)} fusion(f32[512,1152]{1,0:T(8,128)} %fusion.67, f32[512,1152]{1,0:T(8,128)} %fusion.68, bf16[512,1152]{1,0:T(8,128)(2,1)} %collective-permute-done.4, bf16[512,1152]{1,0:T(8,128)(2,1)} %multiply_convert_fusion.1, s32[512]{0:T(512)S(1)} %get-tuple-element.27, s32[512]{0:T(512)S(1)} %get-tuple-element.28, f32[]{:T(128)} %bitcast.107, ...), kind=kOutput, calls=%fused_computation.3 | convolution fusion | flops 1212022784 | bytes 9441800 | tf_op jit(solution)/shard_map/dot_general | solution.py:62
  92.9 5.2 %fusion.66 = f32[512,1152]{1,0:T(8,128)} fusion(bf16[512,1152]{1,0:T(8,128)(2,1)} %collective-permute-done.9, bf16[512,1152]{1,0:T(8,128)(2,1)} %multiply_convert_fusion.1, f32[]{:T(128)} %bitcast.111, f32[]{:T(128)} %bitcast.103), kind=kOutput, calls=%fused_computation.85 | convolution fusion | flops 1209794560 | bytes 4718600 | tf_op jit(solution)/shard_map/dot_general | solution.py:62
  98.1 7.3 %collective-permute-start.13 = (bf16[512,1152]{1,0:T(8,128)(2,1)}, bf16[512,1152]{1,0:T(8,128)(2,1)}, u32[]{:S(2)}, u32[]{:S(2)}) collective-permute-start(bf16[512,1152]{1,0:T(8,128)(2,1)} %collective-permute-done.9), channel_id=1, source_target_pairs={{1,7},{3,5},{4,2},{6,0},{9,15},{11,13},{12,10},{14,8},{17,23},{19,... | collective-permute-start | bytes 3538952 | tf_op jit(solution)/shard_map/ppermute | solution.py:26
  106.8 6.7 %fusion.1 = f32[512,1152]{1,0:T(8,128)} fusion(f32[512,1152]{1,0:T(8,128)} %fusion.66, f32[512,1152]{1,0:T(8,128)} %fusion, bf16[512,1152]{1,0:T(8,128)(2,1)} %multiply_convert_fusion.1, bf16[512,1152]{1,0:T(8,128)(2,1)} %collective-permute-done.7, bf16[512,1152]{1,0:T(8,128)(2,1)} %collective-permute-done.8, pred[]{:T(512)S(6)} %eq.28, f32[]{:T(128)} %bitcast.112, ...), kind=kOutput, calls=%fused_computation.4 | convolution fusion | flops 1212153856 | bytes 10616841 | tf_op jit(solution)/shard_map/dot_general | solution.py:62
  114.8 4.4 %collective-permute-done.13 = bf16[512,1152]{1,0:T(8,128)(2,1)} collective-permute-done((bf16[512,1152]{1,0:T(8,128)(2,1)}, bf16[512,1152]{1,0:T(8,128)(2,1)}, u32[]{:S(2)}, u32[]{:S(2)}) %collective-permute-start.13) | collective-permute-done | bytes 1179680 | tf_op jit(solution)/shard_map/ppermute | solution.py:26
  119.2 5.1 %fusion.65 = f32[512,1152]{1,0:T(8,128)} fusion(bf16[512,1152]{1,0:T(8,128)(2,1)} %multiply_convert_fusion.1, bf16[512,1152]{1,0:T(8,128)(2,1)} %collective-permute-done.12, bf16[512,1152]{1,0:T(8,128)(2,1)} %collective-permute-done.13, pred[]{:T(512)S(6)} %eq.28, f32[]{:T(128)} %bitcast.109, f32[]{:T(128)} %bitcast.102), kind=kOutput, calls=%fused_computation.84 | convolution fusion | flops 1210974208 | bytes 5898249 | tf_op jit(solution)/shard_map/dot_general | solution.py:62
  124.4 6.4 %collective-permute-done.14 = bf16[512,1152]{1,0:T(8,128)(2,1)} collective-permute-done((bf16[512,1152]{1,0:T(8,128)(2,1)S(1)}, bf16[512,1152]{1,0:T(8,128)(2,1)}, u32[]{:S(2)}, u32[]{:S(2)}) %collective-permute-start.14) | collective-permute-done | bytes 1179680 | tf_op jit(solution)/shard_map/ppermute | solution.py:26
  130.8 5.2 %fusion.64 = f32[512,1152]{1,0:T(8,128)} fusion(bf16[512,1152]{1,0:T(8,128)(2,1)} %collective-permute-done.14, bf16[512,1152]{1,0:T(8,128)(2,1)} %multiply_convert_fusion.1, f32[]{:T(128)} %bitcast.108, f32[]{:T(128)} %bitcast.101), kind=kOutput, calls=%fused_computation.83 | convolution fusion | flops 1209794560 | bytes 4718600 | tf_op jit(solution)/shard_map/dot_general | solution.py:62
  135.9 6.8 %multiply_reduce_fusion = (f32[512]{0:T(512)S(1)}, f32[512,1152]{1,0:T(8,128)}) fusion(f32[512,1152]{1,0:T(8,128)S(1)} %get-tuple-element.24, f32[512]{0:T(512)S(1)} %add_rsqrt_fusion, f32[512,1152]{1,0:T(8,128)} %fusion.64, f32[512,1152]{1,0:T(8,128)} %fusion.65, f32[512,1152]{1,0:T(8,128)} %fusion.1, bf16[512,1152]{1,0:T(8,128)(2,1)S(1)} %broadcast_select_fusion, ...), kind=kOutput, calls=%fused_computation.13 | convolution fusion | flops 1213922816 | bytes 14159880 | tf_op jit(solution)/shard_map/dot_general | solution.py:62
  148.9 11.8 %collective-permute-done.16 = bf16[288,512]{1,0:T(8,128)(2,1)S(1)} collective-permute-done((bf16[288,512]{1,0:T(8,128)(2,1)S(1)}, bf16[288,512]{1,0:T(8,128)(2,1)S(1)}, u32[]{:S(2)}, u32[]{:S(2)}) %collective-permute-start.16) | collective-permute-done | bytes 294944 | tf_op jit(solution)/shard_map/ppermute | solution.py:26
  169.8 3.8 %collective-permute-done.22 = bf16[72,1152]{1,0:T(8,128)(2,1)S(1)} collective-permute-done((bf16[72,1152]{1,0:T(8,128)(2,1)S(1)}, bf16[72,1152]{1,0:T(8,128)(2,1)S(1)}, u32[]{:S(2)}, u32[]{:S(2)}) %collective-permute-start.22) | collective-permute-done | bytes 165920 | tf_op jit(solution)/shard_map/ppermute | solution.py:26
  174.4 3.1 %collective-permute-done.24 = bf16[72,1152]{1,0:T(8,128)(2,1)S(1)} collective-permute-done((bf16[72,1152]{1,0:T(8,128)(2,1)S(1)}, bf16[72,1152]{1,0:T(8,128)(2,1)S(1)}, u32[]{:S(2)}, u32[]{:S(2)}) %collective-permute-start.24) | collective-permute-done | bytes 165920 | tf_op jit(solution)/shard_map/ppermute | solution.py:26
  178.6 2.8 %collective-permute-start.26 = (bf16[72,1152]{1,0:T(8,128)(2,1)S(1)}, bf16[72,1152]{1,0:T(8,128)(2,1)S(1)}, u32[]{:S(2)}, u32[]{:S(2)}) collective-permute-start(bf16[72,1152]{1,0:T(8,128)(2,1)S(1)} %fusion.113), channel_id=1, source_target_pairs={{0,24},{1,25},{2,26},{3,27},{4,28},{5,29},{6,30},{7,31},{8,0},{9,1... | collective-permute-start | bytes 497672 | tf_op jit(solution)/shard_map/ppermute | solution.py:26
  181.4 3.1 %collective-permute-start.27 = (bf16[72,1152]{1,0:T(8,128)(2,1)S(1)}, bf16[72,1152]{1,0:T(8,128)(2,1)S(1)}, u32[]{:S(2)}, u32[]{:S(2)}) collective-permute-start(bf16[72,1152]{1,0:T(8,128)(2,1)S(1)} %fusion.113), channel_id=1, source_target_pairs={{0,16},{1,17},{2,18},{3,19},{4,20},{5,21},{6,22},{7,23},{8,24},{9,... | collective-permute-start | bytes 497672 | tf_op jit(solution)/shard_map/ppermute | solution.py:26
  185.7 2.7 %collective-permute-done.27 = bf16[72,1152]{1,0:T(8,128)(2,1)S(1)} collective-permute-done((bf16[72,1152]{1,0:T(8,128)(2,1)S(1)}, bf16[72,1152]{1,0:T(8,128)(2,1)S(1)}, u32[]{:S(2)}, u32[]{:S(2)}) %collective-permute-start.27) | collective-permute-done | bytes 165920 | tf_op jit(solution)/shard_map/ppermute | solution.py:26
  188.6 3.0 %collective-permute-start.28 = (bf16[72,1152]{1,0:T(8,128)(2,1)S(1)}, bf16[72,1152]{1,0:T(8,128)(2,1)S(1)}, u32[]{:S(2)}, u32[]{:S(2)}) collective-permute-start(bf16[72,1152]{1,0:T(8,128)(2,1)S(1)} %add_convert_fusion), channel_id=1, source_target_pairs={{0,4},{1,5},{2,6},{3,7},{4,0},{5,1},{6,2},{7,3},{8,12},{9,13},{10,... | collective-permute-start | bytes 497672 | tf_op jit(solution)/shard_map/ppermute | solution.py:26
  191.7 2.8 %collective-permute-done.28 = bf16[72,1152]{1,0:T(8,128)(2,1)S(1)} collective-permute-done((bf16[72,1152]{1,0:T(8,128)(2,1)S(1)}, bf16[72,1152]{1,0:T(8,128)(2,1)S(1)}, u32[]{:S(2)}, u32[]{:S(2)}) %collective-permute-start.28) | collective-permute-done | bytes 165920 | tf_op jit(solution)/shard_map/ppermute | solution.py:26
  195.3 3.6 %convolution_convert_fusion = bf16[512,1152]{1,0:T(8,128)(2,1)S(1)} fusion(bf16[512,1152]{1,0:T(8,128)(2,1)S(1)} %multiply_convert_fusion, bf16[1152,1152]{1,0:T(8,128)(2,1)} %constant_dynamic-update-slice_fusion), kind=kOutput, calls=%fused_computation.8 | convolution fusion | flops 1359544320 | bytes 5013504 | tf_op jit(solution)/shard_map/dot_general | solution.py:62
  199.9 4.9 %collective-permute-start.15 = (bf16[256,1152]{1,0:T(8,128)(2,1)}, bf16[256,1152]{1,0:T(8,128)(2,1)}, u32[]{:S(2)}, u32[]{:S(2)}) collective-permute-start(bf16[256,1152]{1,0:T(8,128)(2,1)} %slice.10), channel_id=1, source_target_pairs={{0,1},{1,0},{2,3},{3,2},{4,5},{5,4},{6,7},{7,6},{8,9},{9,8},{10,11... | collective-permute-start | bytes 1769480 | tf_op jit(solution)/shard_map/ppermute | solution.py:26
  205.4 10.3 %collective-permute-done.30 = bf16[2,72,1152]{2,1,0:T(8,128)(2,1)S(1)} collective-permute-done((bf16[2,72,1152]{2,1,0:T(8,128)(2,1)S(1)}, bf16[2,72,1152]{2,1,0:T(8,128)(2,1)S(1)}, u32[]{:S(2)}, u32[]{:S(2)}) %collective-permute-start.30) | collective-permute-done | bytes 331808 | tf_op jit(solution)/shard_map/ppermute | solution.py:26
  215.8 7.4 %collective-permute-done.31 = bf16[2,72,1152]{2,1,0:T(8,128)(2,1)S(1)} collective-permute-done((bf16[2,72,1152]{2,1,0:T(8,128)(2,1)S(1)}, bf16[2,72,1152]{2,1,0:T(8,128)(2,1)S(1)}, u32[]{:S(2)}, u32[]{:S(2)}) %collective-permute-start.31) | collective-permute-done | bytes 331808 | tf_op jit(solution)/shard_map/ppermute | solution.py:26
  (106 shorter events, 53.7 us)
Async XLA Ops:
  2.7 9.4 %collective-permute-start.1 = (bf16[288,1152]{1,0:T(8,128)(2,1)}, bf16[288,1152]{1,0:T(8,128)(2,1)S(1)}, u32[]{:S(2)}, u32[]{:S(2)}) collective-permute-start(bf16[288,1152]{1,0:T(8,128)(2,1)} %select_bitcast_fusion), channel_id=1, source_target_pairs={{0,1},{1,0},{2,3},{3,2},{4,5},{5,4},{6,7},{7,6},{8,9},{9,8},{10,11... | collective-permute-start | bytes 1990664 | tf_op jit(solution)/shard_map/ppermute | solution.py:26
  4.1 24.9 %collective-permute-start.3 = (bf16[288,1152]{1,0:T(8,128)(2,1)}, bf16[288,1152]{1,0:T(8,128)(2,1)S(1)}, u32[]{:S(2)}, u32[]{:S(2)}) collective-permute-start(bf16[288,1152]{1,0:T(8,128)(2,1)} %select_bitcast_fusion), channel_id=1, source_target_pairs={{0,7},{1,6},{2,1},{3,0},{4,3},{5,2},{6,5},{7,4},{8,15},{9,14},{10,... | collective-permute-start | bytes 1990664 | tf_op jit(solution)/shard_map/ppermute | solution.py:26
  10.7 17.4 %collective-permute-start.2 = (bf16[288,1152]{1,0:T(8,128)(2,1)}, bf16[288,1152]{1,0:T(8,128)(2,1)S(1)}, u32[]{:S(2)}, u32[]{:S(2)}) collective-permute-start(bf16[288,1152]{1,0:T(8,128)(2,1)} %get-tuple-element.7), channel_id=1, source_target_pairs={{0,2},{1,3},{2,4},{3,5},{4,6},{5,7},{6,0},{7,1},{8,10},{9,11},{10,... | collective-permute-start | bytes 1990664 | tf_op jit(solution)/shard_map/ppermute | solution.py:26
  11.6 18.2 %collective-permute-start = (bf16[256,1152]{1,0:T(8,128)(2,1)}, bf16[256,1152]{1,0:T(8,128)(2,1)S(1)}, u32[]{:S(2)}, u32[]{:S(2)}) collective-permute-start(bf16[256,1152]{1,0:T(8,128)(2,1)} %get-tuple-element.20), channel_id=1, source_target_pairs={{0,1},{1,0},{2,3},{3,2},{4,5},{5,4},{6,7},{7,6},{8,9},{9,8},{10,11... | collective-permute-start | bytes 1769480 | tf_op jit(solution)/shard_map/ppermute | solution.py:26
  35.0 17.0 %collective-permute-start.5 = (bf16[512,1152]{1,0:T(8,128)(2,1)}, bf16[512,1152]{1,0:T(8,128)(2,1)}, u32[]{:S(2)}, u32[]{:S(2)}) collective-permute-start(bf16[512,1152]{1,0:T(8,128)(2,1)} %multiply_convert_fusion.1), channel_id=1, source_target_pairs={{0,121},{1,8},{2,123},{3,10},{4,125},{5,12},{6,127},{7,14},{8,1},{... | collective-permute-start | bytes 3538952 | tf_op jit(solution)/shard_map/ppermute | solution.py:26
  37.5 28.0 %collective-permute-start.6 = (bf16[512,1152]{1,0:T(8,128)(2,1)}, bf16[512,1152]{1,0:T(8,128)(2,1)}, u32[]{:S(2)}, u32[]{:S(2)}) collective-permute-start(bf16[512,1152]{1,0:T(8,128)(2,1)} %multiply_convert_fusion.1), channel_id=1, source_target_pairs={{0,3},{1,2},{2,1},{3,0},{4,7},{5,6},{6,5},{7,4},{8,11},{9,10},{10,... | collective-permute-start | bytes 3538952 | tf_op jit(solution)/shard_map/ppermute | solution.py:26
  40.4 29.0 %collective-permute-start.7 = (bf16[512,1152]{1,0:T(8,128)(2,1)}, bf16[512,1152]{1,0:T(8,128)(2,1)}, u32[]{:S(2)}, u32[]{:S(2)}) collective-permute-start(bf16[512,1152]{1,0:T(8,128)(2,1)} %multiply_convert_fusion.1), channel_id=1, source_target_pairs={{1,6},{3,4},{4,3},{6,1},{9,14},{11,12},{12,11},{14,9},{17,22},{19,... | collective-permute-start | bytes 3538952 | tf_op jit(solution)/shard_map/ppermute | solution.py:26
  51.9 26.1 %collective-permute-start.8 = (bf16[512,1152]{1,0:T(8,128)(2,1)}, bf16[512,1152]{1,0:T(8,128)(2,1)}, u32[]{:S(2)}, u32[]{:S(2)}) collective-permute-start(bf16[512,1152]{1,0:T(8,128)(2,1)} %collective-permute-done.5), channel_id=1, source_target_pairs={{1,7},{3,5},{4,2},{6,0},{9,15},{11,13},{12,10},{14,8},{17,23},{19,... | collective-permute-start | bytes 3538952 | tf_op jit(solution)/shard_map/ppermute | solution.py:26
  55.6 29.3 %collective-permute-start.4 = (bf16[512,1152]{1,0:T(8,128)(2,1)}, bf16[512,1152]{1,0:T(8,128)(2,1)}, u32[]{:S(2)}, u32[]{:S(2)}) collective-permute-start(bf16[512,1152]{1,0:T(8,128)(2,1)} %multiply_convert_fusion.1), channel_id=1, source_target_pairs={{0,1},{1,0},{2,3},{3,2},{4,5},{5,4},{6,7},{7,6},{8,9},{9,8},{10,11... | collective-permute-start | bytes 3538952 | tf_op jit(solution)/shard_map/ppermute | solution.py:26
  59.5 89.4 %collective-permute-start.17 = (bf16[512,1152]{1,0:T(8,128)(2,1)}, bf16[512,1152]{1,0:T(8,128)(2,1)}, u32[]{:S(2)}, u32[]{:S(2)}) collective-permute-start(bf16[512,1152]{1,0:T(8,128)(2,1)} %pad_maximum_fusion), channel_id=1, source_target_pairs={{0,32},{1,33},{2,34},{3,35},{4,36},{5,37},{6,38},{7,39},{8,40},{9,... | collective-permute-start | bytes 3538952 | tf_op jit(solution)/shard_map/ppermute | solution.py:26
  65.5 26.1 %collective-permute-start.9 = (bf16[512,1152]{1,0:T(8,128)(2,1)}, bf16[512,1152]{1,0:T(8,128)(2,1)}, u32[]{:S(2)}, u32[]{:S(2)}) collective-permute-start(bf16[512,1152]{1,0:T(8,128)(2,1)} %collective-permute-done.6), channel_id=1, source_target_pairs={{0,8},{1,121},{2,10},{3,123},{4,12},{5,125},{6,14},{7,127},{8,16},... | collective-permute-start | bytes 3538952 | tf_op jit(solution)/shard_map/ppermute | solution.py:26
  69.4 28.7 %collective-permute-start.10 = (bf16[512,1152]{1,0:T(8,128)(2,1)}, bf16[512,1152]{1,0:T(8,128)(2,1)S(1)}, u32[]{:S(2)}, u32[]{:S(2)}) collective-permute-start(bf16[512,1152]{1,0:T(8,128)(2,1)} %collective-permute-done.7), channel_id=1, source_target_pairs={{1,121},{3,123},{4,12},{6,14},{9,1},{11,3},{12,20},{14,22},{17,9},... | collective-permute-start | bytes 3538952 | tf_op jit(solution)/shard_map/ppermute | solution.py:26
  78.0 27.3 %collective-permute-start.11 = (bf16[512,1152]{1,0:T(8,128)(2,1)}, bf16[512,1152]{1,0:T(8,128)(2,1)}, u32[]{:S(2)}, u32[]{:S(2)}) collective-permute-start(bf16[512,1152]{1,0:T(8,128)(2,1)} %collective-permute-done.8), channel_id=1, source_target_pairs={{0,8},{2,10},{5,125},{7,127},{8,16},{10,18},{13,5},{15,7},{16,24},... | collective-permute-start | bytes 3538952 | tf_op jit(solution)/shard_map/ppermute | solution.py:26
  84.9 77.7 %collective-permute-start.19 = (bf16[512,1152]{1,0:T(8,128)(2,1)}, bf16[512,1152]{1,0:T(8,128)(2,1)}, u32[]{:S(2)}, u32[]{:S(2)}) collective-permute-start(bf16[512,1152]{1,0:T(8,128)(2,1)} %pad_maximum_fusion), channel_id=1, source_target_pairs={{0,96},{1,97},{2,98},{3,99},{4,100},{5,101},{6,102},{7,103},{8,104... | collective-permute-start | bytes 3538952 | tf_op jit(solution)/shard_map/ppermute | solution.py:26
  91.6 23.2 %collective-permute-start.12 = (bf16[512,1152]{1,0:T(8,128)(2,1)}, bf16[512,1152]{1,0:T(8,128)(2,1)}, u32[]{:S(2)}, u32[]{:S(2)}) collective-permute-start(bf16[512,1152]{1,0:T(8,128)(2,1)} %collective-permute-done.6), channel_id=1, source_target_pairs={{0,6},{2,4},{5,3},{7,1},{8,14},{10,12},{13,11},{15,9},{16,22},{18,... | collective-permute-start | bytes 3538952 | tf_op jit(solution)/shard_map/ppermute | solution.py:26
  98.1 21.2 %collective-permute-start.13 = (bf16[512,1152]{1,0:T(8,128)(2,1)}, bf16[512,1152]{1,0:T(8,128)(2,1)}, u32[]{:S(2)}, u32[]{:S(2)}) collective-permute-start(bf16[512,1152]{1,0:T(8,128)(2,1)} %collective-permute-done.9), channel_id=1, source_target_pairs={{1,7},{3,5},{4,2},{6,0},{9,15},{11,13},{12,10},{14,8},{17,23},{19,... | collective-permute-start | bytes 3538952 | tf_op jit(solution)/shard_map/ppermute | solution.py:26
  106.7 24.0 %collective-permute-start.14 = (bf16[512,1152]{1,0:T(8,128)(2,1)S(1)}, bf16[512,1152]{1,0:T(8,128)(2,1)}, u32[]{:S(2)}, u32[]{:S(2)}) collective-permute-start(bf16[512,1152]{1,0:T(8,128)(2,1)S(1)} %broadcast_select_fusion), channel_id=1, source_target_pairs={{0,2},{1,3},{2,0},{3,1},{4,6},{5,7},{6,4},{7,5},{8,10},{9,11},{10,... | collective-permute-start | bytes 3538952 | tf_op jit(solution)/shard_map/ppermute | solution.py:26
  114.8 49.6 %collective-permute-start.21 = (bf16[512,1152]{1,0:T(8,128)(2,1)}, bf16[512,1152]{1,0:T(8,128)(2,1)}, u32[]{:S(2)}, u32[]{:S(2)}) collective-permute-start(bf16[512,1152]{1,0:T(8,128)(2,1)} %pad_maximum_fusion), channel_id=1, source_target_pairs={{0,64},{1,65},{2,66},{3,67},{4,68},{5,69},{6,70},{7,71},{8,72},{9,... | collective-permute-start | bytes 3538952 | tf_op jit(solution)/shard_map/ppermute | solution.py:26
  146.2 14.5 %collective-permute-start.16 = (bf16[288,512]{1,0:T(8,128)(2,1)S(1)}, bf16[288,512]{1,0:T(8,128)(2,1)S(1)}, u32[]{:S(2)}, u32[]{:S(2)}) collective-permute-start(bf16[288,512]{1,0:T(8,128)(2,1)S(1)} %bitcast.124), channel_id=1, source_target_pairs={{0,32},{1,33},{2,34},{3,35},{4,36},{5,37},{6,38},{7,39},{8,40},{9,... | collective-permute-start | bytes 884744 | tf_op jit(solution)/shard_map/ppermute | solution.py:26
  146.2 16.3 %collective-permute-start.18 = (bf16[288,512]{1,0:T(8,128)(2,1)S(1)}, bf16[288,512]{1,0:T(8,128)(2,1)S(1)}, u32[]{:S(2)}, u32[]{:S(2)}) collective-permute-start(bf16[288,512]{1,0:T(8,128)(2,1)S(1)} %bitcast.123), channel_id=1, source_target_pairs={{0,96},{1,97},{2,98},{3,99},{4,100},{5,101},{6,102},{7,103},{8,104... | collective-permute-start | bytes 884744 | tf_op jit(solution)/shard_map/ppermute | solution.py:26
  148.9 15.5 %collective-permute-start.20 = (bf16[288,512]{1,0:T(8,128)(2,1)}, bf16[288,512]{1,0:T(8,128)(2,1)S(1)}, u32[]{:S(2)}, u32[]{:S(2)}) collective-permute-start(bf16[288,512]{1,0:T(8,128)(2,1)} %bitcast.9), channel_id=1, source_target_pairs={{0,64},{1,65},{2,66},{3,67},{4,68},{5,69},{6,70},{7,71},{8,72},{9,... | collective-permute-start | bytes 884744 | tf_op jit(solution)/shard_map/ppermute | solution.py:26
  167.0 6.6 %collective-permute-start.22 = (bf16[72,1152]{1,0:T(8,128)(2,1)S(1)}, bf16[72,1152]{1,0:T(8,128)(2,1)S(1)}, u32[]{:S(2)}, u32[]{:S(2)}) collective-permute-start(bf16[72,1152]{1,0:T(8,128)(2,1)S(1)} %get-tuple-element.12), channel_id=1, source_target_pairs={{0,2},{1,3},{2,4},{3,5},{4,6},{5,7},{6,0},{7,1},{8,10},{9,11},{10,... | collective-permute-start | bytes 497672 | tf_op jit(solution)/shard_map/ppermute | solution.py:26
  167.1 7.2 %collective-permute-start.23 = (bf16[72,1152]{1,0:T(8,128)(2,1)S(1)}, bf16[72,1152]{1,0:T(8,128)(2,1)S(1)}, u32[]{:S(2)}, u32[]{:S(2)}) collective-permute-start(bf16[72,1152]{1,0:T(8,128)(2,1)S(1)} %get-tuple-element.14), channel_id=1, source_target_pairs={{0,6},{1,7},{2,0},{3,1},{4,2},{5,3},{6,4},{7,5},{8,14},{9,15},{10,... | collective-permute-start | bytes 497672 | tf_op jit(solution)/shard_map/ppermute | solution.py:26
  169.8 7.7 %collective-permute-start.24 = (bf16[72,1152]{1,0:T(8,128)(2,1)S(1)}, bf16[72,1152]{1,0:T(8,128)(2,1)S(1)}, u32[]{:S(2)}, u32[]{:S(2)}) collective-permute-start(bf16[72,1152]{1,0:T(8,128)(2,1)S(1)} %get-tuple-element.13), channel_id=1, source_target_pairs={{0,4},{1,5},{2,6},{3,7},{4,0},{5,1},{6,2},{7,3},{8,12},{9,13},{10,... | collective-permute-start | bytes 497672 | tf_op jit(solution)/shard_map/ppermute | solution.py:26
  177.6 7.0 %collective-permute-start.25 = (bf16[72,1152]{1,0:T(8,128)(2,1)S(1)}, bf16[72,1152]{1,0:T(8,128)(2,1)S(1)}, u32[]{:S(2)}, u32[]{:S(2)}) collective-permute-start(bf16[72,1152]{1,0:T(8,128)(2,1)S(1)} %fusion.113), channel_id=1, source_target_pairs={{0,8},{1,9},{2,10},{3,11},{4,12},{5,13},{6,14},{7,15},{8,16},{9,17... | collective-permute-start | bytes 497672 | tf_op jit(solution)/shard_map/ppermute | solution.py:26
  178.6 7.1 %collective-permute-start.26 = (bf16[72,1152]{1,0:T(8,128)(2,1)S(1)}, bf16[72,1152]{1,0:T(8,128)(2,1)S(1)}, u32[]{:S(2)}, u32[]{:S(2)}) collective-permute-start(bf16[72,1152]{1,0:T(8,128)(2,1)S(1)} %fusion.113), channel_id=1, source_target_pairs={{0,24},{1,25},{2,26},{3,27},{4,28},{5,29},{6,30},{7,31},{8,0},{9,1... | collective-permute-start | bytes 497672 | tf_op jit(solution)/shard_map/ppermute | solution.py:26
  181.4 7.1 %collective-permute-start.27 = (bf16[72,1152]{1,0:T(8,128)(2,1)S(1)}, bf16[72,1152]{1,0:T(8,128)(2,1)S(1)}, u32[]{:S(2)}, u32[]{:S(2)}) collective-permute-start(bf16[72,1152]{1,0:T(8,128)(2,1)S(1)} %fusion.113), channel_id=1, source_target_pairs={{0,16},{1,17},{2,18},{3,19},{4,20},{5,21},{6,22},{7,23},{8,24},{9,... | collective-permute-start | bytes 497672 | tf_op jit(solution)/shard_map/ppermute | solution.py:26
  188.6 5.8 %collective-permute-start.28 = (bf16[72,1152]{1,0:T(8,128)(2,1)S(1)}, bf16[72,1152]{1,0:T(8,128)(2,1)S(1)}, u32[]{:S(2)}, u32[]{:S(2)}) collective-permute-start(bf16[72,1152]{1,0:T(8,128)(2,1)S(1)} %add_convert_fusion), channel_id=1, source_target_pairs={{0,4},{1,5},{2,6},{3,7},{4,0},{5,1},{6,2},{7,3},{8,12},{9,13},{10,... | collective-permute-start | bytes 497672 | tf_op jit(solution)/shard_map/ppermute | solution.py:26
  194.5 10.9 %collective-permute-start.29 = (bf16[2,72,1152]{2,1,0:T(8,128)(2,1)S(1)}, bf16[2,72,1152]{2,1,0:T(8,128)(2,1)S(1)}, u32[]{:S(2)}, u32[]{:S(2)}) collective-permute-start(bf16[2,72,1152]{2,1,0:T(8,128)(2,1)S(1)} %pad_maximum_fusion.1), channel_id=1, source_target_pairs={{0,96},{1,97},{2,98},{3,99},{4,100},{5,101},{6,102},{7,103},{8,104... | collective-permute-start | bytes 995336 | tf_op jit(solution)/shard_map/ppermute | solution.py:26
  199.9 24.9 %collective-permute-start.15 = (bf16[256,1152]{1,0:T(8,128)(2,1)}, bf16[256,1152]{1,0:T(8,128)(2,1)}, u32[]{:S(2)}, u32[]{:S(2)}) collective-permute-start(bf16[256,1152]{1,0:T(8,128)(2,1)} %slice.10), channel_id=1, source_target_pairs={{0,1},{1,0},{2,3},{3,2},{4,5},{5,4},{6,7},{7,6},{8,9},{9,8},{10,11... | collective-permute-start | bytes 1769480 | tf_op jit(solution)/shard_map/ppermute | solution.py:26
  204.7 11.0 %collective-permute-start.30 = (bf16[2,72,1152]{2,1,0:T(8,128)(2,1)S(1)}, bf16[2,72,1152]{2,1,0:T(8,128)(2,1)S(1)}, u32[]{:S(2)}, u32[]{:S(2)}) collective-permute-start(bf16[2,72,1152]{2,1,0:T(8,128)(2,1)S(1)} %pad_maximum_fusion.1), channel_id=1, source_target_pairs={{0,64},{1,65},{2,66},{3,67},{4,68},{5,69},{6,70},{7,71},{8,72},{9,... | collective-permute-start | bytes 995336 | tf_op jit(solution)/shard_map/ppermute | solution.py:26
  204.8 18.4 %collective-permute-start.31 = (bf16[2,72,1152]{2,1,0:T(8,128)(2,1)S(1)}, bf16[2,72,1152]{2,1,0:T(8,128)(2,1)S(1)}, u32[]{:S(2)}, u32[]{:S(2)}) collective-permute-start(bf16[2,72,1152]{2,1,0:T(8,128)(2,1)S(1)} %pad_maximum_fusion.1), channel_id=1, source_target_pairs={{0,32},{1,33},{2,34},{3,35},{4,36},{5,37},{6,38},{7,39},{8,40},{9,... | collective-permute-start | bytes 995336 | tf_op jit(solution)/shard_map/ppermute | solution.py:26
  (13 other events, 106.3 us)

commit v2 on v1

v2 whole, which is shorter than its diff:
```python
import functools

import jax
import jax.numpy as jnp
from jax import lax
from jax.experimental import pallas as pl
from jax.experimental.pallas import tpu as pltpu
from jax.sharding import Mesh, PartitionSpec as P

WIN = 4
COST = 10**6
VMEM = 40 * 2**20
AXES = ("z", "x", "yh", "yl", "core")
SIZES = (4, 4, 2, 2, 2)
BF = jnp.bfloat16
F32 = jnp.float32


def flat(z, x, y, core):
    return (((z % 4) * 4 + x % 4) * 4 + y % 4) * 2 + core


def moved(block, route):
    pairs = []
    for z in range(4):
        for x in range(4):
            for y in range(4):
                for core in range(2):
                    place = route(z, x, y, core)
                    if place is not None:
                        pairs.append((flat(z, x, y, core), flat(*place)))
    return lax.ppermute(block, AXES, pairs)


def hop(dz=0, dx=0, dy=0, swap=0):
    return lambda z, x, y, core: (z + dz, x + dx, y + dy, core ^ swap)


def collect(step, parity=None, direct=False):
    def route(z, x, y, core):
        role = core ^ 1 if direct else core
        if role:
            z, x, y = 3 - z, 3 - x, 3 - y
        column, odd, half = z * 4 + x, y // 2, y % 2
        if parity is not None and odd != parity:
            return None
        if step == "half":
            half = 1 - half
        elif step == "column":
            column = (column + 1) % 16
        elif step == "cross":
            odd, half = 1 - odd, 1 - half
        z, x, y = column // 4, column % 4, odd * 2 + half
        if role:
            z, x, y = 3 - z, 3 - x, 3 - y
        return (z, x, y, role)

    return route


def after(value, *others):
    return lax.optimization_barrier((value,) + others)[0]


def dot_nt(left, right):
    return lax.dot_general(
        left, right, (((1,), (1,)), ((), ())), preferred_element_type=F32
    )


def dot_nn(left, right):
    return jnp.dot(left, right, preferred_element_type=F32)


def embed_kernel(place, own, mate, *refs):
    parts, (unit, emb, inverse, head, sem) = refs[:4], refs[4:]
    columns = parts[0].shape[0]
    copies = []
    for i, part in enumerate(parts):
        start = pl.multiple_of(place[i] * columns, 16)
        copies.append(pltpu.make_async_copy(part, head.at[pl.ds(start, columns)], sem.at[i]))
    for copy in copies:
        copy.start()
    for copy in copies:
        copy.wait()
    rows = own.shape[0]
    for at, pool in ((0, own), (rows, mate)):
        raw = dot_nt(pool[...], head[...])
        norm = lax.rsqrt(jnp.sum(raw * raw, axis=1, keepdims=True) + 1e-06)
        raw = raw * norm
        inverse[at : at + rows, :] = norm
        unit[at : at + rows, :] = raw
        emb[at : at + rows, :] = raw.astype(BF)


def embed(own, mate, parts, place):
    rows, width = own.shape
    vmem = pl.BlockSpec(memory_space=pltpu.VMEM)
    return pl.pallas_call(
        embed_kernel,
        in_specs=[pl.BlockSpec(memory_space=pltpu.SMEM), vmem, vmem]
        + [pl.BlockSpec(memory_space=pl.ANY)] * 4,
        out_specs=[vmem] * 4,
        out_shape=[
            jax.ShapeDtypeStruct((2 * rows, width), F32),
            jax.ShapeDtypeStruct((2 * rows, width), BF),
            jax.ShapeDtypeStruct((2 * rows, 1), F32),
            jax.ShapeDtypeStruct((width, width), BF),
        ],
        scratch_shapes=[pltpu.SemaphoreType.DMA((4,))],
        compiler_params=pltpu.CompilerParams(vmem_limit_bytes=VMEM),
        cost_estimate=pl.CostEstimate(flops=COST, bytes_accessed=2**20, transcendentals=0),
        name="embed",
    )(place, own, mate, *parts)


def sums_kernel(plan, *refs):
    names, units, label = plan
    ref = dict(zip(names, refs))
    scale, bias = ref["scale"][0], ref["bias"][0]
    step = pl.program_id(0)
    copies = {}
    for place, unit in enumerate(units):
        if isinstance(unit, tuple):
            copies[place] = [
                pltpu.make_async_copy(ref[name], ref["held"].at[place], ref["sem"].at[place])
                for name in unit
            ]
            for copy, parity in zip(copies[place], (1, 0)):
                pl.when((step == 0) & (ref["odd"][0] == parity))(copy.start)

    emb = ref["emb"][...]
    rows = emb.shape[0]
    total = ref["sum"][...] if "sum" in ref else None
    for place, unit in enumerate(units):
        if place in copies:
            pl.when(step == 0)(copies[place][0].wait)
        block = ref["held"][place] if isinstance(unit, tuple) else ref[unit][...]
        count = block.shape[0]
        score = scale * dot_nt(emb, block) + bias
        below = 1.0 + jnp.exp(-score)
        tile = pl.reciprocal(below, approx=True)
        tile = tile * (2.0 - below * tile)
        if label and place == 0:
            ids = lax.broadcasted_iota(jnp.int32, score.shape, 0) + step * rows
            jds = lax.broadcasted_iota(jnp.int32, score.shape, 1)
            shift = jnp.where(jds < count // 2, count // 2, -(count // 2))
            tile = tile - (ids == jds + shift).astype(F32)
        tile = (tile * (1.0 / (WIN * 2 * count))).astype(BF)
        term = dot_nn(tile, block)
        total = term if total is None else total + term
    if "raw" not in ref:
        ref["out"][...] = total
        return
    unit, inverse = ref["unit"][...], ref["inverse"][...]
    grad = total * scale
    inner = jnp.sum(unit * grad, axis=1, keepdims=True)
    raw = (grad - unit * inner) * inverse
    ref["raw"][...] = raw.astype(BF)
    ref["turned"][...] = raw.T
    piece = ref["to0"].shape[0] // 4
    for ahead in range(4):
        parts = []
        for shard in range(4):
            start = pl.multiple_of(ref["order"][ahead * 4 + shard] * piece, 8)
            parts.append(ref["turned"][pl.ds(start, piece), :])
        ref["to%d" % ahead][...] = jnp.concatenate(parts, axis=0).astype(BF)


def sums(emb, units, scale, bias, odd, total=None, label=False, finish=None):
    count, width = emb.shape
    block = 256
    smem = pl.BlockSpec(memory_space=pltpu.SMEM)
    rows = pl.BlockSpec((block, width), lambda i: (i, 0))
    whole = pl.BlockSpec((count, width), lambda i: (0, 0))
    names, args, specs = ["scale", "bias", "odd", "emb"], [scale, bias, odd, emb], [smem] * 3 + [rows]
    plan = []
    for place, unit in enumerate(units):
        if isinstance(unit, tuple):
            pair = ("a%d" % place, "b%d" % place)
            plan.append(pair)
            names += pair
            args += unit
            specs += [pl.BlockSpec(memory_space=pl.ANY)] * 2
        else:
            plan.append("u%d" % place)
            names.append("u%d" % place)
            args.append(unit)
            specs.append(whole)
    if total is not None:
        names.append("sum")
        args.append(total)
        specs.append(rows)
    if finish is None:
        outs = [("out", (count, width), F32, rows)]
    else:
        unit, inverse, order = finish
        names += ["unit", "inverse", "order"]
        args += [unit, inverse, order]
        specs += [rows, pl.BlockSpec((block, 1), lambda i: (i, 0)), smem]
        outs = [("raw", (count, width), BF, rows)]
        part = pl.BlockSpec((width // 4, block), lambda i: (0, i))
        outs += [("to%d" % i, (width // 4, count), BF, part) for i in range(4)]
    names += [out[0] for out in outs]
    scratch = []
    if any(isinstance(unit, tuple) for unit in units):
        names += ["held", "sem"]
        scratch += [
            pltpu.VMEM((len(units), count, width), BF),
            pltpu.SemaphoreType.DMA((len(units),)),
        ]
    if finish is not None:
        names.append("turned")
        scratch.append(pltpu.VMEM((width, block), F32))
    result = pl.pallas_call(
        functools.partial(sums_kernel, (tuple(names), tuple(plan), label)),
        grid=(count // block,),
        in_specs=specs,
        out_specs=[out[3] for out in outs],
        out_shape=[jax.ShapeDtypeStruct(out[1], out[2]) for out in outs],
        scratch_shapes=scratch,
        compiler_params=pltpu.CompilerParams(vmem_limit_bytes=VMEM),
        cost_estimate=pl.CostEstimate(flops=COST, bytes_accessed=2**20, transcendentals=0),
        name="finish" if finish is not None else "sums",
    )(*args)
    return result if finish is not None else result[0]


def head_kernel(*refs):
    lefts, rights, outs = refs[:4], refs[4:12], refs[12:]
    depth = rights[0].shape[0]
    total = None
    for place, right in enumerate(rights):
        side = place % 2
        left = lefts[place // 2][:, side * depth : (side + 1) * depth]
        term = jnp.dot(left, right[...], preferred_element_type=F32)
        total = term if total is None else total + term
    piece = outs[0].shape[0]
    outs[0][...] = total[:piece]
    for place in range(1, 4):
        outs[place][...] = total[place * piece : (place + 1) * piece].astype(BF)


def head_products(lefts, rights):
    columns, count = lefts[0].shape
    width = rights[0].shape[1]
    depth = count // 2
    tile = 384
    piece = columns // 4
    out = pl.BlockSpec((piece, tile), lambda i: (0, i))
    mine, *sends = pl.pallas_call(
        head_kernel,
        grid=(width // tile,),
        in_specs=[pl.BlockSpec((columns, count), lambda i: (0, 0))] * 4
        + [pl.BlockSpec((depth, tile), lambda i, at=at: (at, i)) for at in (0, 1, 0, 1, 0, 1, 0, 0)],
        out_specs=[out] * 4,
        out_shape=[jax.ShapeDtypeStruct((piece, width), F32)]
        + [jax.ShapeDtypeStruct((piece, width), BF)] * 3,
        compiler_params=pltpu.CompilerParams(vmem_limit_bytes=VMEM),
        cost_estimate=pl.CostEstimate(
            flops=8 * columns * count * width, bytes_accessed=8 * 2**20, transcendentals=0
        ),
        name="head_products",
    )(*lefts, *rights)
    return mine, sends


def body(image_pool, text_pool, image_head, text_head, logit_scale, logit_bias):
    core = lax.axis_index("core")
    half = lax.axis_index("yl")
    odd = lax.axis_index("yh")
    plane = lax.axis_index("z")
    first = core == 0
    rows, width = image_pool.shape
    columns = image_head.shape[1]

    head_own = jnp.where(first, image_head, text_head).T
    head_other = jnp.where(first, text_head, image_head).T
    head_own, head_other = lax.optimization_barrier((head_own, head_other))
    pool_own = jnp.where(first, image_pool, text_pool)
    pool_other = jnp.where(first, text_pool, image_pool)
    head_up = moved(head_own, hop(dy=1))
    head_down = moved(head_other, hop(dy=-1, swap=1))
    pool_mate = moved(pool_other, hop(swap=1))
    head_mate = moved(after(head_other, pool_mate), hop(swap=1))
    pool = jnp.concatenate([pool_own, pool_mate], axis=0)
    pool_z1 = moved(pool, hop(dz=1))
    pool_z3 = moved(pool, hop(dz=-1))
    far = 1 - half
    place = jnp.stack(
        [2 * half + core, 2 * half + 1 - core, 2 * far + core, 2 * far + 1 - core]
    ).astype(jnp.int32)
    unit, emb, inverse, head = embed(
        pool_own, pool_mate, (head_own, head_mate, head_up, head_down), place
    )

    odd_block = jnp.where(first, odd, 1 - odd)
    is_odd = odd_block == 1
    score = functools.partial(
        sums, emb, scale=logit_scale, bias=logit_bias, odd=odd_block.astype(jnp.int32).reshape(1)
    )
    b0n = moved(emb, collect("same", direct=True))
    b2n = moved(emb, collect("column", direct=True))
    b0f_even = moved(emb, collect("half", parity=0, direct=True))
    b1f_odd = moved(after(emb, b0n, pool_z1, pool_z3), collect("cross", parity=0, direct=True))
    b0f_odd = moved(after(emb, b0f_even), collect("half", parity=1, direct=True))
    b1f_even = moved(b2n, collect("cross", parity=1))
    b1f_b0f = jnp.where(is_odd, b1f_odd, b0f_even)
    b3f_b2f = moved(b1f_b0f, collect("column"))
    grad = score([b0n, b2n, b1f_b0f], label=True)
    b0f_odd, b1f_even, grad = lax.optimization_barrier((b0f_odd, b1f_even, grad))
    b0f_b1f = jnp.where(is_odd, b0f_odd, b1f_even)
    b2f_b3f = moved(b0f_b1f, collect("column"))
    b1n_odd = moved(after(b1f_b0f, b1f_even), collect("cross", parity=0))
    b3n_odd = moved(b3f_b2f, collect("half", parity=1))
    grad = score([b3f_b2f, b0f_b1f], total=grad)
    b2f_b3f, b1n_odd, b3n_odd, grad = lax.optimization_barrier((b2f_b3f, b1n_odd, b3n_odd, grad))
    b1n_even = moved(b2f_b3f, collect("cross", parity=1))
    b3n_even = moved(b2f_b3f, collect("half", parity=0))
    grad = score([b2f_b3f], total=grad)
    own_z2 = moved(after(pool_z1[:rows], b2f_b3f), hop(dz=1))
    mate_z2 = moved(after(pool_z3[rows:], b2f_b3f), hop(dz=-1))
    order = []
    for ahead in range(4):
        for far_half, far_odd in ((0, 0), (0, 1), (1, 0), (1, 1)):
            shard = 2 * (half ^ far_half) + (odd ^ far_odd)
            order.append(shard * 4 + (plane + ahead) % 4)
    order = jnp.stack(order).astype(jnp.int32)
    raw_grad, *pieces = score(
        [(b1n_odd, b1n_even), (b3n_odd, b3n_even)],
        total=grad,
        finish=(unit, inverse, order),
    )
    part2 = moved(pieces[2], hop(dz=2))
    part1 = moved(pieces[1], hop(dz=1))
    part3 = moved(pieces[3], hop(dz=-1))
    grad_pool = dot_nn(raw_grad, head).astype(BF)
    pool_back = moved(grad_pool[rows:], hop(swap=1))
    grad_image = jnp.where(first, grad_pool[:rows], pool_back)
    grad_text = jnp.where(first, pool_back, grad_pool[:rows])
    part2, grad_pool = lax.optimization_barrier((part2, grad_pool))
    mine, sends = head_products(
        (pieces[0], part1, part3, part2),
        (pool, pool, pool_z1, pool_z1, pool_z3, pool_z3, own_z2, mate_z2),
    )

    def y_partner(bits):
        return lambda z, x, y, c: (z, x, y ^ bits, c)

    got = [moved(out, y_partner(bits)) for out, bits in zip(sends, (2, 1, 3))]
    for part in got:
        mine = mine + part.astype(F32)
    narrow = mine.astype(BF)
    for part in [moved(narrow, hop(dx=2)), moved(narrow, hop(dx=1)), moved(narrow, hop(dx=-1))]:
        mine = mine + part.astype(F32)
    narrow = mine.astype(BF)

    def hand_one(z, x, y, c):
        return (z, x, y, 1 - c) if c != y // 2 else (z, x, y ^ 2, c)

    def hand_two(z, x, y, c):
        return (z, x, y ^ 2, 1 - c) if c != y // 2 else None

    one = moved(narrow, hand_one)
    two = moved(narrow, hand_two)
    here = core == odd
    same = jnp.where(here, narrow, one)
    other = jnp.where(here, one, two)
    pair = jnp.stack([jnp.where(first, same, other), jnp.where(first, other, same)])
    across = moved(pair, hop(dz=2))
    ring = [pair, moved(pair, hop(dz=-1)), across, moved(pair, hop(dz=1))]
    ring = jnp.stack(ring + ring, axis=1)
    ring = lax.dynamic_slice_in_dim(ring, 4 - plane, 4, 1)
    ring = ring.reshape(2, columns, width).astype(F32)
    return (grad_image, grad_text, ring[0].T, ring[1].T)


def solution(mesh):
    fine = Mesh(mesh.devices.reshape(SIZES), AXES)
    rows = P(AXES, None)
    cols = P(None, ("yl", "core"))
    return jax.shard_map(
        body,
        mesh=fine,
        in_specs=(rows, rows, cols, cols, P(), P()),
        out_specs=(rows, rows, cols, cols),
        check_vma=False,
    )
```

time: 230 us -> 195 us (0.85)
  matrix products: 59.3 us -> 1.84 us
  Pallas kernels: 0 us -> 29.8 us
  waiting for transfers between devices: 86 us -> 70.8 us
  starting transfers between devices: 57.7 us -> 68.6 us
  other arithmetic: 14.1 us -> 7.37 us
  local copies, waits for them, and re-layouts: 9.36 us -> 13.6 us
    dot_general x13 -> x1, matrix products: 55.4 us -> 1.84 us  [dot_nn(): return jnp.dot(left, right, preferred_element_type=F32)]
    pallas_call x0 -> x6, Pallas kernels: none -> 29.8 us  [the longest x4 21.4 us: sums(): pl.pallas_call(functools.partial(sums_kernel, (tuple(names), tuple(plan),...]
    ppermute x33 -> x35, waiting for transfers between devices: 86 us -> 70.8 us  [moved(): return lax.ppermute(block, AXES, pairs)]
    ppermute x33 -> x35, starting transfers between devices: 57.7 us -> 68.6 us  [moved(): return lax.ppermute(block, AXES, pairs)]
    unnamed x29 -> x53, local copies, waits for them, and re-layouts: 2.96 us -> 10.1 us
    dot_general x1 -> x0, matrix products: 3.91 us -> none  [dot_nt(): lax.dot_general(left, right, (((1,), (1,)), ((), ())), preferred_element_...]
    slice x0 -> x3, local copies, waits for them, and re-layouts: none -> 3.39 us  [the longest x1 1.67 us: body(): return (grad_image, grad_text, ring[0].T, ring[1].T)]
    convert_element_type x2 -> x1, other arithmetic: 3.31 us -> 0.2 us  [body(): ring = ring.reshape(2, columns, width).astype(F32)]
  transfers between devices with their start and end apart: 33 -> 35, of which waited for: 15 -> 22; matrix products, arithmetic and copies ran while one was open for 30% -> 5% of each run, Pallas kernels for 0% -> 13%
where the time goes in v2:
time: 195 us; the launch traced here: 194 us
  waiting for transfers between devices  70.8 us (36%)
  starting transfers between devices  68.6 us (35%)
  Pallas kernels  29.8 us (15%)
  local copies, waits for them, and re-layouts  13.6 us (7%)
  other arithmetic  7.37 us (4%)
  between operations  2.33 us (1%)
    ppermute x35, waiting for transfers between devices, moved(): return lax.ppermute(block, AXES, pairs)  70.8 us
    ppermute x35, starting transfers between devices, moved(): return lax.ppermute(block, AXES, pairs)  68.6 us
    pallas_call x4, Pallas kernels, sums(): pl.pallas_call(functools.partial(sums_kernel, (tuple(names), tuple(plan),...  21.4 us
    unnamed x53, local copies, waits for them, and re-layouts  10.1 us
    pallas_call x1, Pallas kernels, embed(): pl.pallas_call(embed_kernel, in_specs=[pl.BlockSpec(memory_space=pltpu.SM...  4.4 us
    pallas_call x1, Pallas kernels, head_products(): pl.pallas_call(head_kernel, grid=(width // tile,), in_specs=[pl.BlockSpec...  3.99 us
  transfers between devices with their start and end apart: 35, of which 22 were waited for; matrix products, arithmetic and copies ran while one was open for 5% of the time, Pallas kernels for 13%

profile of v2, /device:TPU:1, one launch (start us, length us, event | category | flops | bytes accessed | tf_op | source)
XLA Modules:
  0.0 194.4 jit_solution(8556050387081713959)
XLA Ops:
  8.2 3.8 %collective-permute-start.10 = (bf16[512,1152]{1,0:T(8,128)(2,1)S(1)}, bf16[512,1152]{1,0:T(8,128)(2,1)S(1)}, u32[]{:S(2)}, u32[]{:S(2)}) collective-permute-start(bf16[512,1152]{1,0:T(8,128)(2,1)S(1)} %pad_maximum_fusion.refs_4_.refs_5_), channel_id=1, source_target_pairs={{0,96},{1,97},{2,98},{3,99},{4,100},{5,101},{6,102},{7,103},{8,104... | collective-permute-start | bytes 3538952 | tf_op jit(solution)/shard_map/ppermute | solution.py:32
  12.1 11.0 %collective-permute-done.2.refs_2_ = bf16[288,1152]{1,0:T(8,128)(2,1)} collective-permute-done((bf16[288,1152]{1,0:T(8,128)(2,1)}, bf16[288,1152]{1,0:T(8,128)(2,1)}, u32[]{:S(2)}, u32[]{:S(2)}) %collective-permute-start.2) | collective-permute-done | bytes 663584 | tf_op jit(solution)/shard_map/ppermute | solution.py:32
  25.7 4.4 %embed.1 = (f32[512,1152]{1,0:T(8,128)S(1)}, bf16[512,1152]{1,0:T(8,128)(2,1)S(1)}, f32[512,1]{1,0:T(8,128)S(1)}, bf16[1152,1152]{1,0:T(8,128)(2,1)S(1)}) custom-call(s32[4]{0:T(128)S(1)} %pad_add_fusion.place, bf16[256,1152]{1,0:T(8,128)(2,1)S(1)} %copy-done.6, bf16[256,1152]{1,0:T(8,128)(2,1)S(1)} %copy-done.10, ...), custom_call_target="tpu_custom_call" | custom-call | flops 1000000 | bytes 1048576 | tf_op jit(solution)/shard_map/embed/pallas_call | solution.py:99
  34.0 3.4 %collective-permute-start.4 = (bf16[512,1152]{1,0:T(8,128)(2,1)S(1)}, bf16[512,1152]{1,0:T(8,128)(2,1)S(1)}, u32[]{:S(2)}, u32[]{:S(2)}) collective-permute-start(bf16[512,1152]{1,0:T(8,128)(2,1)S(1)} %get-tuple-element.38.refs_3_), channel_id=1, source_target_pairs={{1,2},{3,0},{4,7},{6,5},{9,10},{11,8},{12,15},{14,13},{17,18},{19,... | collective-permute-start | bytes 3538952 | tf_op jit(solution)/shard_map/ppermute | solution.py:32
  37.5 2.6 %collective-permute-done.9.refs_6_.refs_7_ = bf16[512,1152]{1,0:T(8,128)(2,1)S(1)} collective-permute-done((bf16[512,1152]{1,0:T(8,128)(2,1)S(1)}, bf16[512,1152]{1,0:T(8,128)(2,1)S(1)}, u32[]{:S(2)}, u32[]{:S(2)}) %collective-permute-start.9) | collective-permute-done | bytes 1179680 | tf_op jit(solution)/shard_map/ppermute | solution.py:32
  41.2 5.9 %collective-permute-start.11 = (bf16[512,1152]{1,0:T(8,128)(2,1)S(1)}, bf16[512,1152]{1,0:T(8,128)(2,1)}, u32[]{:S(2)}, u32[]{:S(2)}) collective-permute-start(bf16[512,1152]{1,0:T(8,128)(2,1)S(1)} %get-tuple-element.38.refs_3_), channel_id=1, source_target_pairs={{1,6},{3,4},{4,3},{6,1},{9,14},{11,12},{12,11},{14,9},{17,22},{19,... | collective-permute-start | bytes 3538952 | tf_op jit(solution)/shard_map/ppermute | solution.py:32
  47.1 3.3 %collective-permute-done.4 = bf16[512,1152]{1,0:T(8,128)(2,1)S(1)} collective-permute-done((bf16[512,1152]{1,0:T(8,128)(2,1)S(1)}, bf16[512,1152]{1,0:T(8,128)(2,1)S(1)}, u32[]{:S(2)}, u32[]{:S(2)}) %collective-permute-start.4) | collective-permute-done | bytes 1179680 | tf_op jit(solution)/shard_map/ppermute | solution.py:32
  53.5 6.1 %collective-permute-start.7 = (bf16[512,1152]{1,0:T(8,128)(2,1)}, bf16[512,1152]{1,0:T(8,128)(2,1)}, u32[]{:S(2)}, u32[]{:S(2)}) collective-permute-start(bf16[512,1152]{1,0:T(8,128)(2,1)} %collective-permute-done.6.refs_5_), channel_id=1, source_target_pairs={{1,7},{3,5},{4,2},{6,0},{9,15},{11,13},{12,10},{14,8},{17,23},{19,... | collective-permute-start | bytes 3538952 | tf_op jit(solution)/shard_map/ppermute | solution.py:32
  62.5 4.9 %collective-permute-start.14 = (bf16[512,1152]{1,0:T(8,128)(2,1)S(1)}, bf16[512,1152]{1,0:T(8,128)(2,1)S(1)}, u32[]{:S(2)}, u32[]{:S(2)}) collective-permute-start(bf16[512,1152]{1,0:T(8,128)(2,1)S(1)} %broadcast_select_fusion.1.refs_6_), channel_id=1, source_target_pairs={{0,8},{1,121},{2,10},{3,123},{4,12},{5,125},{6,14},{7,127},{8,16},... | collective-permute-start | bytes 3538952 | tf_op jit(solution)/shard_map/ppermute | solution.py:32
  68.8 6.8 %sums.3.refs_6_ = f32[512,1152]{1,0:T(8,128)S(1)} custom-call(f32[1]{0:T(128)S(6)} %copy.17.refs_0_, f32[1]{0:T(128)S(6)} %copy.18.refs_1_, s32[1]{0:T(128)} %bitcast.refs_2_, bf16[512,1152]{1,0:T(8,128)(2,1)S(1)} %get-tuple-element.38.refs_3_, bf16[512,1152]{1,0:T(8,128)(2,1)S(1)} %copy-done.16, bf16[512,1152]{1,0:T(8,128)(2,1)} %collective-permute-done.6.refs_5_, ...), custom_call_target="tpu_custom_call" | custom-call | flops 1000000 | bytes 1048576 | tf_op jit(solution)/shard_map/sums/pallas_call | solution.py:215
  78.3 2.8 %collective-permute-start.12 = (bf16[512,1152]{1,0:T(8,128)(2,1)S(1)}, bf16[512,1152]{1,0:T(8,128)(2,1)}, u32[]{:S(2)}, u32[]{:S(2)}) collective-permute-start(bf16[512,1152]{1,0:T(8,128)(2,1)S(1)} %broadcast_select_fusion.refs_5_), channel_id=1, source_target_pairs={{0,8},{1,121},{2,10},{3,123},{4,12},{5,125},{6,14},{7,127},{8,16},... | collective-permute-start | bytes 3538952 | tf_op jit(solution)/shard_map/ppermute | solution.py:32
  83.0 3.9 %sums.4.refs_5_ = f32[512,1152]{1,0:T(8,128)S(1)} custom-call(f32[1]{0:T(128)S(6)} %copy.17.refs_0_, f32[1]{0:T(128)S(6)} %copy.18.refs_1_, s32[1]{0:T(128)} %bitcast.refs_2_, bf16[512,1152]{1,0:T(8,128)(2,1)S(1)} %get-tuple-element.38.refs_3_, bf16[512,1152]{1,0:T(8,128)(2,1)S(1)} %collective-permute-done.14.refs_4_, ...), custom_call_target="tpu_custom_call" | custom-call | flops 1000000 | bytes 1048576 | tf_op jit(solution)/shard_map/sums/pallas_call | solution.py:215
  88.4 5.8 %collective-permute-done.13.refs_4_ = bf16[512,1152]{1,0:T(8,128)(2,1)S(1)} collective-permute-done((bf16[512,1152]{1,0:T(8,128)(2,1)S(1)}, bf16[512,1152]{1,0:T(8,128)(2,1)S(1)}, u32[]{:S(2)}, u32[]{:S(2)}) %collective-permute-start.13) | collective-permute-done | bytes 1179680 | tf_op jit(solution)/shard_map/ppermute | solution.py:32
  94.2 4.2 %collective-permute-done.15.refs_6_ = bf16[512,1152]{1,0:T(8,128)(2,1)S(1)} collective-permute-done((bf16[512,1152]{1,0:T(8,128)(2,1)S(1)}, bf16[512,1152]{1,0:T(8,128)(2,1)S(1)}, u32[]{:S(2)}, u32[]{:S(2)}) %collective-permute-start.15) | collective-permute-done | bytes 1179680 | tf_op jit(solution)/shard_map/ppermute | solution.py:32
  98.4 2.3 %collective-permute-start.16 = (bf16[512,1152]{1,0:T(8,128)(2,1)}, bf16[512,1152]{1,0:T(8,128)(2,1)}, u32[]{:S(2)}, u32[]{:S(2)}) collective-permute-start(bf16[512,1152]{1,0:T(8,128)(2,1)} %collective-permute-done.12.refs_4_), channel_id=1, source_target_pairs={{1,7},{3,5},{4,2},{6,0},{9,15},{11,13},{12,10},{14,8},{17,23},{19,... | collective-permute-start | bytes 3538952 | tf_op jit(solution)/shard_map/ppermute | solution.py:32
  104.2 2.7 %collective-permute-start.23 = (bf16[256,1152]{1,0:T(8,128)(2,1)}, bf16[256,1152]{1,0:T(8,128)(2,1)}, u32[]{:S(2)}, u32[]{:S(2)}) collective-permute-start(bf16[256,1152]{1,0:T(8,128)(2,1)} %slice.30), channel_id=1, source_target_pairs={{0,96},{1,97},{2,98},{3,99},{4,100},{5,101},{6,102},{7,103},{8,104... | collective-permute-start | bytes 1769480 | tf_op jit(solution)/shard_map/ppermute | solution.py:32
  108.6 3.6 %sums.5.refs_8_ = f32[512,1152]{1,0:T(8,128)S(1)} custom-call(f32[1]{0:T(128)S(6)} %copy.17.refs_0_, f32[1]{0:T(128)S(6)} %copy.18.refs_1_, s32[1]{0:T(128)} %bitcast.refs_2_, bf16[512,1152]{1,0:T(8,128)(2,1)S(1)} %get-tuple-element.38.refs_3_, bf16[512,1152]{1,0:T(8,128)(2,1)} %collective-permute-done.12.refs_4_, f32[512,1152]{1,0:T(8,128)S(1)} %copy-done.1), custom_call_target="tpu_custom_call" | custom-call | flops 1000000 | bytes 1048576 | tf_op jit(solution)/shard_map/sums/pallas_call | solution.py:215
  113.2 7.1 %finish.1 = (bf16[512,1152]{1,0:T(8,128)(2,1)S(1)}, bf16[288,512]{1,0:T(8,128)(2,1)S(1)}, bf16[288,512]{1,0:T(8,128)(2,1)S(1)}, bf16[288,512]{1,0:T(8,128)(2,1)S(1)}, bf16[288,512]{1,0:T(8,128)(2,1)S(1)}) custom-call(f32[1]{0:T(128)S(6)} %copy.17.refs_0_, f32[1]{0:T(128)S(6)} %copy.18.refs_1_, s32[1]{0:T(128)} %bitcast.refs_2_, ...), custom_call_target="tpu_custom_call" | custom-call | flops 1000000 | bytes 1048576 | tf_op jit(solution)/shard_map/finish/pallas_call | solution.py:215
  121.0 2.2 %collective-permute-start.20 = (bf16[288,512]{1,0:T(8,128)(2,1)S(1)}, bf16[288,512]{1,0:T(8,128)(2,1)S(1)}, u32[]{:S(2)}, u32[]{:S(2)}) collective-permute-start(bf16[288,512]{1,0:T(8,128)(2,1)S(1)} %get-tuple-element.53), channel_id=1, source_target_pairs={{0,96},{1,97},{2,98},{3,99},{4,100},{5,101},{6,102},{7,103},{8,104... | collective-permute-start | bytes 884744 | tf_op jit(solution)/shard_map/ppermute | solution.py:32
  125.0 2.6 %collective-permute-done.21.refs_3_ = bf16[288,512]{1,0:T(8,128)(2,1)S(1)} collective-permute-done((bf16[288,512]{1,0:T(8,128)(2,1)S(1)}, bf16[288,512]{1,0:T(8,128)(2,1)S(1)}, u32[]{:S(2)}, u32[]{:S(2)}) %collective-permute-start.21) | collective-permute-done | bytes 294944 | tf_op jit(solution)/shard_map/ppermute | solution.py:32
  127.6 2.8 %collective-permute-done.19.refs_1_ = bf16[288,512]{1,0:T(8,128)(2,1)S(1)} collective-permute-done((bf16[288,512]{1,0:T(8,128)(2,1)S(1)}, bf16[288,512]{1,0:T(8,128)(2,1)S(1)}, u32[]{:S(2)}, u32[]{:S(2)}) %collective-permute-start.19) | collective-permute-done | bytes 294944 | tf_op jit(solution)/shard_map/ppermute | solution.py:32
  130.4 4.0 %head_products.1 = (f32[72,1152]{1,0:T(8,128)S(1)}, bf16[72,1152]{1,0:T(8,128)(2,1)S(1)}, bf16[72,1152]{1,0:T(8,128)(2,1)S(1)}, bf16[72,1152]{1,0:T(8,128)(2,1)S(1)}) custom-call(bf16[288,512]{1,0:T(8,128)(2,1)S(1)} %get-tuple-element.51.refs_0_, bf16[288,512]{1,0:T(8,128)(2,1)S(1)} %collective-permute-done.19.refs_1_, ...), custom_call_target="tpu_custom_call" | custom-call | flops 1358954496 | bytes 8388608 | tf_op jit(solution)/shard_map/head_products/pallas_call | solution.py:251
  134.4 10.2 %collective-permute-start.24 = (bf16[72,1152]{1,0:T(8,128)(2,1)S(1)}, bf16[72,1152]{1,0:T(8,128)(2,1)S(1)}, u32[]{:S(2)}, u32[]{:S(2)}) collective-permute-start(bf16[72,1152]{1,0:T(8,128)(2,1)S(1)} %get-tuple-element.59), channel_id=1, source_target_pairs={{0,4},{1,5},{2,6},{3,7},{4,0},{5,1},{6,2},{7,3},{8,12},{9,13},{10,... | collective-permute-start | bytes 497672 | tf_op jit(solution)/shard_map/ppermute | solution.py:32
  147.6 5.3 %collective-permute-done.25 = bf16[72,1152]{1,0:T(8,128)(2,1)S(1)} collective-permute-done((bf16[72,1152]{1,0:T(8,128)(2,1)S(1)}, bf16[72,1152]{1,0:T(8,128)(2,1)S(1)}, u32[]{:S(2)}, u32[]{:S(2)}) %collective-permute-start.25) | collective-permute-done | bytes 165920 | tf_op jit(solution)/shard_map/ppermute | solution.py:32
  156.1 3.0 %collective-permute-done.27 = bf16[72,1152]{1,0:T(8,128)(2,1)S(1)} collective-permute-done((bf16[72,1152]{1,0:T(8,128)(2,1)S(1)}, bf16[72,1152]{1,0:T(8,128)(2,1)S(1)}, u32[]{:S(2)}, u32[]{:S(2)}) %collective-permute-start.27) | collective-permute-done | bytes 165920 | tf_op jit(solution)/shard_map/ppermute | solution.py:32
  159.1 5.0 %collective-permute-done.28 = bf16[72,1152]{1,0:T(8,128)(2,1)S(1)} collective-permute-done((bf16[72,1152]{1,0:T(8,128)(2,1)S(1)}, bf16[72,1152]{1,0:T(8,128)(2,1)S(1)}, u32[]{:S(2)}, u32[]{:S(2)}) %collective-permute-start.28) | collective-permute-done | bytes 165920 | tf_op jit(solution)/shard_map/ppermute | solution.py:32
  165.1 4.5 %collective-permute-start.31 = (bf16[72,1152]{1,0:T(8,128)(2,1)S(1)}, bf16[72,1152]{1,0:T(8,128)(2,1)S(1)}, u32[]{:S(2)}, u32[]{:S(2)}) collective-permute-start(bf16[72,1152]{1,0:T(8,128)(2,1)S(1)} %add_convert_fusion), channel_id=1, source_target_pairs={{1,4},{3,6},{4,1},{6,3},{9,12},{11,14},{12,9},{14,11},{17,20},{19,... | collective-permute-start | bytes 497672 | tf_op jit(solution)/shard_map/ppermute | solution.py:32
  170.1 3.2 %collective-permute-done.31 = bf16[72,1152]{1,0:T(8,128)(2,1)S(1)} collective-permute-done((bf16[72,1152]{1,0:T(8,128)(2,1)S(1)}, bf16[72,1152]{1,0:T(8,128)(2,1)S(1)}, u32[]{:S(2)}, u32[]{:S(2)}) %collective-permute-start.31) | collective-permute-done | bytes 165920 | tf_op jit(solution)/shard_map/ppermute | solution.py:32
  173.3 2.6 %collective-permute-start.32 = (bf16[2,72,1152]{2,1,0:T(8,128)(2,1)S(1)}, bf16[2,72,1152]{2,1,0:T(8,128)(2,1)S(1)}, u32[]{:S(2)}, u32[]{:S(2)}) collective-permute-start(bf16[2,72,1152]{2,1,0:T(8,128)(2,1)S(1)} %pad_maximum_fusion.1), channel_id=1, source_target_pairs={{0,96},{1,97},{2,98},{3,99},{4,100},{5,101},{6,102},{7,103},{8,104... | collective-permute-start | bytes 995336 | tf_op jit(solution)/shard_map/ppermute | solution.py:32
  177.7 5.6 %collective-permute-done.32 = bf16[2,72,1152]{2,1,0:T(8,128)(2,1)S(1)} collective-permute-done((bf16[2,72,1152]{2,1,0:T(8,128)(2,1)S(1)}, bf16[2,72,1152]{2,1,0:T(8,128)(2,1)S(1)}, u32[]{:S(2)}, u32[]{:S(2)}) %collective-permute-start.32) | collective-permute-done | bytes 331808 | tf_op jit(solution)/shard_map/ppermute | solution.py:32
  183.3 4.8 %collective-permute-done.33 = bf16[2,72,1152]{2,1,0:T(8,128)(2,1)S(1)} collective-permute-done((bf16[2,72,1152]{2,1,0:T(8,128)(2,1)S(1)}, bf16[2,72,1152]{2,1,0:T(8,128)(2,1)S(1)}, u32[]{:S(2)}, u32[]{:S(2)}) %collective-permute-start.33) | collective-permute-done | bytes 331808 | tf_op jit(solution)/shard_map/ppermute | solution.py:32
  188.2 4.2 %collective-permute-done.34 = bf16[2,72,1152]{2,1,0:T(8,128)(2,1)S(1)} collective-permute-done((bf16[2,72,1152]{2,1,0:T(8,128)(2,1)S(1)}, bf16[2,72,1152]{2,1,0:T(8,128)(2,1)S(1)}, u32[]{:S(2)}, u32[]{:S(2)}) %collective-permute-start.34) | collective-permute-done | bytes 331808 | tf_op jit(solution)/shard_map/ppermute | solution.py:32
  (118 shorter events, 47.3 us)
Async XLA Ops:
  4.8 18.3 %collective-permute-start.2 = (bf16[288,1152]{1,0:T(8,128)(2,1)}, bf16[288,1152]{1,0:T(8,128)(2,1)}, u32[]{:S(2)}, u32[]{:S(2)}) collective-permute-start(bf16[288,1152]{1,0:T(8,128)(2,1)} %get-tuple-element.33.refs_0_), channel_id=1, source_target_pairs={{0,2},{1,3},{2,4},{3,5},{4,6},{5,7},{6,0},{7,1},{8,10},{9,11},{10,... | collective-permute-start | bytes 1990664 | tf_op jit(solution)/shard_map/ppermute | solution.py:32
  6.2 17.4 %collective-permute-start.3 = (bf16[288,1152]{1,0:T(8,128)(2,1)}, bf16[288,1152]{1,0:T(8,128)(2,1)}, u32[]{:S(2)}, u32[]{:S(2)}) collective-permute-start(bf16[288,1152]{1,0:T(8,128)(2,1)} %get-tuple-element.35), channel_id=1, source_target_pairs={{0,7},{1,6},{2,1},{3,0},{4,3},{5,2},{6,5},{7,4},{8,15},{9,14},{10,... | collective-permute-start | bytes 1990664 | tf_op jit(solution)/shard_map/ppermute | solution.py:32
  7.8 15.8 %collective-permute-start.1 = (bf16[288,1152]{1,0:T(8,128)(2,1)}, bf16[288,1152]{1,0:T(8,128)(2,1)}, u32[]{:S(2)}, u32[]{:S(2)}) collective-permute-start(bf16[288,1152]{1,0:T(8,128)(2,1)} %get-tuple-element.35), channel_id=1, source_target_pairs={{0,1},{1,0},{2,3},{3,2},{4,5},{5,4},{6,7},{7,6},{8,9},{9,8},{10,11... | collective-permute-start | bytes 1990664 | tf_op jit(solution)/shard_map/ppermute | solution.py:32
  8.2 29.3 %collective-permute-start.10 = (bf16[512,1152]{1,0:T(8,128)(2,1)S(1)}, bf16[512,1152]{1,0:T(8,128)(2,1)S(1)}, u32[]{:S(2)}, u32[]{:S(2)}) collective-permute-start(bf16[512,1152]{1,0:T(8,128)(2,1)S(1)} %pad_maximum_fusion.refs_4_.refs_5_), channel_id=1, source_target_pairs={{0,96},{1,97},{2,98},{3,99},{4,100},{5,101},{6,102},{7,103},{8,104... | collective-permute-start | bytes 3538952 | tf_op jit(solution)/shard_map/ppermute | solution.py:32
  12.1 28.1 %collective-permute-start.9 = (bf16[512,1152]{1,0:T(8,128)(2,1)S(1)}, bf16[512,1152]{1,0:T(8,128)(2,1)S(1)}, u32[]{:S(2)}, u32[]{:S(2)}) collective-permute-start(bf16[512,1152]{1,0:T(8,128)(2,1)S(1)} %pad_maximum_fusion.refs_4_.refs_5_), channel_id=1, source_target_pairs={{0,32},{1,33},{2,34},{3,35},{4,36},{5,37},{6,38},{7,39},{8,40},{9,... | collective-permute-start | bytes 3538952 | tf_op jit(solution)/shard_map/ppermute | solution.py:32
  33.8 6.4 %collective-permute-start.8 = (bf16[512,1152]{1,0:T(8,128)(2,1)S(1)}, bf16[512,1152]{1,0:T(8,128)(2,1)S(1)}, u32[]{:S(2)}, u32[]{:S(2)}) collective-permute-start(bf16[512,1152]{1,0:T(8,128)(2,1)S(1)} %get-tuple-element.38.refs_3_), channel_id=1, source_target_pairs={{0,1},{1,0},{2,3},{3,2},{4,5},{5,4},{6,7},{7,6},{8,9},{9,8},{10,11... | collective-permute-start | bytes 3538952 | tf_op jit(solution)/shard_map/ppermute | solution.py:32
  34.0 16.5 %collective-permute-start.4 = (bf16[512,1152]{1,0:T(8,128)(2,1)S(1)}, bf16[512,1152]{1,0:T(8,128)(2,1)S(1)}, u32[]{:S(2)}, u32[]{:S(2)}) collective-permute-start(bf16[512,1152]{1,0:T(8,128)(2,1)S(1)} %get-tuple-element.38.refs_3_), channel_id=1, source_target_pairs={{1,2},{3,0},{4,7},{6,5},{9,10},{11,8},{12,15},{14,13},{17,18},{19,... | collective-permute-start | bytes 3538952 | tf_op jit(solution)/shard_map/ppermute | solution.py:32
  37.4 16.1 %collective-permute-start.6 = (bf16[512,1152]{1,0:T(8,128)(2,1)S(1)}, bf16[512,1152]{1,0:T(8,128)(2,1)}, u32[]{:S(2)}, u32[]{:S(2)}) collective-permute-start(bf16[512,1152]{1,0:T(8,128)(2,1)S(1)} %get-tuple-element.38.refs_3_), channel_id=1, source_target_pairs={{0,121},{1,8},{2,123},{3,10},{4,125},{5,12},{6,127},{7,14},{8,1},{... | collective-permute-start | bytes 3538952 | tf_op jit(solution)/shard_map/ppermute | solution.py:32
  41.2 19.9 %collective-permute-start.11 = (bf16[512,1152]{1,0:T(8,128)(2,1)S(1)}, bf16[512,1152]{1,0:T(8,128)(2,1)}, u32[]{:S(2)}, u32[]{:S(2)}) collective-permute-start(bf16[512,1152]{1,0:T(8,128)(2,1)S(1)} %get-tuple-element.38.refs_3_), channel_id=1, source_target_pairs={{1,6},{3,4},{4,3},{6,1},{9,14},{11,12},{12,11},{14,9},{17,22},{19,... | collective-permute-start | bytes 3538952 | tf_op jit(solution)/shard_map/ppermute | solution.py:32
  50.5 25.1 %collective-permute-start.5 = (bf16[512,1152]{1,0:T(8,128)(2,1)S(1)}, bf16[512,1152]{1,0:T(8,128)(2,1)}, u32[]{:S(2)}, u32[]{:S(2)}) collective-permute-start(bf16[512,1152]{1,0:T(8,128)(2,1)S(1)} %get-tuple-element.38.refs_3_), channel_id=1, source_target_pairs={{0,3},{2,1},{5,6},{7,4},{8,11},{10,9},{13,14},{15,12},{16,19},{18,... | collective-permute-start | bytes 3538952 | tf_op jit(solution)/shard_map/ppermute | solution.py:32
  53.5 22.0 %collective-permute-start.7 = (bf16[512,1152]{1,0:T(8,128)(2,1)}, bf16[512,1152]{1,0:T(8,128)(2,1)}, u32[]{:S(2)}, u32[]{:S(2)}) collective-permute-start(bf16[512,1152]{1,0:T(8,128)(2,1)} %collective-permute-done.6.refs_5_), channel_id=1, source_target_pairs={{1,7},{3,5},{4,2},{6,0},{9,15},{11,13},{12,10},{14,8},{17,23},{19,... | collective-permute-start | bytes 3538952 | tf_op jit(solution)/shard_map/ppermute | solution.py:32
  62.5 18.6 %collective-permute-start.14 = (bf16[512,1152]{1,0:T(8,128)(2,1)S(1)}, bf16[512,1152]{1,0:T(8,128)(2,1)S(1)}, u32[]{:S(2)}, u32[]{:S(2)}) collective-permute-start(bf16[512,1152]{1,0:T(8,128)(2,1)S(1)} %broadcast_select_fusion.1.refs_6_), channel_id=1, source_target_pairs={{0,8},{1,121},{2,10},{3,123},{4,12},{5,125},{6,14},{7,127},{8,16},... | collective-permute-start | bytes 3538952 | tf_op jit(solution)/shard_map/ppermute | solution.py:32
  75.6 18.6 %collective-permute-start.13 = (bf16[512,1152]{1,0:T(8,128)(2,1)S(1)}, bf16[512,1152]{1,0:T(8,128)(2,1)S(1)}, u32[]{:S(2)}, u32[]{:S(2)}) collective-permute-start(bf16[512,1152]{1,0:T(8,128)(2,1)S(1)} %broadcast_select_fusion.1.refs_6_), channel_id=1, source_target_pairs={{0,6},{2,4},{5,3},{7,1},{8,14},{10,12},{13,11},{15,9},{16,22},{18,... | collective-permute-start | bytes 3538952 | tf_op jit(solution)/shard_map/ppermute | solution.py:32
  78.3 15.9 %collective-permute-start.12 = (bf16[512,1152]{1,0:T(8,128)(2,1)S(1)}, bf16[512,1152]{1,0:T(8,128)(2,1)}, u32[]{:S(2)}, u32[]{:S(2)}) collective-permute-start(bf16[512,1152]{1,0:T(8,128)(2,1)S(1)} %broadcast_select_fusion.refs_5_), channel_id=1, source_target_pairs={{0,8},{1,121},{2,10},{3,123},{4,12},{5,125},{6,14},{7,127},{8,16},... | collective-permute-start | bytes 3538952 | tf_op jit(solution)/shard_map/ppermute | solution.py:32
  81.1 17.3 %collective-permute-start.15 = (bf16[512,1152]{1,0:T(8,128)(2,1)S(1)}, bf16[512,1152]{1,0:T(8,128)(2,1)S(1)}, u32[]{:S(2)}, u32[]{:S(2)}) collective-permute-start(bf16[512,1152]{1,0:T(8,128)(2,1)S(1)} %collective-permute-done.14.refs_4_), channel_id=1, source_target_pairs={{1,3},{3,1},{4,6},{6,4},{9,11},{11,9},{12,14},{14,12},{17,19},{19,... | collective-permute-start | bytes 3538952 | tf_op jit(solution)/shard_map/ppermute | solution.py:32
  98.4 14.7 %collective-permute-start.16 = (bf16[512,1152]{1,0:T(8,128)(2,1)}, bf16[512,1152]{1,0:T(8,128)(2,1)}, u32[]{:S(2)}, u32[]{:S(2)}) collective-permute-start(bf16[512,1152]{1,0:T(8,128)(2,1)} %collective-permute-done.12.refs_4_), channel_id=1, source_target_pairs={{1,7},{3,5},{4,2},{6,0},{9,15},{11,13},{12,10},{14,8},{17,23},{19,... | collective-permute-start | bytes 3538952 | tf_op jit(solution)/shard_map/ppermute | solution.py:32
  100.8 12.4 %collective-permute-start.17 = (bf16[512,1152]{1,0:T(8,128)(2,1)}, bf16[512,1152]{1,0:T(8,128)(2,1)}, u32[]{:S(2)}, u32[]{:S(2)}) collective-permute-start(bf16[512,1152]{1,0:T(8,128)(2,1)} %collective-permute-done.12.refs_4_), channel_id=1, source_target_pairs={{0,2},{2,0},{5,7},{7,5},{8,10},{10,8},{13,15},{15,13},{16,18},{18,... | collective-permute-start | bytes 3538952 | tf_op jit(solution)/shard_map/ppermute | solution.py:32
  104.2 23.4 %collective-permute-start.22 = (bf16[256,1152]{1,0:T(8,128)(2,1)}, bf16[256,1152]{1,0:T(8,128)(2,1)}, u32[]{:S(2)}, u32[]{:S(2)}) collective-permute-start(bf16[256,1152]{1,0:T(8,128)(2,1)} %slice.29), channel_id=1, source_target_pairs={{0,32},{1,33},{2,34},{3,35},{4,36},{5,37},{6,38},{7,39},{8,40},{9,... | collective-permute-start | bytes 1769480 | tf_op jit(solution)/shard_map/ppermute | solution.py:32
  104.2 23.4 %collective-permute-start.23 = (bf16[256,1152]{1,0:T(8,128)(2,1)}, bf16[256,1152]{1,0:T(8,128)(2,1)}, u32[]{:S(2)}, u32[]{:S(2)}) collective-permute-start(bf16[256,1152]{1,0:T(8,128)(2,1)} %slice.30), channel_id=1, source_target_pairs={{0,96},{1,97},{2,98},{3,99},{4,100},{5,101},{6,102},{7,103},{8,104... | collective-permute-start | bytes 1769480 | tf_op jit(solution)/shard_map/ppermute | solution.py:32
  120.3 7.3 %collective-permute-start.21 = (bf16[288,512]{1,0:T(8,128)(2,1)S(1)}, bf16[288,512]{1,0:T(8,128)(2,1)S(1)}, u32[]{:S(2)}, u32[]{:S(2)}) collective-permute-start(bf16[288,512]{1,0:T(8,128)(2,1)S(1)} %get-tuple-element.54), channel_id=1, source_target_pairs={{0,64},{1,65},{2,66},{3,67},{4,68},{5,69},{6,70},{7,71},{8,72},{9,... | collective-permute-start | bytes 884744 | tf_op jit(solution)/shard_map/ppermute | solution.py:32
  120.4 10.0 %collective-permute-start.19 = (bf16[288,512]{1,0:T(8,128)(2,1)S(1)}, bf16[288,512]{1,0:T(8,128)(2,1)S(1)}, u32[]{:S(2)}, u32[]{:S(2)}) collective-permute-start(bf16[288,512]{1,0:T(8,128)(2,1)S(1)} %get-tuple-element.52), channel_id=1, source_target_pairs={{0,32},{1,33},{2,34},{3,35},{4,36},{5,37},{6,38},{7,39},{8,40},{9,... | collective-permute-start | bytes 884744 | tf_op jit(solution)/shard_map/ppermute | solution.py:32
  121.0 9.5 %collective-permute-start.20 = (bf16[288,512]{1,0:T(8,128)(2,1)S(1)}, bf16[288,512]{1,0:T(8,128)(2,1)S(1)}, u32[]{:S(2)}, u32[]{:S(2)}) collective-permute-start(bf16[288,512]{1,0:T(8,128)(2,1)S(1)} %get-tuple-element.53), channel_id=1, source_target_pairs={{0,96},{1,97},{2,98},{3,99},{4,100},{5,101},{6,102},{7,103},{8,104... | collective-permute-start | bytes 884744 | tf_op jit(solution)/shard_map/ppermute | solution.py:32
  134.4 13.1 %collective-permute-start.24 = (bf16[72,1152]{1,0:T(8,128)(2,1)S(1)}, bf16[72,1152]{1,0:T(8,128)(2,1)S(1)}, u32[]{:S(2)}, u32[]{:S(2)}) collective-permute-start(bf16[72,1152]{1,0:T(8,128)(2,1)S(1)} %get-tuple-element.59), channel_id=1, source_target_pairs={{0,4},{1,5},{2,6},{3,7},{4,0},{5,1},{6,2},{7,3},{8,12},{9,13},{10,... | collective-permute-start | bytes 497672 | tf_op jit(solution)/shard_map/ppermute | solution.py:32
  144.7 8.2 %collective-permute-start.25 = (bf16[72,1152]{1,0:T(8,128)(2,1)S(1)}, bf16[72,1152]{1,0:T(8,128)(2,1)S(1)}, u32[]{:S(2)}, u32[]{:S(2)}) collective-permute-start(bf16[72,1152]{1,0:T(8,128)(2,1)S(1)} %get-tuple-element.60), channel_id=1, source_target_pairs={{0,2},{1,3},{2,0},{3,1},{4,6},{5,7},{6,4},{7,5},{8,10},{9,11},{10,... | collective-permute-start | bytes 497672 | tf_op jit(solution)/shard_map/ppermute | solution.py:32
  145.6 7.5 %collective-permute-start.26 = (bf16[72,1152]{1,0:T(8,128)(2,1)S(1)}, bf16[72,1152]{1,0:T(8,128)(2,1)S(1)}, u32[]{:S(2)}, u32[]{:S(2)}) collective-permute-start(bf16[72,1152]{1,0:T(8,128)(2,1)S(1)} %get-tuple-element.61), channel_id=1, source_target_pairs={{0,6},{1,7},{2,4},{3,5},{4,2},{5,3},{6,0},{7,1},{8,14},{9,15},{10,... | collective-permute-start | bytes 497672 | tf_op jit(solution)/shard_map/ppermute | solution.py:32
  153.3 10.8 %collective-permute-start.28 = (bf16[72,1152]{1,0:T(8,128)(2,1)S(1)}, bf16[72,1152]{1,0:T(8,128)(2,1)S(1)}, u32[]{:S(2)}, u32[]{:S(2)}) collective-permute-start(bf16[72,1152]{1,0:T(8,128)(2,1)S(1)} %fusion), channel_id=1, source_target_pairs={{0,8},{1,9},{2,10},{3,11},{4,12},{5,13},{6,14},{7,15},{8,16},{9,17... | collective-permute-start | bytes 497672 | tf_op jit(solution)/shard_map/ppermute | solution.py:32
  154.9 9.3 %collective-permute-start.29 = (bf16[72,1152]{1,0:T(8,128)(2,1)S(1)}, bf16[72,1152]{1,0:T(8,128)(2,1)S(1)}, u32[]{:S(2)}, u32[]{:S(2)}) collective-permute-start(bf16[72,1152]{1,0:T(8,128)(2,1)S(1)} %fusion), channel_id=1, source_target_pairs={{0,24},{1,25},{2,26},{3,27},{4,28},{5,29},{6,30},{7,31},{8,0},{9,1... | collective-permute-start | bytes 497672 | tf_op jit(solution)/shard_map/ppermute | solution.py:32
  165.1 8.2 %collective-permute-start.31 = (bf16[72,1152]{1,0:T(8,128)(2,1)S(1)}, bf16[72,1152]{1,0:T(8,128)(2,1)S(1)}, u32[]{:S(2)}, u32[]{:S(2)}) collective-permute-start(bf16[72,1152]{1,0:T(8,128)(2,1)S(1)} %add_convert_fusion), channel_id=1, source_target_pairs={{1,4},{3,6},{4,1},{6,3},{9,12},{11,14},{12,9},{14,11},{17,20},{19,... | collective-permute-start | bytes 497672 | tf_op jit(solution)/shard_map/ppermute | solution.py:32
  169.7 6.2 %collective-permute-start.18 = (bf16[256,1152]{1,0:T(8,128)(2,1)S(1)}, bf16[256,1152]{1,0:T(8,128)(2,1)S(1)}, u32[]{:S(2)}, u32[]{:S(2)}) collective-permute-start(bf16[256,1152]{1,0:T(8,128)(2,1)S(1)} %slice.28), channel_id=1, source_target_pairs={{0,1},{1,0},{2,3},{3,2},{4,5},{5,4},{6,7},{7,6},{8,9},{9,8},{10,11... | collective-permute-start | bytes 1769480 | tf_op jit(solution)/shard_map/ppermute | solution.py:32
  173.3 9.9 %collective-permute-start.32 = (bf16[2,72,1152]{2,1,0:T(8,128)(2,1)S(1)}, bf16[2,72,1152]{2,1,0:T(8,128)(2,1)S(1)}, u32[]{:S(2)}, u32[]{:S(2)}) collective-permute-start(bf16[2,72,1152]{2,1,0:T(8,128)(2,1)S(1)} %pad_maximum_fusion.1), channel_id=1, source_target_pairs={{0,96},{1,97},{2,98},{3,99},{4,100},{5,101},{6,102},{7,103},{8,104... | collective-permute-start | bytes 995336 | tf_op jit(solution)/shard_map/ppermute | solution.py:32
  177.0 11.1 %collective-permute-start.33 = (bf16[2,72,1152]{2,1,0:T(8,128)(2,1)S(1)}, bf16[2,72,1152]{2,1,0:T(8,128)(2,1)S(1)}, u32[]{:S(2)}, u32[]{:S(2)}) collective-permute-start(bf16[2,72,1152]{2,1,0:T(8,128)(2,1)S(1)} %pad_maximum_fusion.1), channel_id=1, source_target_pairs={{0,64},{1,65},{2,66},{3,67},{4,68},{5,69},{6,70},{7,71},{8,72},{9,... | collective-permute-start | bytes 995336 | tf_op jit(solution)/shard_map/ppermute | solution.py:32
  177.0 15.3 %collective-permute-start.34 = (bf16[2,72,1152]{2,1,0:T(8,128)(2,1)S(1)}, bf16[2,72,1152]{2,1,0:T(8,128)(2,1)S(1)}, u32[]{:S(2)}, u32[]{:S(2)}) collective-permute-start(bf16[2,72,1152]{2,1,0:T(8,128)(2,1)S(1)} %pad_maximum_fusion.1), channel_id=1, source_target_pairs={{0,32},{1,33},{2,34},{3,35},{4,36},{5,37},{6,38},{7,39},{8,40},{9,... | collective-permute-start | bytes 995336 | tf_op jit(solution)/shard_map/ppermute | solution.py:32
  (27 other events, 155.2 us)

commit v3 on v2

--- a/solution.py
+++ b/solution.py
@@ -10,6 +10,8 @@
 WIN = 4
 COST = 10**6
 VMEM = 40 * 2**20
+VMEM_LARGE = 40 * 2**20
+VMEM_SMALL = 24 * 2**20
 AXES = ("z", "x", "yh", "yl", "core")
 SIZES = (4, 4, 2, 2, 2)
 BF = jnp.bfloat16
@@ -73,42 +75,58 @@
 
 
 def embed_kernel(place, own, mate, *refs):
-    parts, (unit, emb, inverse, head, sem) = refs[:4], refs[4:]
+    parts, (unit, emb, inverse), scratch = refs[:4], refs[4:7], refs[7:]
+    pool_v, head_v, unit_v, emb_v, inverse_v, sem, out_sem = scratch
     columns = parts[0].shape[0]
-    copies = []
+    rows = own.shape[0]
+    copies = [
+        pltpu.make_async_copy(own, pool_v.at[pl.ds(0, rows)], sem.at[4]),
+        pltpu.make_async_copy(mate, pool_v.at[pl.ds(rows, rows)], sem.at[5]),
+    ]
     for i, part in enumerate(parts):
         start = pl.multiple_of(place[i] * columns, 16)
-        copies.append(pltpu.make_async_copy(part, head.at[pl.ds(start, columns)], sem.at[i]))
+        copies.append(pltpu.make_async_copy(part, head_v.at[pl.ds(start, columns)], sem.at[i]))
     for copy in copies:
         copy.start()
     for copy in copies:
         copy.wait()
-    rows = own.shape[0]
-    for at, pool in ((0, own), (rows, mate)):
-        raw = dot_nt(pool[...], head[...])
+    outs = []
+    for i in range(2):
+        half = pl.ds(i * rows, rows)
+        raw = dot_nt(pool_v[half, :], head_v[...])
         norm = lax.rsqrt(jnp.sum(raw * raw, axis=1, keepdims=True) + 1e-06)
         raw = raw * norm
-        inverse[at : at + rows, :] = norm
-        unit[at : at + rows, :] = raw
-        emb[at : at + rows, :] = raw.astype(BF)
+        emb_v[half, :] = raw.astype(BF)
+        unit_v[half, :] = raw
+        inverse_v[half, :] = jnp.broadcast_to(norm, (rows, 128))
+        for j, (source, target) in enumerate(((emb_v, emb), (unit_v, unit), (inverse_v, inverse))):
+            outs.append(
+                pltpu.make_async_copy(source.at[half], target.at[half], out_sem.at[3 * i + j])
+            )
+            outs[-1].start()
+    for out in outs:
+        out.wait()
 
 
 def embed(own, mate, parts, place):
     rows, width = own.shape
-    vmem = pl.BlockSpec(memory_space=pltpu.VMEM)
+    shapes = [((2 * rows, width), F32), ((2 * rows, width), BF), ((2 * rows, 128), F32)]
     return pl.pallas_call(
         embed_kernel,
-        in_specs=[pl.BlockSpec(memory_space=pltpu.SMEM), vmem, vmem]
-        + [pl.BlockSpec(memory_space=pl.ANY)] * 4,
-        out_specs=[vmem] * 4,
-        out_shape=[
-            jax.ShapeDtypeStruct((2 * rows, width), F32),
-            jax.ShapeDtypeStruct((2 * rows, width), BF),
-            jax.ShapeDtypeStruct((2 * rows, 1), F32),
-            jax.ShapeDtypeStruct((width, width), BF),
+        in_specs=[pl.BlockSpec(memory_space=pltpu.SMEM)]
+        + [pl.BlockSpec(memory_space=pltpu.HBM)] * 6,
+        out_specs=[pl.BlockSpec(memory_space=pltpu.HBM)] * 3,
+        out_shape=[jax.ShapeDtypeStruct(*shape) for shape in shapes],
+        scratch_shapes=[
+            pltpu.VMEM((2 * rows, width), BF),
+            pltpu.VMEM((width, width), BF),
+            pltpu.VMEM((2 * rows, width), F32),
+            pltpu.VMEM((2 * rows, width), BF),
+            pltpu.VMEM((2 * rows, 128), F32),
+            pltpu.SemaphoreType.DMA((6,)),
+            pltpu.SemaphoreType.DMA((6,)),
         ],
-        scratch_shapes=[pltpu.SemaphoreType.DMA((4,))],
-        compiler_params=pltpu.CompilerParams(vmem_limit_bytes=VMEM),
+        compiler_params=pltpu.CompilerParams(vmem_limit_bytes=VMEM_LARGE),
         cost_estimate=pl.CostEstimate(flops=COST, bytes_accessed=2**20, transcendentals=0),
         name="embed",
     )(place, own, mate, *parts)
@@ -152,7 +170,7 @@
     if "raw" not in ref:
         ref["out"][...] = total
         return
-    unit, inverse = ref["unit"][...], ref["inverse"][...]
+    unit, inverse = ref["unit"][...], ref["inverse"][:, :1]
     grad = total * scale
     inner = jnp.sum(unit * grad, axis=1, keepdims=True)
     raw = (grad - unit * inner) * inverse
@@ -197,7 +215,7 @@
         unit, inverse, order = finish
         names += ["unit", "inverse", "order"]
         args += [unit, inverse, order]
-        specs += [rows, pl.BlockSpec((block, 1), lambda i: (i, 0)), smem]
+        specs += [rows, pl.BlockSpec((block, 128), lambda i: (i, 0)), smem]
         outs = [("raw", (count, width), BF, rows)]
         part = pl.BlockSpec((width // 4, block), lambda i: (0, i))
         outs += [("to%d" % i, (width // 4, count), BF, part) for i in range(4)]
@@ -227,39 +245,33 @@
 
 
 def head_kernel(*refs):
-    lefts, rights, outs = refs[:4], refs[4:12], refs[12:]
-    depth = rights[0].shape[0]
+    lefts, rights, outs = refs[:4], refs[4:9], refs[9:]
+    half = rights[0].shape[0] // 2
     total = None
-    for place, right in enumerate(rights):
-        side = place % 2
-        left = lefts[place // 2][:, side * depth : (side + 1) * depth]
-        term = jnp.dot(left, right[...], preferred_element_type=F32)
+    for left, right in zip(lefts[:3], rights[:3]):
+        term = dot_nn(left[...], right[...])
         total = term if total is None else total + term
+    total = total + dot_nn(lefts[3][:, :half], rights[3][...])
+    total = total + dot_nn(lefts[3][:, half:], rights[4][...])
     piece = outs[0].shape[0]
     outs[0][...] = total[:piece]
-    for place in range(1, 4):
-        outs[place][...] = total[place * piece : (place + 1) * piece].astype(BF)
+    for i in range(1, 4):
+        outs[i][...] = total[i * piece : (i + 1) * piece].astype(BF)
 
 
 def head_products(lefts, rights):
     columns, count = lefts[0].shape
     width = rights[0].shape[1]
-    depth = count // 2
-    tile = 384
     piece = columns // 4
-    out = pl.BlockSpec((piece, tile), lambda i: (0, i))
+    vmem = pl.BlockSpec(memory_space=pltpu.VMEM)
     mine, *sends = pl.pallas_call(
         head_kernel,
-        grid=(width // tile,),
-        in_specs=[pl.BlockSpec((columns, count), lambda i: (0, 0))] * 4
-        + [pl.BlockSpec((depth, tile), lambda i, at=at: (at, i)) for at in (0, 1, 0, 1, 0, 1, 0, 0)],
-        out_specs=[out] * 4,
+        in_specs=[vmem] * 9,
+        out_specs=[vmem] * 4,
         out_shape=[jax.ShapeDtypeStruct((piece, width), F32)]
         + [jax.ShapeDtypeStruct((piece, width), BF)] * 3,
-        compiler_params=pltpu.CompilerParams(vmem_limit_bytes=VMEM),
-        cost_estimate=pl.CostEstimate(
-            flops=8 * columns * count * width, bytes_accessed=8 * 2**20, transcendentals=0
-        ),
+        compiler_params=pltpu.CompilerParams(vmem_limit_bytes=VMEM_SMALL),
+        cost_estimate=pl.CostEstimate(flops=COST, bytes_accessed=2**20, transcendentals=0),
         name="head_products",
     )(*lefts, *rights)
     return mine, sends
@@ -290,9 +302,8 @@
     place = jnp.stack(
         [2 * half + core, 2 * half + 1 - core, 2 * far + core, 2 * far + 1 - core]
     ).astype(jnp.int32)
-    unit, emb, inverse, head = embed(
-        pool_own, pool_mate, (head_own, head_mate, head_up, head_down), place
-    )
+    parts = (head_own, head_mate, head_up, head_down)
+    unit, emb, inverse = embed(pool_own, pool_mate, parts, place)
 
     odd_block = jnp.where(first, odd, 1 - odd)
     is_odd = odd_block == 1
@@ -334,14 +345,17 @@
     part2 = moved(pieces[2], hop(dz=2))
     part1 = moved(pieces[1], hop(dz=1))
     part3 = moved(pieces[3], hop(dz=-1))
+    head = jnp.zeros((width, width), BF)
+    for i in range(4):
+        head = lax.dynamic_update_slice(head, parts[i], (place[i] * columns, 0))
     grad_pool = dot_nn(raw_grad, head).astype(BF)
+    part2, grad_pool = lax.optimization_barrier((part2, grad_pool))
     pool_back = moved(grad_pool[rows:], hop(swap=1))
     grad_image = jnp.where(first, grad_pool[:rows], pool_back)
     grad_text = jnp.where(first, pool_back, grad_pool[:rows])
-    part2, grad_pool = lax.optimization_barrier((part2, grad_pool))
     mine, sends = head_products(
         (pieces[0], part1, part3, part2),
-        (pool, pool, pool_z1, pool_z1, pool_z3, pool_z3, own_z2, mate_z2),
+        (pool, pool_z1, pool_z3, own_z2, mate_z2),
     )
 
     def y_partner(bits):
@@ -350,7 +364,7 @@
     got = [moved(out, y_partner(bits)) for out, bits in zip(sends, (2, 1, 3))]
     for part in got:
         mine = mine + part.astype(F32)
-    narrow = mine.astype(BF)
+    narrow = after(mine.astype(BF), pool_back)
     for part in [moved(narrow, hop(dx=2)), moved(narrow, hop(dx=1)), moved(narrow, hop(dx=-1))]:
         mine = mine + part.astype(F32)
     narrow = mine.astype(BF)
@@ -367,6 +381,7 @@
     same = jnp.where(here, narrow, one)
     other = jnp.where(here, one, two)
     pair = jnp.stack([jnp.where(first, same, other), jnp.where(first, other, same)])
+    pair, grad_image, grad_text = lax.optimization_barrier((pair, grad_image, grad_text))
     across = moved(pair, hop(dz=2))
     ring = [pair, moved(pair, hop(dz=-1)), across, moved(pair, hop(dz=1))]
     ring = jnp.stack(ring + ring, axis=1)

time: 195 us -> 191 us (0.979)
  local copies, waits for them, and re-layouts: 13.6 us -> 11.5 us
    unnamed x53 -> x55, local copies, waits for them, and re-layouts: 10.1 us -> 7.76 us
    pallas_call x1, Pallas kernels: 3.99 us -> 1.69 us  [head_products(): pl.pallas_call(head_kernel, in_specs=[vmem] * 9, out_specs=[vmem] * 4, ou...]
  transfers between devices with their start and end apart: 35 -> 35, of which waited for: 22 -> 19; matrix products, arithmetic and copies ran while one was open for 5% -> 5% of each run, Pallas kernels for 13% -> 14%
where the time goes in v3:
time: 191 us; the launch traced here: 190 us
  waiting for transfers between devices  69 us (36%)
  starting transfers between devices  68.7 us (36%)
  Pallas kernels  28.7 us (15%)
  local copies, waits for them, and re-layouts  11.5 us (6%)
  other arithmetic  8.13 us (4%)
  between operations  2.41 us (1%)
    ppermute x35, waiting for transfers between devices, moved(): return lax.ppermute(block, AXES, pairs)  69 us
    ppermute x35, starting transfers between devices, moved(): return lax.ppermute(block, AXES, pairs)  68.7 us
    pallas_call x4, Pallas kernels, sums(): pl.pallas_call(functools.partial(sums_kernel, (tuple(names), tuple(plan),...  21.3 us
    unnamed x55, local copies, waits for them, and re-layouts  7.76 us
    pallas_call x1, Pallas kernels, embed(): pl.pallas_call(embed_kernel, in_specs=[pl.BlockSpec(memory_space=pltpu.SM...  5.79 us
  transfers between devices with their start and end apart: 35, of which 19 were waited for; matrix products, arithmetic and copies ran while one was open for 5% of the time, Pallas kernels for 14%

profile of v3, /device:TPU:1, one launch (start us, length us, event | category | flops | bytes accessed | tf_op | source)
XLA Modules:
  0.0 190.3 jit_solution(8997628142474980982)
XLA Ops:
  9.1 3.8 %collective-permute-start.10 = (bf16[512,1152]{1,0:T(8,128)(2,1)S(1)}, bf16[512,1152]{1,0:T(8,128)(2,1)S(1)}, u32[]{:S(2)}, u32[]{:S(2)}) collective-permute-start(bf16[512,1152]{1,0:T(8,128)(2,1)S(1)} %pad_maximum_fusion.refs_4_), channel_id=1, source_target_pairs={{0,96},{1,97},{2,98},{3,99},{4,100},{5,101},{6,102},{7,103},{8,104... | collective-permute-start | bytes 3538952 | tf_op jit(solution)/shard_map/ppermute | solution.py:34
  12.9 9.7 %collective-permute-done.2.refs_2_ = bf16[288,1152]{1,0:T(8,128)(2,1)S(1)} collective-permute-done((bf16[288,1152]{1,0:T(8,128)(2,1)S(1)}, bf16[288,1152]{1,0:T(8,128)(2,1)S(1)}, u32[]{:S(2)}, u32[]{:S(2)}) %collective-permute-start.2) | collective-permute-done | bytes 663584 | tf_op jit(solution)/shard_map/ppermute | solution.py:34
  24.8 5.8 %embed.1 = (f32[512,1152]{1,0:T(8,128)S(1)}, bf16[512,1152]{1,0:T(8,128)(2,1)S(1)}, f32[512,128]{1,0:T(8,128)S(1)}) custom-call(s32[4]{0:T(128)S(1)} %pad_add_fusion.place, bf16[256,1152]{1,0:T(8,128)(2,1)S(1)} %get-tuple-element.77.own, bf16[256,1152]{1,0:T(8,128)(2,1)} %collective-permute-done.mate, bf16[288,1152]{1,0:T(8,128)(2,1)S(1)} %get-tuple-element.37.refs_0_, ...), custom_call_target="tpu_custom_call" | custom-call | flops 1000000 | bytes 1048576 | tf_op jit(solution)/shard_map/embed/pallas_call | solution.py:114
  33.4 2.9 %collective-permute-start.4 = (bf16[512,1152]{1,0:T(8,128)(2,1)S(1)}, bf16[512,1152]{1,0:T(8,128)(2,1)S(1)}, u32[]{:S(2)}, u32[]{:S(2)}) collective-permute-start(bf16[512,1152]{1,0:T(8,128)(2,1)S(1)} %get-tuple-element.42.refs_3_), channel_id=1, source_target_pairs={{1,2},{3,0},{4,7},{6,5},{9,10},{11,8},{12,15},{14,13},{17,18},{19,... | collective-permute-start | bytes 3538952 | tf_op jit(solution)/shard_map/ppermute | solution.py:34
  38.0 3.1 %collective-permute-done.9.refs_5_ = bf16[512,1152]{1,0:T(8,128)(2,1)S(1)} collective-permute-done((bf16[512,1152]{1,0:T(8,128)(2,1)S(1)}, bf16[512,1152]{1,0:T(8,128)(2,1)S(1)}, u32[]{:S(2)}, u32[]{:S(2)}) %collective-permute-start.9) | collective-permute-done | bytes 1179680 | tf_op jit(solution)/shard_map/ppermute | solution.py:34
  41.0 4.7 %collective-permute-start.11 = (bf16[512,1152]{1,0:T(8,128)(2,1)S(1)}, bf16[512,1152]{1,0:T(8,128)(2,1)}, u32[]{:S(2)}, u32[]{:S(2)}) collective-permute-start(bf16[512,1152]{1,0:T(8,128)(2,1)S(1)} %get-tuple-element.42.refs_3_), channel_id=1, source_target_pairs={{1,6},{3,4},{4,3},{6,1},{9,14},{11,12},{12,11},{14,9},{17,22},{19,... | collective-permute-start | bytes 3538952 | tf_op jit(solution)/shard_map/ppermute | solution.py:34
  45.8 3.6 %collective-permute-done.4 = bf16[512,1152]{1,0:T(8,128)(2,1)S(1)} collective-permute-done((bf16[512,1152]{1,0:T(8,128)(2,1)S(1)}, bf16[512,1152]{1,0:T(8,128)(2,1)S(1)}, u32[]{:S(2)}, u32[]{:S(2)}) %collective-permute-start.4) | collective-permute-done | bytes 1179680 | tf_op jit(solution)/shard_map/ppermute | solution.py:34
  52.4 6.0 %collective-permute-start.7 = (bf16[512,1152]{1,0:T(8,128)(2,1)}, bf16[512,1152]{1,0:T(8,128)(2,1)}, u32[]{:S(2)}, u32[]{:S(2)}) collective-permute-start(bf16[512,1152]{1,0:T(8,128)(2,1)} %collective-permute-done.6.refs_5_), channel_id=1, source_target_pairs={{1,7},{3,5},{4,2},{6,0},{9,15},{11,13},{12,10},{14,8},{17,23},{19,... | collective-permute-start | bytes 3538952 | tf_op jit(solution)/shard_map/ppermute | solution.py:34
  61.3 4.8 %collective-permute-start.14 = (bf16[512,1152]{1,0:T(8,128)(2,1)S(1)}, bf16[512,1152]{1,0:T(8,128)(2,1)S(1)}, u32[]{:S(2)}, u32[]{:S(2)}) collective-permute-start(bf16[512,1152]{1,0:T(8,128)(2,1)S(1)} %broadcast_select_fusion.1.refs_6_), channel_id=1, source_target_pairs={{0,8},{1,121},{2,10},{3,123},{4,12},{5,125},{6,14},{7,127},{8,16},... | collective-permute-start | bytes 3538952 | tf_op jit(solution)/shard_map/ppermute | solution.py:34
  67.4 6.8 %sums.3.refs_6_ = f32[512,1152]{1,0:T(8,128)S(1)} custom-call(f32[1]{0:T(128)S(6)} %copy.21.refs_0_, f32[1]{0:T(128)S(6)} %copy.22.refs_1_, s32[1]{0:T(128)} %bitcast.refs_2_, bf16[512,1152]{1,0:T(8,128)(2,1)S(1)} %get-tuple-element.42.refs_3_, bf16[512,1152]{1,0:T(8,128)(2,1)S(1)} %collective-permute-done.8.refs_4_, ...), custom_call_target="tpu_custom_call" | custom-call | flops 1000000 | bytes 1048576 | tf_op jit(solution)/shard_map/sums/pallas_call | solution.py:233
  76.9 2.9 %collective-permute-start.12 = (bf16[512,1152]{1,0:T(8,128)(2,1)S(1)}, bf16[512,1152]{1,0:T(8,128)(2,1)}, u32[]{:S(2)}, u32[]{:S(2)}) collective-permute-start(bf16[512,1152]{1,0:T(8,128)(2,1)S(1)} %broadcast_select_fusion.refs_5_), channel_id=1, source_target_pairs={{0,8},{1,121},{2,10},{3,123},{4,12},{5,125},{6,14},{7,127},{8,16},... | collective-permute-start | bytes 3538952 | tf_op jit(solution)/shard_map/ppermute | solution.py:34
  81.7 3.9 %sums.4.refs_5_ = f32[512,1152]{1,0:T(8,128)S(1)} custom-call(f32[1]{0:T(128)S(6)} %copy.21.refs_0_, f32[1]{0:T(128)S(6)} %copy.22.refs_1_, s32[1]{0:T(128)} %bitcast.refs_2_, bf16[512,1152]{1,0:T(8,128)(2,1)S(1)} %get-tuple-element.42.refs_3_, bf16[512,1152]{1,0:T(8,128)(2,1)S(1)} %collective-permute-done.14.refs_4_, ...), custom_call_target="tpu_custom_call" | custom-call | flops 1000000 | bytes 1048576 | tf_op jit(solution)/shard_map/sums/pallas_call | solution.py:233
  85.7 7.1 %collective-permute-done.13.refs_4_ = bf16[512,1152]{1,0:T(8,128)(2,1)S(1)} collective-permute-done((bf16[512,1152]{1,0:T(8,128)(2,1)S(1)}, bf16[512,1152]{1,0:T(8,128)(2,1)S(1)}, u32[]{:S(2)}, u32[]{:S(2)}) %collective-permute-start.13) | collective-permute-done | bytes 1179680 | tf_op jit(solution)/shard_map/ppermute | solution.py:34
  93.8 3.4 %collective-permute-done.15.refs_6_ = bf16[512,1152]{1,0:T(8,128)(2,1)S(1)} collective-permute-done((bf16[512,1152]{1,0:T(8,128)(2,1)S(1)}, bf16[512,1152]{1,0:T(8,128)(2,1)S(1)}, u32[]{:S(2)}, u32[]{:S(2)}) %collective-permute-start.15) | collective-permute-done | bytes 1179680 | tf_op jit(solution)/shard_map/ppermute | solution.py:34
  98.2 2.3 %collective-permute-start.16 = (bf16[512,1152]{1,0:T(8,128)(2,1)}, bf16[512,1152]{1,0:T(8,128)(2,1)}, u32[]{:S(2)}, u32[]{:S(2)}) collective-permute-start(bf16[512,1152]{1,0:T(8,128)(2,1)} %collective-permute-done.12.refs_4_), channel_id=1, source_target_pairs={{1,7},{3,5},{4,2},{6,0},{9,15},{11,13},{12,10},{14,8},{17,23},{19,... | collective-permute-start | bytes 3538952 | tf_op jit(solution)/shard_map/ppermute | solution.py:34
  105.4 2.7 %collective-permute-start.22 = (bf16[256,1152]{1,0:T(8,128)(2,1)S(1)}, bf16[256,1152]{1,0:T(8,128)(2,1)S(1)}, u32[]{:S(2)}, u32[]{:S(2)}) collective-permute-start(bf16[256,1152]{1,0:T(8,128)(2,1)S(1)} %slice.28), channel_id=1, source_target_pairs={{0,96},{1,97},{2,98},{3,99},{4,100},{5,101},{6,102},{7,103},{8,104... | collective-permute-start | bytes 1769480 | tf_op jit(solution)/shard_map/ppermute | solution.py:34
  108.2 3.6 %sums.5.refs_8_ = f32[512,1152]{1,0:T(8,128)S(1)} custom-call(f32[1]{0:T(128)S(6)} %copy.21.refs_0_, f32[1]{0:T(128)S(6)} %copy.22.refs_1_, s32[1]{0:T(128)} %bitcast.refs_2_, bf16[512,1152]{1,0:T(8,128)(2,1)S(1)} %get-tuple-element.42.refs_3_, bf16[512,1152]{1,0:T(8,128)(2,1)} %collective-permute-done.12.refs_4_, f32[512,1152]{1,0:T(8,128)S(1)} %sums.4.refs_5_), custom_call_target="tpu_custom_call" | custom-call | flops 1000000 | bytes 1048576 | tf_op jit(solution)/shard_map/sums/pallas_call | solution.py:233
  112.9 6.9 %finish.1 = (bf16[512,1152]{1,0:T(8,128)(2,1)S(1)}, bf16[288,512]{1,0:T(8,128)(2,1)S(1)}, bf16[288,512]{1,0:T(8,128)(2,1)S(1)}, bf16[288,512]{1,0:T(8,128)(2,1)S(1)}, bf16[288,512]{1,0:T(8,128)(2,1)S(1)}) custom-call(f32[1]{0:T(128)S(6)} %copy.21.refs_0_, f32[1]{0:T(128)S(6)} %copy.22.refs_1_, s32[1]{0:T(128)} %bitcast.refs_2_, ...), custom_call_target="tpu_custom_call" | custom-call | flops 1000000 | bytes 1048576 | tf_op jit(solution)/shard_map/finish/pallas_call | solution.py:233
  120.6 2.1 %collective-permute-start.19 = (bf16[288,512]{1,0:T(8,128)(2,1)S(1)}, bf16[288,512]{1,0:T(8,128)(2,1)S(1)}, u32[]{:S(2)}, u32[]{:S(2)}) collective-permute-start(bf16[288,512]{1,0:T(8,128)(2,1)S(1)} %get-tuple-element.55), channel_id=1, source_target_pairs={{0,96},{1,97},{2,98},{3,99},{4,100},{5,101},{6,102},{7,103},{8,104... | collective-permute-start | bytes 884744 | tf_op jit(solution)/shard_map/ppermute | solution.py:34
  124.5 2.6 %collective-permute-done.20.refs_3_ = bf16[288,512]{1,0:T(8,128)(2,1)S(1)} collective-permute-done((bf16[288,512]{1,0:T(8,128)(2,1)S(1)}, bf16[288,512]{1,0:T(8,128)(2,1)S(1)}, u32[]{:S(2)}, u32[]{:S(2)}) %collective-permute-start.20) | collective-permute-done | bytes 294944 | tf_op jit(solution)/shard_map/ppermute | solution.py:34
  127.1 2.8 %collective-permute-done.18.refs_1_ = bf16[288,512]{1,0:T(8,128)(2,1)S(1)} collective-permute-done((bf16[288,512]{1,0:T(8,128)(2,1)S(1)}, bf16[288,512]{1,0:T(8,128)(2,1)S(1)}, u32[]{:S(2)}, u32[]{:S(2)}) %collective-permute-start.18) | collective-permute-done | bytes 294944 | tf_op jit(solution)/shard_map/ppermute | solution.py:34
  131.7 9.9 %collective-permute-start.23 = (bf16[72,1152]{1,0:T(8,128)(2,1)S(1)}, bf16[72,1152]{1,0:T(8,128)(2,1)S(1)}, u32[]{:S(2)}, u32[]{:S(2)}) collective-permute-start(bf16[72,1152]{1,0:T(8,128)(2,1)S(1)} %get-tuple-element.62), channel_id=1, source_target_pairs={{0,4},{1,5},{2,6},{3,7},{4,0},{5,1},{6,2},{7,3},{8,12},{9,13},{10,... | collective-permute-start | bytes 497672 | tf_op jit(solution)/shard_map/ppermute | solution.py:34
  144.6 5.2 %collective-permute-done.24 = bf16[72,1152]{1,0:T(8,128)(2,1)S(1)} collective-permute-done((bf16[72,1152]{1,0:T(8,128)(2,1)S(1)}, bf16[72,1152]{1,0:T(8,128)(2,1)S(1)}, u32[]{:S(2)}, u32[]{:S(2)}) %collective-permute-start.24) | collective-permute-done | bytes 165920 | tf_op jit(solution)/shard_map/ppermute | solution.py:34
  150.5 2.1 %collective-permute-start.28 = (bf16[72,1152]{1,0:T(8,128)(2,1)S(1)}, bf16[72,1152]{1,0:T(8,128)(2,1)S(1)}, u32[]{:S(2)}, u32[]{:S(2)}) collective-permute-start(bf16[72,1152]{1,0:T(8,128)(2,1)S(1)} %fusion), channel_id=1, source_target_pairs={{0,8},{1,9},{2,10},{3,11},{4,12},{5,13},{6,14},{7,15},{8,16},{9,17... | collective-permute-start | bytes 497672 | tf_op jit(solution)/shard_map/ppermute | solution.py:34
  153.3 3.4 %collective-permute-done.27 = bf16[72,1152]{1,0:T(8,128)(2,1)S(1)} collective-permute-done((bf16[72,1152]{1,0:T(8,128)(2,1)S(1)}, bf16[72,1152]{1,0:T(8,128)(2,1)S(1)}, u32[]{:S(2)}, u32[]{:S(2)}) %collective-permute-start.27) | collective-permute-done | bytes 165920 | tf_op jit(solution)/shard_map/ppermute | solution.py:34
  156.6 4.7 %collective-permute-done.28 = bf16[72,1152]{1,0:T(8,128)(2,1)S(1)} collective-permute-done((bf16[72,1152]{1,0:T(8,128)(2,1)S(1)}, bf16[72,1152]{1,0:T(8,128)(2,1)S(1)}, u32[]{:S(2)}, u32[]{:S(2)}) %collective-permute-start.28) | collective-permute-done | bytes 165920 | tf_op jit(solution)/shard_map/ppermute | solution.py:34
  162.3 4.3 %collective-permute-start.31 = (bf16[72,1152]{1,0:T(8,128)(2,1)S(1)}, bf16[72,1152]{1,0:T(8,128)(2,1)S(1)}, u32[]{:S(2)}, u32[]{:S(2)}) collective-permute-start(bf16[72,1152]{1,0:T(8,128)(2,1)S(1)} %add_convert_fusion), channel_id=1, source_target_pairs={{1,4},{3,6},{4,1},{6,3},{9,12},{11,14},{12,9},{14,11},{17,20},{19,... | collective-permute-start | bytes 497672 | tf_op jit(solution)/shard_map/ppermute | solution.py:34
  167.7 2.7 %collective-permute-done.31 = bf16[72,1152]{1,0:T(8,128)(2,1)S(1)} collective-permute-done((bf16[72,1152]{1,0:T(8,128)(2,1)S(1)}, bf16[72,1152]{1,0:T(8,128)(2,1)S(1)}, u32[]{:S(2)}, u32[]{:S(2)}) %collective-permute-start.31) | collective-permute-done | bytes 165920 | tf_op jit(solution)/shard_map/ppermute | solution.py:34
  170.5 2.6 %collective-permute-start.32 = (bf16[2,72,1152]{2,1,0:T(8,128)(2,1)S(1)}, bf16[2,72,1152]{2,1,0:T(8,128)(2,1)S(1)}, u32[]{:S(2)}, u32[]{:S(2)}) collective-permute-start(bf16[2,72,1152]{2,1,0:T(8,128)(2,1)S(1)} %pad_maximum_fusion.1), channel_id=1, source_target_pairs={{0,96},{1,97},{2,98},{3,99},{4,100},{5,101},{6,102},{7,103},{8,104... | collective-permute-start | bytes 995336 | tf_op jit(solution)/shard_map/ppermute | solution.py:34
  173.8 6.7 %collective-permute-done.32 = bf16[2,72,1152]{2,1,0:T(8,128)(2,1)S(1)} collective-permute-done((bf16[2,72,1152]{2,1,0:T(8,128)(2,1)S(1)}, bf16[2,72,1152]{2,1,0:T(8,128)(2,1)S(1)}, u32[]{:S(2)}, u32[]{:S(2)}) %collective-permute-start.32) | collective-permute-done | bytes 331808 | tf_op jit(solution)/shard_map/ppermute | solution.py:34
  180.5 3.7 %collective-permute-done.33 = bf16[2,72,1152]{2,1,0:T(8,128)(2,1)S(1)} collective-permute-done((bf16[2,72,1152]{2,1,0:T(8,128)(2,1)S(1)}, bf16[2,72,1152]{2,1,0:T(8,128)(2,1)S(1)}, u32[]{:S(2)}, u32[]{:S(2)}) %collective-permute-start.33) | collective-permute-done | bytes 331808 | tf_op jit(solution)/shard_map/ppermute | solution.py:34
  184.2 4.0 %collective-permute-done.34 = bf16[2,72,1152]{2,1,0:T(8,128)(2,1)S(1)} collective-permute-done((bf16[2,72,1152]{2,1,0:T(8,128)(2,1)S(1)}, bf16[2,72,1152]{2,1,0:T(8,128)(2,1)S(1)}, u32[]{:S(2)}, u32[]{:S(2)}) %collective-permute-start.34) | collective-permute-done | bytes 331808 | tf_op jit(solution)/shard_map/ppermute | solution.py:34
  (123 shorter events, 47.1 us)
Async XLA Ops:
  4.6 18.0 %collective-permute-start.2 = (bf16[288,1152]{1,0:T(8,128)(2,1)S(1)}, bf16[288,1152]{1,0:T(8,128)(2,1)S(1)}, u32[]{:S(2)}, u32[]{:S(2)}) collective-permute-start(bf16[288,1152]{1,0:T(8,128)(2,1)S(1)} %get-tuple-element.37.refs_0_), channel_id=1, source_target_pairs={{0,2},{1,3},{2,4},{3,5},{4,6},{5,7},{6,0},{7,1},{8,10},{9,11},{10,... | collective-permute-start | bytes 1990664 | tf_op jit(solution)/shard_map/ppermute | solution.py:34
  6.0 17.4 %collective-permute-start.3 = (bf16[288,1152]{1,0:T(8,128)(2,1)}, bf16[288,1152]{1,0:T(8,128)(2,1)S(1)}, u32[]{:S(2)}, u32[]{:S(2)}) collective-permute-start(bf16[288,1152]{1,0:T(8,128)(2,1)} %get-tuple-element.39), channel_id=1, source_target_pairs={{0,7},{1,6},{2,1},{3,0},{4,3},{5,2},{6,5},{7,4},{8,15},{9,14},{10,... | collective-permute-start | bytes 1990664 | tf_op jit(solution)/shard_map/ppermute | solution.py:34
  7.5 15.9 %collective-permute-start.1 = (bf16[288,1152]{1,0:T(8,128)(2,1)}, bf16[288,1152]{1,0:T(8,128)(2,1)}, u32[]{:S(2)}, u32[]{:S(2)}) collective-permute-start(bf16[288,1152]{1,0:T(8,128)(2,1)} %get-tuple-element.39), channel_id=1, source_target_pairs={{0,1},{1,0},{2,3},{3,2},{4,5},{5,4},{6,7},{7,6},{8,9},{9,8},{10,11... | collective-permute-start | bytes 1990664 | tf_op jit(solution)/shard_map/ppermute | solution.py:34
  9.1 28.9 %collective-permute-start.10 = (bf16[512,1152]{1,0:T(8,128)(2,1)S(1)}, bf16[512,1152]{1,0:T(8,128)(2,1)S(1)}, u32[]{:S(2)}, u32[]{:S(2)}) collective-permute-start(bf16[512,1152]{1,0:T(8,128)(2,1)S(1)} %pad_maximum_fusion.refs_4_), channel_id=1, source_target_pairs={{0,96},{1,97},{2,98},{3,99},{4,100},{5,101},{6,102},{7,103},{8,104... | collective-permute-start | bytes 3538952 | tf_op jit(solution)/shard_map/ppermute | solution.py:34
  12.9 28.2 %collective-permute-start.9 = (bf16[512,1152]{1,0:T(8,128)(2,1)S(1)}, bf16[512,1152]{1,0:T(8,128)(2,1)S(1)}, u32[]{:S(2)}, u32[]{:S(2)}) collective-permute-start(bf16[512,1152]{1,0:T(8,128)(2,1)S(1)} %pad_maximum_fusion.refs_4_), channel_id=1, source_target_pairs={{0,32},{1,33},{2,34},{3,35},{4,36},{5,37},{6,38},{7,39},{8,40},{9,... | collective-permute-start | bytes 3538952 | tf_op jit(solution)/shard_map/ppermute | solution.py:34
  32.7 8.4 %collective-permute-start.8 = (bf16[512,1152]{1,0:T(8,128)(2,1)S(1)}, bf16[512,1152]{1,0:T(8,128)(2,1)S(1)}, u32[]{:S(2)}, u32[]{:S(2)}) collective-permute-start(bf16[512,1152]{1,0:T(8,128)(2,1)S(1)} %get-tuple-element.42.refs_3_), channel_id=1, source_target_pairs={{0,1},{1,0},{2,3},{3,2},{4,5},{5,4},{6,7},{7,6},{8,9},{9,8},{10,11... | collective-permute-start | bytes 3538952 | tf_op jit(solution)/shard_map/ppermute | solution.py:34
  33.4 15.9 %collective-permute-start.4 = (bf16[512,1152]{1,0:T(8,128)(2,1)S(1)}, bf16[512,1152]{1,0:T(8,128)(2,1)S(1)}, u32[]{:S(2)}, u32[]{:S(2)}) collective-permute-start(bf16[512,1152]{1,0:T(8,128)(2,1)S(1)} %get-tuple-element.42.refs_3_), channel_id=1, source_target_pairs={{1,2},{3,0},{4,7},{6,5},{9,10},{11,8},{12,15},{14,13},{17,18},{19,... | collective-permute-start | bytes 3538952 | tf_op jit(solution)/shard_map/ppermute | solution.py:34
  36.3 16.1 %collective-permute-start.6 = (bf16[512,1152]{1,0:T(8,128)(2,1)S(1)}, bf16[512,1152]{1,0:T(8,128)(2,1)}, u32[]{:S(2)}, u32[]{:S(2)}) collective-permute-start(bf16[512,1152]{1,0:T(8,128)(2,1)S(1)} %get-tuple-element.42.refs_3_), channel_id=1, source_target_pairs={{0,121},{1,8},{2,123},{3,10},{4,125},{5,12},{6,127},{7,14},{8,1},{... | collective-permute-start | bytes 3538952 | tf_op jit(solution)/shard_map/ppermute | solution.py:34
  41.0 18.8 %collective-permute-start.11 = (bf16[512,1152]{1,0:T(8,128)(2,1)S(1)}, bf16[512,1152]{1,0:T(8,128)(2,1)}, u32[]{:S(2)}, u32[]{:S(2)}) collective-permute-start(bf16[512,1152]{1,0:T(8,128)(2,1)S(1)} %get-tuple-element.42.refs_3_), channel_id=1, source_target_pairs={{1,6},{3,4},{4,3},{6,1},{9,14},{11,12},{12,11},{14,9},{17,22},{19,... | collective-permute-start | bytes 3538952 | tf_op jit(solution)/shard_map/ppermute | solution.py:34
  49.3 24.9 %collective-permute-start.5 = (bf16[512,1152]{1,0:T(8,128)(2,1)S(1)}, bf16[512,1152]{1,0:T(8,128)(2,1)}, u32[]{:S(2)}, u32[]{:S(2)}) collective-permute-start(bf16[512,1152]{1,0:T(8,128)(2,1)S(1)} %get-tuple-element.42.refs_3_), channel_id=1, source_target_pairs={{0,3},{2,1},{5,6},{7,4},{8,11},{10,9},{13,14},{15,12},{16,19},{18,... | collective-permute-start | bytes 3538952 | tf_op jit(solution)/shard_map/ppermute | solution.py:34
  52.4 21.8 %collective-permute-start.7 = (bf16[512,1152]{1,0:T(8,128)(2,1)}, bf16[512,1152]{1,0:T(8,128)(2,1)}, u32[]{:S(2)}, u32[]{:S(2)}) collective-permute-start(bf16[512,1152]{1,0:T(8,128)(2,1)} %collective-permute-done.6.refs_5_), channel_id=1, source_target_pairs={{1,7},{3,5},{4,2},{6,0},{9,15},{11,13},{12,10},{14,8},{17,23},{19,... | collective-permute-start | bytes 3538952 | tf_op jit(solution)/shard_map/ppermute | solution.py:34
  61.3 18.5 %collective-permute-start.14 = (bf16[512,1152]{1,0:T(8,128)(2,1)S(1)}, bf16[512,1152]{1,0:T(8,128)(2,1)S(1)}, u32[]{:S(2)}, u32[]{:S(2)}) collective-permute-start(bf16[512,1152]{1,0:T(8,128)(2,1)S(1)} %broadcast_select_fusion.1.refs_6_), channel_id=1, source_target_pairs={{0,8},{1,121},{2,10},{3,123},{4,12},{5,125},{6,14},{7,127},{8,16},... | collective-permute-start | bytes 3538952 | tf_op jit(solution)/shard_map/ppermute | solution.py:34
  74.2 18.6 %collective-permute-start.13 = (bf16[512,1152]{1,0:T(8,128)(2,1)S(1)}, bf16[512,1152]{1,0:T(8,128)(2,1)S(1)}, u32[]{:S(2)}, u32[]{:S(2)}) collective-permute-start(bf16[512,1152]{1,0:T(8,128)(2,1)S(1)} %broadcast_select_fusion.1.refs_6_), channel_id=1, source_target_pairs={{0,6},{2,4},{5,3},{7,1},{8,14},{10,12},{13,11},{15,9},{16,22},{18,... | collective-permute-start | bytes 3538952 | tf_op jit(solution)/shard_map/ppermute | solution.py:34
  76.9 16.9 %collective-permute-start.12 = (bf16[512,1152]{1,0:T(8,128)(2,1)S(1)}, bf16[512,1152]{1,0:T(8,128)(2,1)}, u32[]{:S(2)}, u32[]{:S(2)}) collective-permute-start(bf16[512,1152]{1,0:T(8,128)(2,1)S(1)} %broadcast_select_fusion.refs_5_), channel_id=1, source_target_pairs={{0,8},{1,121},{2,10},{3,123},{4,12},{5,125},{6,14},{7,127},{8,16},... | collective-permute-start | bytes 3538952 | tf_op jit(solution)/shard_map/ppermute | solution.py:34
  79.8 17.3 %collective-permute-start.15 = (bf16[512,1152]{1,0:T(8,128)(2,1)S(1)}, bf16[512,1152]{1,0:T(8,128)(2,1)S(1)}, u32[]{:S(2)}, u32[]{:S(2)}) collective-permute-start(bf16[512,1152]{1,0:T(8,128)(2,1)S(1)} %collective-permute-done.14.refs_4_), channel_id=1, source_target_pairs={{1,3},{3,1},{4,6},{6,4},{9,11},{11,9},{12,14},{14,12},{17,19},{19,... | collective-permute-start | bytes 3538952 | tf_op jit(solution)/shard_map/ppermute | solution.py:34
  98.2 14.7 %collective-permute-start.16 = (bf16[512,1152]{1,0:T(8,128)(2,1)}, bf16[512,1152]{1,0:T(8,128)(2,1)}, u32[]{:S(2)}, u32[]{:S(2)}) collective-permute-start(bf16[512,1152]{1,0:T(8,128)(2,1)} %collective-permute-done.12.refs_4_), channel_id=1, source_target_pairs={{1,7},{3,5},{4,2},{6,0},{9,15},{11,13},{12,10},{14,8},{17,23},{19,... | collective-permute-start | bytes 3538952 | tf_op jit(solution)/shard_map/ppermute | solution.py:34
  100.5 12.4 %collective-permute-start.17 = (bf16[512,1152]{1,0:T(8,128)(2,1)}, bf16[512,1152]{1,0:T(8,128)(2,1)}, u32[]{:S(2)}, u32[]{:S(2)}) collective-permute-start(bf16[512,1152]{1,0:T(8,128)(2,1)} %collective-permute-done.12.refs_4_), channel_id=1, source_target_pairs={{0,2},{2,0},{5,7},{7,5},{8,10},{10,8},{13,15},{15,13},{16,18},{18,... | collective-permute-start | bytes 3538952 | tf_op jit(solution)/shard_map/ppermute | solution.py:34
  105.3 21.8 %collective-permute-start.21 = (bf16[256,1152]{1,0:T(8,128)(2,1)S(1)}, bf16[256,1152]{1,0:T(8,128)(2,1)S(1)}, u32[]{:S(2)}, u32[]{:S(2)}) collective-permute-start(bf16[256,1152]{1,0:T(8,128)(2,1)S(1)} %slice.27), channel_id=1, source_target_pairs={{0,32},{1,33},{2,34},{3,35},{4,36},{5,37},{6,38},{7,39},{8,40},{9,... | collective-permute-start | bytes 1769480 | tf_op jit(solution)/shard_map/ppermute | solution.py:34
  105.4 21.7 %collective-permute-start.22 = (bf16[256,1152]{1,0:T(8,128)(2,1)S(1)}, bf16[256,1152]{1,0:T(8,128)(2,1)S(1)}, u32[]{:S(2)}, u32[]{:S(2)}) collective-permute-start(bf16[256,1152]{1,0:T(8,128)(2,1)S(1)} %slice.28), channel_id=1, source_target_pairs={{0,96},{1,97},{2,98},{3,99},{4,100},{5,101},{6,102},{7,103},{8,104... | collective-permute-start | bytes 1769480 | tf_op jit(solution)/shard_map/ppermute | solution.py:34
  119.9 7.3 %collective-permute-start.20 = (bf16[288,512]{1,0:T(8,128)(2,1)S(1)}, bf16[288,512]{1,0:T(8,128)(2,1)S(1)}, u32[]{:S(2)}, u32[]{:S(2)}) collective-permute-start(bf16[288,512]{1,0:T(8,128)(2,1)S(1)} %get-tuple-element.56), channel_id=1, source_target_pairs={{0,64},{1,65},{2,66},{3,67},{4,68},{5,69},{6,70},{7,71},{8,72},{9,... | collective-permute-start | bytes 884744 | tf_op jit(solution)/shard_map/ppermute | solution.py:34
  120.0 10.0 %collective-permute-start.18 = (bf16[288,512]{1,0:T(8,128)(2,1)S(1)}, bf16[288,512]{1,0:T(8,128)(2,1)S(1)}, u32[]{:S(2)}, u32[]{:S(2)}) collective-permute-start(bf16[288,512]{1,0:T(8,128)(2,1)S(1)} %get-tuple-element.54), channel_id=1, source_target_pairs={{0,32},{1,33},{2,34},{3,35},{4,36},{5,37},{6,38},{7,39},{8,40},{9,... | collective-permute-start | bytes 884744 | tf_op jit(solution)/shard_map/ppermute | solution.py:34
  120.6 9.4 %collective-permute-start.19 = (bf16[288,512]{1,0:T(8,128)(2,1)S(1)}, bf16[288,512]{1,0:T(8,128)(2,1)S(1)}, u32[]{:S(2)}, u32[]{:S(2)}) collective-permute-start(bf16[288,512]{1,0:T(8,128)(2,1)S(1)} %get-tuple-element.55), channel_id=1, source_target_pairs={{0,96},{1,97},{2,98},{3,99},{4,100},{5,101},{6,102},{7,103},{8,104... | collective-permute-start | bytes 884744 | tf_op jit(solution)/shard_map/ppermute | solution.py:34
  131.7 12.9 %collective-permute-start.23 = (bf16[72,1152]{1,0:T(8,128)(2,1)S(1)}, bf16[72,1152]{1,0:T(8,128)(2,1)S(1)}, u32[]{:S(2)}, u32[]{:S(2)}) collective-permute-start(bf16[72,1152]{1,0:T(8,128)(2,1)S(1)} %get-tuple-element.62), channel_id=1, source_target_pairs={{0,4},{1,5},{2,6},{3,7},{4,0},{5,1},{6,2},{7,3},{8,12},{9,13},{10,... | collective-permute-start | bytes 497672 | tf_op jit(solution)/shard_map/ppermute | solution.py:34
  141.6 8.2 %collective-permute-start.24 = (bf16[72,1152]{1,0:T(8,128)(2,1)S(1)}, bf16[72,1152]{1,0:T(8,128)(2,1)S(1)}, u32[]{:S(2)}, u32[]{:S(2)}) collective-permute-start(bf16[72,1152]{1,0:T(8,128)(2,1)S(1)} %get-tuple-element.63), channel_id=1, source_target_pairs={{0,2},{1,3},{2,0},{3,1},{4,6},{5,7},{6,4},{7,5},{8,10},{9,11},{10,... | collective-permute-start | bytes 497672 | tf_op jit(solution)/shard_map/ppermute | solution.py:34
  142.6 7.7 %collective-permute-start.25 = (bf16[72,1152]{1,0:T(8,128)(2,1)S(1)}, bf16[72,1152]{1,0:T(8,128)(2,1)S(1)}, u32[]{:S(2)}, u32[]{:S(2)}) collective-permute-start(bf16[72,1152]{1,0:T(8,128)(2,1)S(1)} %get-tuple-element.64), channel_id=1, source_target_pairs={{0,6},{1,7},{2,4},{3,5},{4,2},{5,3},{6,0},{7,1},{8,14},{9,15},{10,... | collective-permute-start | bytes 497672 | tf_op jit(solution)/shard_map/ppermute | solution.py:34
  142.6 7.8 %collective-permute-start.26 = (bf16[256,1152]{1,0:T(8,128)(2,1)S(1)}, bf16[256,1152]{1,0:T(8,128)(2,1)S(1)}, u32[]{:S(2)}, u32[]{:S(2)}) collective-permute-start(bf16[256,1152]{1,0:T(8,128)(2,1)S(1)} %slice.23), channel_id=1, source_target_pairs={{0,1},{1,0},{2,3},{3,2},{4,5},{5,4},{6,7},{7,6},{8,9},{9,8},{10,11... | collective-permute-start | bytes 1769480 | tf_op jit(solution)/shard_map/ppermute | solution.py:34
  150.5 10.8 %collective-permute-start.28 = (bf16[72,1152]{1,0:T(8,128)(2,1)S(1)}, bf16[72,1152]{1,0:T(8,128)(2,1)S(1)}, u32[]{:S(2)}, u32[]{:S(2)}) collective-permute-start(bf16[72,1152]{1,0:T(8,128)(2,1)S(1)} %fusion), channel_id=1, source_target_pairs={{0,8},{1,9},{2,10},{3,11},{4,12},{5,13},{6,14},{7,15},{8,16},{9,17... | collective-permute-start | bytes 497672 | tf_op jit(solution)/shard_map/ppermute | solution.py:34
  152.7 8.6 %collective-permute-start.29 = (bf16[72,1152]{1,0:T(8,128)(2,1)S(1)}, bf16[72,1152]{1,0:T(8,128)(2,1)S(1)}, u32[]{:S(2)}, u32[]{:S(2)}) collective-permute-start(bf16[72,1152]{1,0:T(8,128)(2,1)S(1)} %fusion), channel_id=1, source_target_pairs={{0,24},{1,25},{2,26},{3,27},{4,28},{5,29},{6,30},{7,31},{8,0},{9,1... | collective-permute-start | bytes 497672 | tf_op jit(solution)/shard_map/ppermute | solution.py:34
  162.3 8.2 %collective-permute-start.31 = (bf16[72,1152]{1,0:T(8,128)(2,1)S(1)}, bf16[72,1152]{1,0:T(8,128)(2,1)S(1)}, u32[]{:S(2)}, u32[]{:S(2)}) collective-permute-start(bf16[72,1152]{1,0:T(8,128)(2,1)S(1)} %add_convert_fusion), channel_id=1, source_target_pairs={{1,4},{3,6},{4,1},{6,3},{9,12},{11,14},{12,9},{14,11},{17,20},{19,... | collective-permute-start | bytes 497672 | tf_op jit(solution)/shard_map/ppermute | solution.py:34
  170.5 10.0 %collective-permute-start.32 = (bf16[2,72,1152]{2,1,0:T(8,128)(2,1)S(1)}, bf16[2,72,1152]{2,1,0:T(8,128)(2,1)S(1)}, u32[]{:S(2)}, u32[]{:S(2)}) collective-permute-start(bf16[2,72,1152]{2,1,0:T(8,128)(2,1)S(1)} %pad_maximum_fusion.1), channel_id=1, source_target_pairs={{0,96},{1,97},{2,98},{3,99},{4,100},{5,101},{6,102},{7,103},{8,104... | collective-permute-start | bytes 995336 | tf_op jit(solution)/shard_map/ppermute | solution.py:34
  173.1 11.1 %collective-permute-start.33 = (bf16[2,72,1152]{2,1,0:T(8,128)(2,1)S(1)}, bf16[2,72,1152]{2,1,0:T(8,128)(2,1)S(1)}, u32[]{:S(2)}, u32[]{:S(2)}) collective-permute-start(bf16[2,72,1152]{2,1,0:T(8,128)(2,1)S(1)} %pad_maximum_fusion.1), channel_id=1, source_target_pairs={{0,64},{1,65},{2,66},{3,67},{4,68},{5,69},{6,70},{7,71},{8,72},{9,... | collective-permute-start | bytes 995336 | tf_op jit(solution)/shard_map/ppermute | solution.py:34
  173.1 15.1 %collective-permute-start.34 = (bf16[2,72,1152]{2,1,0:T(8,128)(2,1)S(1)}, bf16[2,72,1152]{2,1,0:T(8,128)(2,1)S(1)}, u32[]{:S(2)}, u32[]{:S(2)}) collective-permute-start(bf16[2,72,1152]{2,1,0:T(8,128)(2,1)S(1)} %pad_maximum_fusion.1), channel_id=1, source_target_pairs={{0,32},{1,33},{2,34},{3,35},{4,36},{5,37},{6,38},{7,39},{8,40},{9,... | collective-permute-start | bytes 995336 | tf_op jit(solution)/shard_map/ppermute | solution.py:34
  (27 other events, 203.9 us)

commit v4 on v3

--- a/solution.py
+++ b/solution.py
@@ -8,7 +8,7 @@
 from jax.sharding import Mesh, PartitionSpec as P
 
 WIN = 4
-COST = 10**6
+COST = 3 * 10**8
 VMEM = 40 * 2**20
 VMEM_LARGE = 40 * 2**20
 VMEM_SMALL = 24 * 2**20
@@ -114,8 +114,8 @@
     return pl.pallas_call(
         embed_kernel,
         in_specs=[pl.BlockSpec(memory_space=pltpu.SMEM)]
-        + [pl.BlockSpec(memory_space=pltpu.HBM)] * 6,
-        out_specs=[pl.BlockSpec(memory_space=pltpu.HBM)] * 3,
+        + [pl.BlockSpec(memory_space=pl.ANY)] * 6,
+        out_specs=[pl.BlockSpec(memory_space=pl.ANY)] * 3,
         out_shape=[jax.ShapeDtypeStruct(*shape) for shape in shapes],
         scratch_shapes=[
             pltpu.VMEM((2 * rows, width), BF),
@@ -325,12 +325,12 @@
     b1n_odd = moved(after(b1f_b0f, b1f_even), collect("cross", parity=0))
     b3n_odd = moved(b3f_b2f, collect("half", parity=1))
     grad = score([b3f_b2f, b0f_b1f], total=grad)
-    b2f_b3f, b1n_odd, b3n_odd, grad = lax.optimization_barrier((b2f_b3f, b1n_odd, b3n_odd, grad))
+    b2f_b3f, grad = lax.optimization_barrier((b2f_b3f, grad))
     b1n_even = moved(b2f_b3f, collect("cross", parity=1))
     b3n_even = moved(b2f_b3f, collect("half", parity=0))
     grad = score([b2f_b3f], total=grad)
-    own_z2 = moved(after(pool_z1[:rows], b2f_b3f), hop(dz=1))
-    mate_z2 = moved(after(pool_z3[rows:], b2f_b3f), hop(dz=-1))
+    own_z2 = moved(after(pool_z1[:rows], b2f_b3f, b1n_odd, b3n_odd), hop(dz=1))
+    mate_z2 = moved(after(pool_z3[rows:], b2f_b3f, b1n_odd, b3n_odd), hop(dz=-1))
     order = []
     for ahead in range(4):
         for far_half, far_odd in ((0, 0), (0, 1), (1, 0), (1, 1)):

time: 191 us -> 190 us (level)
  Pallas kernels: 28.7 us -> 31 us
  waiting for transfers between devices: 69 us -> 66.8 us
  local copies, waits for them, and re-layouts: 11.5 us -> 9.4 us
    pallas_call x4, Pallas kernels: 21.3 us -> 23.5 us  [sums(): pl.pallas_call(functools.partial(sums_kernel, (tuple(names), tuple(plan),...]
    ppermute x35, waiting for transfers between devices: 69 us -> 66.8 us  [moved(): return lax.ppermute(block, AXES, pairs)]
    unnamed x55 -> x47, local copies, waits for them, and re-layouts: 7.76 us -> 5.7 us
  transfers between devices with their start and end apart: 35 -> 35, of which waited for: 19 -> 18; matrix products, arithmetic and copies ran while one was open for 5% -> 6% of each run, Pallas kernels for 14% -> 15%
where the time goes in v4:
time: 190 us
  starting transfers between devices  69.1 us (36%)
  waiting for transfers between devices  66.8 us (35%)
  Pallas kernels  31 us (16%)
  local copies, waits for them, and re-layouts  9.4 us (5%)
  other arithmetic  9.16 us (5%)
  between operations  2.4 us (1%)
    ppermute x35, starting transfers between devices, moved(): return lax.ppermute(block, AXES, pairs)  69.1 us
    ppermute x35, waiting for transfers between devices, moved(): return lax.ppermute(block, AXES, pairs)  66.8 us
    pallas_call x4, Pallas kernels, sums(): pl.pallas_call(functools.partial(sums_kernel, (tuple(names), tuple(plan),...  23.5 us
    pallas_call x1, Pallas kernels, embed(): pl.pallas_call(embed_kernel, in_specs=[pl.BlockSpec(memory_space=pltpu.SM...  5.79 us
    unnamed x47, local copies, waits for them, and re-layouts  5.7 us
  transfers between devices with their start and end apart: 35, of which 18 were waited for; matrix products, arithmetic and copies ran while one was open for 6% of the time, Pallas kernels for 15%

profile of v4, /device:TPU:1, one launch (start us, length us, event | category | flops | bytes accessed | tf_op | source)
XLA Modules:
  0.0 189.6 jit_solution(8689474530661488942)
XLA Ops:
  10.8 2.2 %collective-permute-start.6 = (bf16[512,1152]{1,0:T(8,128)(2,1)S(1)}, bf16[512,1152]{1,0:T(8,128)(2,1)S(1)}, u32[]{:S(2)}, u32[]{:S(2)}) collective-permute-start(bf16[512,1152]{1,0:T(8,128)(2,1)S(1)} %pad_maximum_fusion.refs_4_), channel_id=1, source_target_pairs={{0,96},{1,97},{2,98},{3,99},{4,100},{5,101},{6,102},{7,103},{8,104... | collective-permute-start | bytes 3538952 | tf_op jit(solution)/shard_map/ppermute | solution.py:34
  13.0 9.6 %collective-permute-done.2.refs_2_ = bf16[288,1152]{1,0:T(8,128)(2,1)S(1)} collective-permute-done((bf16[288,1152]{1,0:T(8,128)(2,1)S(1)}, bf16[288,1152]{1,0:T(8,128)(2,1)S(1)}, u32[]{:S(2)}, u32[]{:S(2)}) %collective-permute-start.2) | collective-permute-done | bytes 663584 | tf_op jit(solution)/shard_map/ppermute | solution.py:34
  24.8 5.8 %embed.1 = (f32[512,1152]{1,0:T(8,128)S(1)}, bf16[512,1152]{1,0:T(8,128)(2,1)S(1)}, f32[512,128]{1,0:T(8,128)S(1)}) custom-call(s32[4]{0:T(128)S(1)} %pad_add_fusion.place, bf16[256,1152]{1,0:T(8,128)(2,1)S(1)} %get-tuple-element.73.own, bf16[256,1152]{1,0:T(8,128)(2,1)} %collective-permute-done.mate, bf16[288,1152]{1,0:T(8,128)(2,1)S(1)} %get-tuple-element.35.refs_0_, ...), custom_call_target="tpu_custom_call" | custom-call | flops 300000000 | bytes 1048576 | tf_op jit(solution)/shard_map/embed/pallas_call | solution.py:114
  33.4 2.9 %collective-permute-start.8 = (bf16[512,1152]{1,0:T(8,128)(2,1)S(1)}, bf16[512,1152]{1,0:T(8,128)(2,1)S(1)}, u32[]{:S(2)}, u32[]{:S(2)}) collective-permute-start(bf16[512,1152]{1,0:T(8,128)(2,1)S(1)} %get-tuple-element.40.refs_3_), channel_id=1, source_target_pairs={{1,2},{3,0},{4,7},{6,5},{9,10},{11,8},{12,15},{14,13},{17,18},{19,... | collective-permute-start | bytes 3538952 | tf_op jit(solution)/shard_map/ppermute | solution.py:34
  36.4 2.7 %collective-permute-done.5.refs_5_ = bf16[512,1152]{1,0:T(8,128)(2,1)S(1)} collective-permute-done((bf16[512,1152]{1,0:T(8,128)(2,1)S(1)}, bf16[512,1152]{1,0:T(8,128)(2,1)S(1)}, u32[]{:S(2)}, u32[]{:S(2)}) %collective-permute-start.5) | collective-permute-done | bytes 1179680 | tf_op jit(solution)/shard_map/ppermute | solution.py:34
  39.0 5.8 %collective-permute-start.7 = (bf16[512,1152]{1,0:T(8,128)(2,1)S(1)}, bf16[512,1152]{1,0:T(8,128)(2,1)}, u32[]{:S(2)}, u32[]{:S(2)}) collective-permute-start(bf16[512,1152]{1,0:T(8,128)(2,1)S(1)} %get-tuple-element.40.refs_3_), channel_id=1, source_target_pairs={{1,6},{3,4},{4,3},{6,1},{9,14},{11,12},{12,11},{14,9},{17,22},{19,... | collective-permute-start | bytes 3538952 | tf_op jit(solution)/shard_map/ppermute | solution.py:34
  44.8 4.5 %collective-permute-done.8 = bf16[512,1152]{1,0:T(8,128)(2,1)S(1)} collective-permute-done((bf16[512,1152]{1,0:T(8,128)(2,1)S(1)}, bf16[512,1152]{1,0:T(8,128)(2,1)S(1)}, u32[]{:S(2)}, u32[]{:S(2)}) %collective-permute-start.8) | collective-permute-done | bytes 1179680 | tf_op jit(solution)/shard_map/ppermute | solution.py:34
  52.4 6.0 %collective-permute-start.11 = (bf16[512,1152]{1,0:T(8,128)(2,1)}, bf16[512,1152]{1,0:T(8,128)(2,1)}, u32[]{:S(2)}, u32[]{:S(2)}) collective-permute-start(bf16[512,1152]{1,0:T(8,128)(2,1)} %collective-permute-done.10.refs_5_), channel_id=1, source_target_pairs={{1,7},{3,5},{4,2},{6,0},{9,15},{11,13},{12,10},{14,8},{17,23},{19,... | collective-permute-start | bytes 3538952 | tf_op jit(solution)/shard_map/ppermute | solution.py:34
  59.7 2.4 %broadcast_select_fusion.1.refs_6_ = bf16[512,1152]{1,0:T(8,128)(2,1)} fusion(bf16[512,1152]{1,0:T(8,128)(2,1)} %collective-permute-done.7, bf16[512,1152]{1,0:T(8,128)(2,1)} %copy-done.17, pred[]{:T(512)S(6)} %eq.28), kind=kLoop, calls=%fused_computation.4 | loop fusion | flops 589824 | bytes 3538945 | tf_op jit(solution)/shard_map/jit(_where)/select_n | solution.py:319
  62.1 6.2 %collective-permute-start.14 = (bf16[512,1152]{1,0:T(8,128)(2,1)}, bf16[512,1152]{1,0:T(8,128)(2,1)}, u32[]{:S(2)}, u32[]{:S(2)}) collective-permute-start(bf16[512,1152]{1,0:T(8,128)(2,1)} %broadcast_select_fusion.1.refs_6_), channel_id=1, source_target_pairs={{0,8},{1,121},{2,10},{3,123},{4,12},{5,125},{6,14},{7,127},{8,16},... | collective-permute-start | bytes 3538952 | tf_op jit(solution)/shard_map/ppermute | solution.py:34
  68.3 7.1 %sums.3.refs_6_ = f32[512,1152]{1,0:T(8,128)S(1)} custom-call(f32[1]{0:T(128)S(6)} %copy.21.refs_0_, f32[1]{0:T(128)S(6)} %copy.22.refs_1_, s32[1]{0:T(128)} %bitcast.refs_2_, bf16[512,1152]{1,0:T(8,128)(2,1)S(1)} %get-tuple-element.40.refs_3_, bf16[512,1152]{1,0:T(8,128)(2,1)S(1)} %collective-permute-done.4.refs_4_, ...), custom_call_target="tpu_custom_call" | custom-call | flops 300000000 | bytes 1048576 | tf_op jit(solution)/shard_map/sums/pallas_call | solution.py:233
  79.8 2.0 %collective-permute-done.14.refs_4_ = bf16[512,1152]{1,0:T(8,128)(2,1)} collective-permute-done((bf16[512,1152]{1,0:T(8,128)(2,1)}, bf16[512,1152]{1,0:T(8,128)(2,1)}, u32[]{:S(2)}, u32[]{:S(2)}) %collective-permute-start.14) | collective-permute-done | bytes 1179680 | tf_op jit(solution)/shard_map/ppermute | solution.py:34
  81.8 1.9 %collective-permute-start.16 = (bf16[512,1152]{1,0:T(8,128)(2,1)}, bf16[512,1152]{1,0:T(8,128)(2,1)}, u32[]{:S(2)}, u32[]{:S(2)}) collective-permute-start(bf16[512,1152]{1,0:T(8,128)(2,1)} %collective-permute-done.14.refs_4_), channel_id=1, source_target_pairs={{1,3},{3,1},{4,6},{6,4},{9,11},{11,9},{12,14},{14,12},{17,19},{19,... | collective-permute-start | bytes 3538952 | tf_op jit(solution)/shard_map/ppermute | solution.py:34
  83.7 5.2 %sums.4.refs_5_ = f32[512,1152]{1,0:T(8,128)S(1)} custom-call(f32[1]{0:T(128)S(6)} %copy.21.refs_0_, f32[1]{0:T(128)S(6)} %copy.22.refs_1_, s32[1]{0:T(128)} %bitcast.refs_2_, bf16[512,1152]{1,0:T(8,128)(2,1)S(1)} %get-tuple-element.40.refs_3_, bf16[512,1152]{1,0:T(8,128)(2,1)} %collective-permute-done.14.refs_4_, ...), custom_call_target="tpu_custom_call" | custom-call | flops 300000000 | bytes 1048576 | tf_op jit(solution)/shard_map/sums/pallas_call | solution.py:233
  89.0 5.4 %collective-permute-done.13.refs_4_ = bf16[512,1152]{1,0:T(8,128)(2,1)} collective-permute-done((bf16[512,1152]{1,0:T(8,128)(2,1)S(1)}, bf16[512,1152]{1,0:T(8,128)(2,1)}, u32[]{:S(2)}, u32[]{:S(2)}) %collective-permute-start.13) | collective-permute-done | bytes 1179680 | tf_op jit(solution)/shard_map/ppermute | solution.py:34
  94.3 3.4 %collective-permute-start.15 = (bf16[512,1152]{1,0:T(8,128)(2,1)}, bf16[512,1152]{1,0:T(8,128)(2,1)}, u32[]{:S(2)}, u32[]{:S(2)}) collective-permute-start(bf16[512,1152]{1,0:T(8,128)(2,1)} %collective-permute-done.13.refs_4_), channel_id=1, source_target_pairs={{1,7},{3,5},{4,2},{6,0},{9,15},{11,13},{12,10},{14,8},{17,23},{19,... | collective-permute-start | bytes 3538952 | tf_op jit(solution)/shard_map/ppermute | solution.py:34
  104.2 3.6 %sums.5.refs_8_ = f32[512,1152]{1,0:T(8,128)S(1)} custom-call(f32[1]{0:T(128)S(6)} %copy.21.refs_0_, f32[1]{0:T(128)S(6)} %copy.22.refs_1_, s32[1]{0:T(128)} %bitcast.refs_2_, bf16[512,1152]{1,0:T(8,128)(2,1)S(1)} %get-tuple-element.40.refs_3_, bf16[512,1152]{1,0:T(8,128)(2,1)} %collective-permute-done.13.refs_4_, f32[512,1152]{1,0:T(8,128)S(1)} %sums.4.refs_5_), custom_call_target="tpu_custom_call" | custom-call | flops 300000000 | bytes 1048576 | tf_op jit(solution)/shard_map/sums/pallas_call | solution.py:233
  107.9 2.3 %collective-permute-done.15.refs_5_ = bf16[512,1152]{1,0:T(8,128)(2,1)} collective-permute-done((bf16[512,1152]{1,0:T(8,128)(2,1)}, bf16[512,1152]{1,0:T(8,128)(2,1)}, u32[]{:S(2)}, u32[]{:S(2)}) %collective-permute-start.15) | collective-permute-done | bytes 1179680 | tf_op jit(solution)/shard_map/ppermute | solution.py:34
  110.1 7.5 %finish.1 = (bf16[512,1152]{1,0:T(8,128)(2,1)S(1)}, bf16[288,512]{1,0:T(8,128)(2,1)S(1)}, bf16[288,512]{1,0:T(8,128)(2,1)S(1)}, bf16[288,512]{1,0:T(8,128)(2,1)S(1)}, bf16[288,512]{1,0:T(8,128)(2,1)S(1)}) custom-call(f32[1]{0:T(128)S(6)} %copy.21.refs_0_, f32[1]{0:T(128)S(6)} %copy.22.refs_1_, s32[1]{0:T(128)} %bitcast.refs_2_, ...), custom_call_target="tpu_custom_call" | custom-call | flops 300000000 | bytes 1048576 | tf_op jit(solution)/shard_map/finish/pallas_call | solution.py:233
  118.6 1.9 %collective-permute-start.19 = (bf16[288,512]{1,0:T(8,128)(2,1)S(1)}, bf16[288,512]{1,0:T(8,128)(2,1)S(1)}, u32[]{:S(2)}, u32[]{:S(2)}) collective-permute-start(bf16[288,512]{1,0:T(8,128)(2,1)S(1)} %get-tuple-element.51), channel_id=1, source_target_pairs={{0,96},{1,97},{2,98},{3,99},{4,100},{5,101},{6,102},{7,103},{8,104... | collective-permute-start | bytes 884744 | tf_op jit(solution)/shard_map/ppermute | solution.py:34
  122.4 2.5 %collective-permute-done.20.refs_3_ = bf16[288,512]{1,0:T(8,128)(2,1)S(1)} collective-permute-done((bf16[288,512]{1,0:T(8,128)(2,1)S(1)}, bf16[288,512]{1,0:T(8,128)(2,1)S(1)}, u32[]{:S(2)}, u32[]{:S(2)}) %collective-permute-start.20) | collective-permute-done | bytes 294944 | tf_op jit(solution)/shard_map/ppermute | solution.py:34
  124.9 2.9 %collective-permute-done.18.refs_1_ = bf16[288,512]{1,0:T(8,128)(2,1)S(1)} collective-permute-done((bf16[288,512]{1,0:T(8,128)(2,1)S(1)}, bf16[288,512]{1,0:T(8,128)(2,1)S(1)}, u32[]{:S(2)}, u32[]{:S(2)}) %collective-permute-start.18) | collective-permute-done | bytes 294944 | tf_op jit(solution)/shard_map/ppermute | solution.py:34
  129.6 11.3 %collective-permute-start.23 = (bf16[72,1152]{1,0:T(8,128)(2,1)S(1)}, bf16[72,1152]{1,0:T(8,128)(2,1)S(1)}, u32[]{:S(2)}, u32[]{:S(2)}) collective-permute-start(bf16[72,1152]{1,0:T(8,128)(2,1)S(1)} %get-tuple-element.58), channel_id=1, source_target_pairs={{0,4},{1,5},{2,6},{3,7},{4,0},{5,1},{6,2},{7,3},{8,12},{9,13},{10,... | collective-permute-start | bytes 497672 | tf_op jit(solution)/shard_map/ppermute | solution.py:34
  140.9 2.4 %collective-permute-start.24 = (bf16[72,1152]{1,0:T(8,128)(2,1)S(1)}, bf16[72,1152]{1,0:T(8,128)(2,1)S(1)}, u32[]{:S(2)}, u32[]{:S(2)}) collective-permute-start(bf16[72,1152]{1,0:T(8,128)(2,1)S(1)} %get-tuple-element.59), channel_id=1, source_target_pairs={{0,2},{1,3},{2,0},{3,1},{4,6},{5,7},{6,4},{7,5},{8,10},{9,11},{10,... | collective-permute-start | bytes 497672 | tf_op jit(solution)/shard_map/ppermute | solution.py:34
  145.2 5.5 %collective-permute-done.24 = bf16[72,1152]{1,0:T(8,128)(2,1)S(1)} collective-permute-done((bf16[72,1152]{1,0:T(8,128)(2,1)S(1)}, bf16[72,1152]{1,0:T(8,128)(2,1)S(1)}, u32[]{:S(2)}, u32[]{:S(2)}) %collective-permute-start.24) | collective-permute-done | bytes 165920 | tf_op jit(solution)/shard_map/ppermute | solution.py:34
  151.0 2.7 %collective-permute-start.29 = (bf16[72,1152]{1,0:T(8,128)(2,1)S(1)}, bf16[72,1152]{1,0:T(8,128)(2,1)S(1)}, u32[]{:S(2)}, u32[]{:S(2)}) collective-permute-start(bf16[72,1152]{1,0:T(8,128)(2,1)S(1)} %fusion), channel_id=1, source_target_pairs={{0,24},{1,25},{2,26},{3,27},{4,28},{5,29},{6,30},{7,31},{8,0},{9,1... | collective-permute-start | bytes 497672 | tf_op jit(solution)/shard_map/ppermute | solution.py:34
  153.6 3.0 %collective-permute-done.27 = bf16[72,1152]{1,0:T(8,128)(2,1)S(1)} collective-permute-done((bf16[72,1152]{1,0:T(8,128)(2,1)S(1)}, bf16[72,1152]{1,0:T(8,128)(2,1)S(1)}, u32[]{:S(2)}, u32[]{:S(2)}) %collective-permute-start.27) | collective-permute-done | bytes 165920 | tf_op jit(solution)/shard_map/ppermute | solution.py:34
  156.7 5.0 %collective-permute-done.28 = bf16[72,1152]{1,0:T(8,128)(2,1)S(1)} collective-permute-done((bf16[72,1152]{1,0:T(8,128)(2,1)S(1)}, bf16[72,1152]{1,0:T(8,128)(2,1)S(1)}, u32[]{:S(2)}, u32[]{:S(2)}) %collective-permute-start.28) | collective-permute-done | bytes 165920 | tf_op jit(solution)/shard_map/ppermute | solution.py:34
  162.6 3.2 %collective-permute-start.31 = (bf16[72,1152]{1,0:T(8,128)(2,1)S(1)}, bf16[72,1152]{1,0:T(8,128)(2,1)S(1)}, u32[]{:S(2)}, u32[]{:S(2)}) collective-permute-start(bf16[72,1152]{1,0:T(8,128)(2,1)S(1)} %add_convert_fusion), channel_id=1, source_target_pairs={{1,4},{3,6},{4,1},{6,3},{9,12},{11,14},{12,9},{14,11},{17,20},{19,... | collective-permute-start | bytes 497672 | tf_op jit(solution)/shard_map/ppermute | solution.py:34
  167.6 3.2 %collective-permute-done.31 = bf16[72,1152]{1,0:T(8,128)(2,1)S(1)} collective-permute-done((bf16[72,1152]{1,0:T(8,128)(2,1)S(1)}, bf16[72,1152]{1,0:T(8,128)(2,1)S(1)}, u32[]{:S(2)}, u32[]{:S(2)}) %collective-permute-start.31) | collective-permute-done | bytes 165920 | tf_op jit(solution)/shard_map/ppermute | solution.py:34
  172.5 8.4 %collective-permute-done.32 = bf16[2,72,1152]{2,1,0:T(8,128)(2,1)S(1)} collective-permute-done((bf16[2,72,1152]{2,1,0:T(8,128)(2,1)S(1)}, bf16[2,72,1152]{2,1,0:T(8,128)(2,1)S(1)}, u32[]{:S(2)}, u32[]{:S(2)}) %collective-permute-start.32) | collective-permute-done | bytes 331808 | tf_op jit(solution)/shard_map/ppermute | solution.py:34
  182.6 4.9 %collective-permute-done.34 = bf16[2,72,1152]{2,1,0:T(8,128)(2,1)S(1)} collective-permute-done((bf16[2,72,1152]{2,1,0:T(8,128)(2,1)S(1)}, bf16[2,72,1152]{2,1,0:T(8,128)(2,1)S(1)}, u32[]{:S(2)}, u32[]{:S(2)}) %collective-permute-start.34) | collective-permute-done | bytes 331808 | tf_op jit(solution)/shard_map/ppermute | solution.py:34
  (115 shorter events, 43.8 us)
Async XLA Ops:
  4.6 18.0 %collective-permute-start.2 = (bf16[288,1152]{1,0:T(8,128)(2,1)S(1)}, bf16[288,1152]{1,0:T(8,128)(2,1)S(1)}, u32[]{:S(2)}, u32[]{:S(2)}) collective-permute-start(bf16[288,1152]{1,0:T(8,128)(2,1)S(1)} %get-tuple-element.35.refs_0_), channel_id=1, source_target_pairs={{0,2},{1,3},{2,4},{3,5},{4,6},{5,7},{6,0},{7,1},{8,10},{9,11},{10,... | collective-permute-start | bytes 1990664 | tf_op jit(solution)/shard_map/ppermute | solution.py:34
  6.0 17.4 %collective-permute-start.3 = (bf16[288,1152]{1,0:T(8,128)(2,1)}, bf16[288,1152]{1,0:T(8,128)(2,1)S(1)}, u32[]{:S(2)}, u32[]{:S(2)}) collective-permute-start(bf16[288,1152]{1,0:T(8,128)(2,1)} %get-tuple-element.37), channel_id=1, source_target_pairs={{0,7},{1,6},{2,1},{3,0},{4,3},{5,2},{6,5},{7,4},{8,15},{9,14},{10,... | collective-permute-start | bytes 1990664 | tf_op jit(solution)/shard_map/ppermute | solution.py:34
  7.5 15.9 %collective-permute-start.1 = (bf16[288,1152]{1,0:T(8,128)(2,1)}, bf16[288,1152]{1,0:T(8,128)(2,1)}, u32[]{:S(2)}, u32[]{:S(2)}) collective-permute-start(bf16[288,1152]{1,0:T(8,128)(2,1)} %get-tuple-element.37), channel_id=1, source_target_pairs={{0,1},{1,0},{2,3},{3,2},{4,5},{5,4},{6,7},{7,6},{8,9},{9,8},{10,11... | collective-permute-start | bytes 1990664 | tf_op jit(solution)/shard_map/ppermute | solution.py:34
  9.1 30.0 %collective-permute-start.5 = (bf16[512,1152]{1,0:T(8,128)(2,1)S(1)}, bf16[512,1152]{1,0:T(8,128)(2,1)S(1)}, u32[]{:S(2)}, u32[]{:S(2)}) collective-permute-start(bf16[512,1152]{1,0:T(8,128)(2,1)S(1)} %pad_maximum_fusion.refs_4_), channel_id=1, source_target_pairs={{0,32},{1,33},{2,34},{3,35},{4,36},{5,37},{6,38},{7,39},{8,40},{9,... | collective-permute-start | bytes 3538952 | tf_op jit(solution)/shard_map/ppermute | solution.py:34
  10.8 28.3 %collective-permute-start.6 = (bf16[512,1152]{1,0:T(8,128)(2,1)S(1)}, bf16[512,1152]{1,0:T(8,128)(2,1)S(1)}, u32[]{:S(2)}, u32[]{:S(2)}) collective-permute-start(bf16[512,1152]{1,0:T(8,128)(2,1)S(1)} %pad_maximum_fusion.refs_4_), channel_id=1, source_target_pairs={{0,96},{1,97},{2,98},{3,99},{4,100},{5,101},{6,102},{7,103},{8,104... | collective-permute-start | bytes 3538952 | tf_op jit(solution)/shard_map/ppermute | solution.py:34
  32.7 6.4 %collective-permute-start.4 = (bf16[512,1152]{1,0:T(8,128)(2,1)S(1)}, bf16[512,1152]{1,0:T(8,128)(2,1)S(1)}, u32[]{:S(2)}, u32[]{:S(2)}) collective-permute-start(bf16[512,1152]{1,0:T(8,128)(2,1)S(1)} %get-tuple-element.40.refs_3_), channel_id=1, source_target_pairs={{0,1},{1,0},{2,3},{3,2},{4,5},{5,4},{6,7},{7,6},{8,9},{9,8},{10,11... | collective-permute-start | bytes 3538952 | tf_op jit(solution)/shard_map/ppermute | solution.py:34
  33.4 16.0 %collective-permute-start.8 = (bf16[512,1152]{1,0:T(8,128)(2,1)S(1)}, bf16[512,1152]{1,0:T(8,128)(2,1)S(1)}, u32[]{:S(2)}, u32[]{:S(2)}) collective-permute-start(bf16[512,1152]{1,0:T(8,128)(2,1)S(1)} %get-tuple-element.40.refs_3_), channel_id=1, source_target_pairs={{1,2},{3,0},{4,7},{6,5},{9,10},{11,8},{12,15},{14,13},{17,18},{19,... | collective-permute-start | bytes 3538952 | tf_op jit(solution)/shard_map/ppermute | solution.py:34
  36.3 16.1 %collective-permute-start.10 = (bf16[512,1152]{1,0:T(8,128)(2,1)S(1)}, bf16[512,1152]{1,0:T(8,128)(2,1)}, u32[]{:S(2)}, u32[]{:S(2)}) collective-permute-start(bf16[512,1152]{1,0:T(8,128)(2,1)S(1)} %get-tuple-element.40.refs_3_), channel_id=1, source_target_pairs={{0,121},{1,8},{2,123},{3,10},{4,125},{5,12},{6,127},{7,14},{8,1},{... | collective-permute-start | bytes 3538952 | tf_op jit(solution)/shard_map/ppermute | solution.py:34
  39.0 20.7 %collective-permute-start.7 = (bf16[512,1152]{1,0:T(8,128)(2,1)S(1)}, bf16[512,1152]{1,0:T(8,128)(2,1)}, u32[]{:S(2)}, u32[]{:S(2)}) collective-permute-start(bf16[512,1152]{1,0:T(8,128)(2,1)S(1)} %get-tuple-element.40.refs_3_), channel_id=1, source_target_pairs={{1,6},{3,4},{4,3},{6,1},{9,14},{11,12},{12,11},{14,9},{17,22},{19,... | collective-permute-start | bytes 3538952 | tf_op jit(solution)/shard_map/ppermute | solution.py:34
  49.3 26.2 %collective-permute-start.9 = (bf16[512,1152]{1,0:T(8,128)(2,1)S(1)}, bf16[512,1152]{1,0:T(8,128)(2,1)}, u32[]{:S(2)}, u32[]{:S(2)}) collective-permute-start(bf16[512,1152]{1,0:T(8,128)(2,1)S(1)} %get-tuple-element.40.refs_3_), channel_id=1, source_target_pairs={{0,3},{2,1},{5,6},{7,4},{8,11},{10,9},{13,14},{15,12},{16,19},{18,... | collective-permute-start | bytes 3538952 | tf_op jit(solution)/shard_map/ppermute | solution.py:34
  52.4 23.1 %collective-permute-start.11 = (bf16[512,1152]{1,0:T(8,128)(2,1)}, bf16[512,1152]{1,0:T(8,128)(2,1)}, u32[]{:S(2)}, u32[]{:S(2)}) collective-permute-start(bf16[512,1152]{1,0:T(8,128)(2,1)} %collective-permute-done.10.refs_5_), channel_id=1, source_target_pairs={{1,7},{3,5},{4,2},{6,0},{9,15},{11,13},{12,10},{14,8},{17,23},{19,... | collective-permute-start | bytes 3538952 | tf_op jit(solution)/shard_map/ppermute | solution.py:34
  62.1 19.7 %collective-permute-start.14 = (bf16[512,1152]{1,0:T(8,128)(2,1)}, bf16[512,1152]{1,0:T(8,128)(2,1)}, u32[]{:S(2)}, u32[]{:S(2)}) collective-permute-start(bf16[512,1152]{1,0:T(8,128)(2,1)} %broadcast_select_fusion.1.refs_6_), channel_id=1, source_target_pairs={{0,8},{1,121},{2,10},{3,123},{4,12},{5,125},{6,14},{7,127},{8,16},... | collective-permute-start | bytes 3538952 | tf_op jit(solution)/shard_map/ppermute | solution.py:34
  76.9 17.4 %collective-permute-start.13 = (bf16[512,1152]{1,0:T(8,128)(2,1)S(1)}, bf16[512,1152]{1,0:T(8,128)(2,1)}, u32[]{:S(2)}, u32[]{:S(2)}) collective-permute-start(bf16[512,1152]{1,0:T(8,128)(2,1)S(1)} %broadcast_select_fusion.refs_5_), channel_id=1, source_target_pairs={{0,8},{1,121},{2,10},{3,123},{4,12},{5,125},{6,14},{7,127},{8,16},... | collective-permute-start | bytes 3538952 | tf_op jit(solution)/shard_map/ppermute | solution.py:34
  78.5 24.0 %collective-permute-start.12 = (bf16[512,1152]{1,0:T(8,128)(2,1)}, bf16[512,1152]{1,0:T(8,128)(2,1)}, u32[]{:S(2)}, u32[]{:S(2)}) collective-permute-start(bf16[512,1152]{1,0:T(8,128)(2,1)} %broadcast_select_fusion.1.refs_6_), channel_id=1, source_target_pairs={{0,6},{2,4},{5,3},{7,1},{8,14},{10,12},{13,11},{15,9},{16,22},{18,... | collective-permute-start | bytes 3538952 | tf_op jit(solution)/shard_map/ppermute | solution.py:34
  81.8 20.7 %collective-permute-start.16 = (bf16[512,1152]{1,0:T(8,128)(2,1)}, bf16[512,1152]{1,0:T(8,128)(2,1)}, u32[]{:S(2)}, u32[]{:S(2)}) collective-permute-start(bf16[512,1152]{1,0:T(8,128)(2,1)} %collective-permute-done.14.refs_4_), channel_id=1, source_target_pairs={{1,3},{3,1},{4,6},{6,4},{9,11},{11,9},{12,14},{14,12},{17,19},{19,... | collective-permute-start | bytes 3538952 | tf_op jit(solution)/shard_map/ppermute | solution.py:34
  94.3 15.8 %collective-permute-start.15 = (bf16[512,1152]{1,0:T(8,128)(2,1)}, bf16[512,1152]{1,0:T(8,128)(2,1)}, u32[]{:S(2)}, u32[]{:S(2)}) collective-permute-start(bf16[512,1152]{1,0:T(8,128)(2,1)} %collective-permute-done.13.refs_4_), channel_id=1, source_target_pairs={{1,7},{3,5},{4,2},{6,0},{9,15},{11,13},{12,10},{14,8},{17,23},{19,... | collective-permute-start | bytes 3538952 | tf_op jit(solution)/shard_map/ppermute | solution.py:34
  97.8 12.4 %collective-permute-start.17 = (bf16[512,1152]{1,0:T(8,128)(2,1)}, bf16[512,1152]{1,0:T(8,128)(2,1)}, u32[]{:S(2)}, u32[]{:S(2)}) collective-permute-start(bf16[512,1152]{1,0:T(8,128)(2,1)} %collective-permute-done.13.refs_4_), channel_id=1, source_target_pairs={{0,2},{2,0},{5,7},{7,5},{8,10},{10,8},{13,15},{15,13},{16,18},{18,... | collective-permute-start | bytes 3538952 | tf_op jit(solution)/shard_map/ppermute | solution.py:34
  102.6 25.3 %collective-permute-start.22 = (bf16[256,1152]{1,0:T(8,128)(2,1)S(1)}, bf16[256,1152]{1,0:T(8,128)(2,1)S(1)}, u32[]{:S(2)}, u32[]{:S(2)}) collective-permute-start(bf16[256,1152]{1,0:T(8,128)(2,1)S(1)} %slice.28), channel_id=1, source_target_pairs={{0,96},{1,97},{2,98},{3,99},{4,100},{5,101},{6,102},{7,103},{8,104... | collective-permute-start | bytes 1769480 | tf_op jit(solution)/shard_map/ppermute | solution.py:34
  103.0 24.9 %collective-permute-start.21 = (bf16[256,1152]{1,0:T(8,128)(2,1)S(1)}, bf16[256,1152]{1,0:T(8,128)(2,1)S(1)}, u32[]{:S(2)}, u32[]{:S(2)}) collective-permute-start(bf16[256,1152]{1,0:T(8,128)(2,1)S(1)} %slice.27), channel_id=1, source_target_pairs={{0,32},{1,33},{2,34},{3,35},{4,36},{5,37},{6,38},{7,39},{8,40},{9,... | collective-permute-start | bytes 1769480 | tf_op jit(solution)/shard_map/ppermute | solution.py:34
  117.7 7.3 %collective-permute-start.20 = (bf16[288,512]{1,0:T(8,128)(2,1)S(1)}, bf16[288,512]{1,0:T(8,128)(2,1)S(1)}, u32[]{:S(2)}, u32[]{:S(2)}) collective-permute-start(bf16[288,512]{1,0:T(8,128)(2,1)S(1)} %get-tuple-element.52), channel_id=1, source_target_pairs={{0,64},{1,65},{2,66},{3,67},{4,68},{5,69},{6,70},{7,71},{8,72},{9,... | collective-permute-start | bytes 884744 | tf_op jit(solution)/shard_map/ppermute | solution.py:34
  117.9 9.9 %collective-permute-start.18 = (bf16[288,512]{1,0:T(8,128)(2,1)S(1)}, bf16[288,512]{1,0:T(8,128)(2,1)S(1)}, u32[]{:S(2)}, u32[]{:S(2)}) collective-permute-start(bf16[288,512]{1,0:T(8,128)(2,1)S(1)} %get-tuple-element.50), channel_id=1, source_target_pairs={{0,32},{1,33},{2,34},{3,35},{4,36},{5,37},{6,38},{7,39},{8,40},{9,... | collective-permute-start | bytes 884744 | tf_op jit(solution)/shard_map/ppermute | solution.py:34
  118.6 9.2 %collective-permute-start.19 = (bf16[288,512]{1,0:T(8,128)(2,1)S(1)}, bf16[288,512]{1,0:T(8,128)(2,1)S(1)}, u32[]{:S(2)}, u32[]{:S(2)}) collective-permute-start(bf16[288,512]{1,0:T(8,128)(2,1)S(1)} %get-tuple-element.51), channel_id=1, source_target_pairs={{0,96},{1,97},{2,98},{3,99},{4,100},{5,101},{6,102},{7,103},{8,104... | collective-permute-start | bytes 884744 | tf_op jit(solution)/shard_map/ppermute | solution.py:34
  129.6 15.6 %collective-permute-start.23 = (bf16[72,1152]{1,0:T(8,128)(2,1)S(1)}, bf16[72,1152]{1,0:T(8,128)(2,1)S(1)}, u32[]{:S(2)}, u32[]{:S(2)}) collective-permute-start(bf16[72,1152]{1,0:T(8,128)(2,1)S(1)} %get-tuple-element.58), channel_id=1, source_target_pairs={{0,4},{1,5},{2,6},{3,7},{4,0},{5,1},{6,2},{7,3},{8,12},{9,13},{10,... | collective-permute-start | bytes 497672 | tf_op jit(solution)/shard_map/ppermute | solution.py:34
  140.9 9.8 %collective-permute-start.24 = (bf16[72,1152]{1,0:T(8,128)(2,1)S(1)}, bf16[72,1152]{1,0:T(8,128)(2,1)S(1)}, u32[]{:S(2)}, u32[]{:S(2)}) collective-permute-start(bf16[72,1152]{1,0:T(8,128)(2,1)S(1)} %get-tuple-element.59), channel_id=1, source_target_pairs={{0,2},{1,3},{2,0},{3,1},{4,6},{5,7},{6,4},{7,5},{8,10},{9,11},{10,... | collective-permute-start | bytes 497672 | tf_op jit(solution)/shard_map/ppermute | solution.py:34
  143.2 7.5 %collective-permute-start.25 = (bf16[72,1152]{1,0:T(8,128)(2,1)S(1)}, bf16[72,1152]{1,0:T(8,128)(2,1)S(1)}, u32[]{:S(2)}, u32[]{:S(2)}) collective-permute-start(bf16[72,1152]{1,0:T(8,128)(2,1)S(1)} %get-tuple-element.60), channel_id=1, source_target_pairs={{0,6},{1,7},{2,4},{3,5},{4,2},{5,3},{6,0},{7,1},{8,14},{9,15},{10,... | collective-permute-start | bytes 497672 | tf_op jit(solution)/shard_map/ppermute | solution.py:34
  143.3 7.5 %collective-permute-start.26 = (bf16[256,1152]{1,0:T(8,128)(2,1)S(1)}, bf16[256,1152]{1,0:T(8,128)(2,1)S(1)}, u32[]{:S(2)}, u32[]{:S(2)}) collective-permute-start(bf16[256,1152]{1,0:T(8,128)(2,1)S(1)} %slice.23), channel_id=1, source_target_pairs={{0,1},{1,0},{2,3},{3,2},{4,5},{5,4},{6,7},{7,6},{8,9},{9,8},{10,11... | collective-permute-start | bytes 1769480 | tf_op jit(solution)/shard_map/ppermute | solution.py:34
  150.9 10.8 %collective-permute-start.28 = (bf16[72,1152]{1,0:T(8,128)(2,1)S(1)}, bf16[72,1152]{1,0:T(8,128)(2,1)S(1)}, u32[]{:S(2)}, u32[]{:S(2)}) collective-permute-start(bf16[72,1152]{1,0:T(8,128)(2,1)S(1)} %fusion), channel_id=1, source_target_pairs={{0,8},{1,9},{2,10},{3,11},{4,12},{5,13},{6,14},{7,15},{8,16},{9,17... | collective-permute-start | bytes 497672 | tf_op jit(solution)/shard_map/ppermute | solution.py:34
  151.0 10.7 %collective-permute-start.29 = (bf16[72,1152]{1,0:T(8,128)(2,1)S(1)}, bf16[72,1152]{1,0:T(8,128)(2,1)S(1)}, u32[]{:S(2)}, u32[]{:S(2)}) collective-permute-start(bf16[72,1152]{1,0:T(8,128)(2,1)S(1)} %fusion), channel_id=1, source_target_pairs={{0,24},{1,25},{2,26},{3,27},{4,28},{5,29},{6,30},{7,31},{8,0},{9,1... | collective-permute-start | bytes 497672 | tf_op jit(solution)/shard_map/ppermute | solution.py:34
  162.6 8.2 %collective-permute-start.31 = (bf16[72,1152]{1,0:T(8,128)(2,1)S(1)}, bf16[72,1152]{1,0:T(8,128)(2,1)S(1)}, u32[]{:S(2)}, u32[]{:S(2)}) collective-permute-start(bf16[72,1152]{1,0:T(8,128)(2,1)S(1)} %add_convert_fusion), channel_id=1, source_target_pairs={{1,4},{3,6},{4,1},{6,3},{9,12},{11,14},{12,9},{14,11},{17,20},{19,... | collective-permute-start | bytes 497672 | tf_op jit(solution)/shard_map/ppermute | solution.py:34
  170.9 10.0 %collective-permute-start.32 = (bf16[2,72,1152]{2,1,0:T(8,128)(2,1)S(1)}, bf16[2,72,1152]{2,1,0:T(8,128)(2,1)S(1)}, u32[]{:S(2)}, u32[]{:S(2)}) collective-permute-start(bf16[2,72,1152]{2,1,0:T(8,128)(2,1)S(1)} %pad_maximum_fusion.1), channel_id=1, source_target_pairs={{0,96},{1,97},{2,98},{3,99},{4,100},{5,101},{6,102},{7,103},{8,104... | collective-permute-start | bytes 995336 | tf_op jit(solution)/shard_map/ppermute | solution.py:34
  171.5 11.1 %collective-permute-start.33 = (bf16[2,72,1152]{2,1,0:T(8,128)(2,1)S(1)}, bf16[2,72,1152]{2,1,0:T(8,128)(2,1)S(1)}, u32[]{:S(2)}, u32[]{:S(2)}) collective-permute-start(bf16[2,72,1152]{2,1,0:T(8,128)(2,1)S(1)} %pad_maximum_fusion.1), channel_id=1, source_target_pairs={{0,64},{1,65},{2,66},{3,67},{4,68},{5,69},{6,70},{7,71},{8,72},{9,... | collective-permute-start | bytes 995336 | tf_op jit(solution)/shard_map/ppermute | solution.py:34
  171.5 16.0 %collective-permute-start.34 = (bf16[2,72,1152]{2,1,0:T(8,128)(2,1)S(1)}, bf16[2,72,1152]{2,1,0:T(8,128)(2,1)S(1)}, u32[]{:S(2)}, u32[]{:S(2)}) collective-permute-start(bf16[2,72,1152]{2,1,0:T(8,128)(2,1)S(1)} %pad_maximum_fusion.1), channel_id=1, source_target_pairs={{0,32},{1,33},{2,34},{3,35},{4,36},{5,37},{6,38},{7,39},{8,40},{9,... | collective-permute-start | bytes 995336 | tf_op jit(solution)/shard_map/ppermute | solution.py:34
  (23 other events, 194.7 us)

commit v5 on v4

--- a/solution.py
+++ b/solution.py
@@ -382,8 +382,9 @@
     other = jnp.where(here, one, two)
     pair = jnp.stack([jnp.where(first, same, other), jnp.where(first, other, same)])
     pair, grad_image, grad_text = lax.optimization_barrier((pair, grad_image, grad_text))
-    across = moved(pair, hop(dz=2))
-    ring = [pair, moved(pair, hop(dz=-1)), across, moved(pair, hop(dz=1))]
+    below, above = moved(pair, hop(dz=1)), moved(pair, hop(dz=-1))
+    across = jnp.stack([moved(below[0], hop(dz=1)), moved(above[1], hop(dz=-1))])
+    ring = [pair, above, across, below]
     ring = jnp.stack(ring + ring, axis=1)
     ring = lax.dynamic_slice_in_dim(ring, 4 - plane, 4, 1)
     ring = ring.reshape(2, columns, width).astype(F32)

time: 190 us -> 190 us (level)
  waiting for transfers between devices: 66.8 us -> 62.4 us
  starting transfers between devices: 69.1 us -> 71.9 us
    ppermute x35 -> x36, waiting for transfers between devices: 66.8 us -> 62.4 us  [moved(): return lax.ppermute(block, AXES, pairs)]
    ppermute x35 -> x36, starting transfers between devices: 69.1 us -> 71.9 us  [moved(): return lax.ppermute(block, AXES, pairs)]
    unnamed x47 -> x45, local copies, waits for them, and re-layouts: 5.7 us -> 5.64 us
  transfers between devices with their start and end apart: 35 -> 36, of which waited for: 18 -> 17; matrix products, arithmetic and copies ran while one was open for 6% -> 6% of each run, Pallas kernels for 15% -> 16%
where the time goes in v5:
time: 190 us; the launch traced here: 188 us
  starting transfers between devices  71.9 us (38%)
  waiting for transfers between devices  62.4 us (33%)
  Pallas kernels  31 us (16%)
  local copies, waits for them, and re-layouts  9.37 us (5%)
  other arithmetic  9.22 us (5%)
  between operations  2.43 us (1%)
    ppermute x36, starting transfers between devices, moved(): return lax.ppermute(block, AXES, pairs)  71.9 us
    ppermute x36, waiting for transfers between devices, moved(): return lax.ppermute(block, AXES, pairs)  62.4 us
    pallas_call x4, Pallas kernels, sums(): pl.pallas_call(functools.partial(sums_kernel, (tuple(names), tuple(plan),...  23.5 us
    pallas_call x1, Pallas kernels, embed(): pl.pallas_call(embed_kernel, in_specs=[pl.BlockSpec(memory_space=pltpu.SM...  5.79 us
    unnamed x45, local copies, waits for them, and re-layouts  5.64 us
  transfers between devices with their start and end apart: 36, of which 17 were waited for; matrix products, arithmetic and copies ran while one was open for 6% of the time, Pallas kernels for 16%

profile of v5, /device:TPU:1, one launch (start us, length us, event | category | flops | bytes accessed | tf_op | source)
XLA Modules:
  0.0 188.2 jit_solution(8726429992674977299)
XLA Ops:
  10.8 2.2 %collective-permute-start.6 = (bf16[512,1152]{1,0:T(8,128)(2,1)S(1)}, bf16[512,1152]{1,0:T(8,128)(2,1)S(1)}, u32[]{:S(2)}, u32[]{:S(2)}) collective-permute-start(bf16[512,1152]{1,0:T(8,128)(2,1)S(1)} %pad_maximum_fusion.refs_4_), channel_id=1, source_target_pairs={{0,96},{1,97},{2,98},{3,99},{4,100},{5,101},{6,102},{7,103},{8,104... | collective-permute-start | bytes 3538952 | tf_op jit(solution)/shard_map/ppermute | solution.py:34
  13.0 9.6 %collective-permute-done.2.refs_2_ = bf16[288,1152]{1,0:T(8,128)(2,1)S(1)} collective-permute-done((bf16[288,1152]{1,0:T(8,128)(2,1)S(1)}, bf16[288,1152]{1,0:T(8,128)(2,1)S(1)}, u32[]{:S(2)}, u32[]{:S(2)}) %collective-permute-start.2) | collective-permute-done | bytes 663584 | tf_op jit(solution)/shard_map/ppermute | solution.py:34
  24.7 5.8 %embed.1 = (f32[512,1152]{1,0:T(8,128)S(1)}, bf16[512,1152]{1,0:T(8,128)(2,1)S(1)}, f32[512,128]{1,0:T(8,128)S(1)}) custom-call(s32[4]{0:T(128)S(1)} %pad_add_fusion.place, bf16[256,1152]{1,0:T(8,128)(2,1)S(1)} %get-tuple-element.73.own, bf16[256,1152]{1,0:T(8,128)(2,1)} %collective-permute-done.mate, bf16[288,1152]{1,0:T(8,128)(2,1)S(1)} %get-tuple-element.35.refs_0_, ...), custom_call_target="tpu_custom_call" | custom-call | flops 300000000 | bytes 1048576 | tf_op jit(solution)/shard_map/embed/pallas_call | solution.py:114
  33.4 2.9 %collective-permute-start.8 = (bf16[512,1152]{1,0:T(8,128)(2,1)S(1)}, bf16[512,1152]{1,0:T(8,128)(2,1)S(1)}, u32[]{:S(2)}, u32[]{:S(2)}) collective-permute-start(bf16[512,1152]{1,0:T(8,128)(2,1)S(1)} %get-tuple-element.40.refs_3_), channel_id=1, source_target_pairs={{1,2},{3,0},{4,7},{6,5},{9,10},{11,8},{12,15},{14,13},{17,18},{19,... | collective-permute-start | bytes 3538952 | tf_op jit(solution)/shard_map/ppermute | solution.py:34
  36.4 2.6 %collective-permute-done.5.refs_5_ = bf16[512,1152]{1,0:T(8,128)(2,1)S(1)} collective-permute-done((bf16[512,1152]{1,0:T(8,128)(2,1)S(1)}, bf16[512,1152]{1,0:T(8,128)(2,1)S(1)}, u32[]{:S(2)}, u32[]{:S(2)}) %collective-permute-start.5) | collective-permute-done | bytes 1179680 | tf_op jit(solution)/shard_map/ppermute | solution.py:34
  39.0 5.8 %collective-permute-start.7 = (bf16[512,1152]{1,0:T(8,128)(2,1)S(1)}, bf16[512,1152]{1,0:T(8,128)(2,1)}, u32[]{:S(2)}, u32[]{:S(2)}) collective-permute-start(bf16[512,1152]{1,0:T(8,128)(2,1)S(1)} %get-tuple-element.40.refs_3_), channel_id=1, source_target_pairs={{1,6},{3,4},{4,3},{6,1},{9,14},{11,12},{12,11},{14,9},{17,22},{19,... | collective-permute-start | bytes 3538952 | tf_op jit(solution)/shard_map/ppermute | solution.py:34
  44.8 4.5 %collective-permute-done.8 = bf16[512,1152]{1,0:T(8,128)(2,1)S(1)} collective-permute-done((bf16[512,1152]{1,0:T(8,128)(2,1)S(1)}, bf16[512,1152]{1,0:T(8,128)(2,1)S(1)}, u32[]{:S(2)}, u32[]{:S(2)}) %collective-permute-start.8) | collective-permute-done | bytes 1179680 | tf_op jit(solution)/shard_map/ppermute | solution.py:34
  52.4 6.0 %collective-permute-start.11 = (bf16[512,1152]{1,0:T(8,128)(2,1)}, bf16[512,1152]{1,0:T(8,128)(2,1)}, u32[]{:S(2)}, u32[]{:S(2)}) collective-permute-start(bf16[512,1152]{1,0:T(8,128)(2,1)} %collective-permute-done.10.refs_5_), channel_id=1, source_target_pairs={{1,7},{3,5},{4,2},{6,0},{9,15},{11,13},{12,10},{14,8},{17,23},{19,... | collective-permute-start | bytes 3538952 | tf_op jit(solution)/shard_map/ppermute | solution.py:34
  59.7 2.4 %broadcast_select_fusion.1.refs_6_ = bf16[512,1152]{1,0:T(8,128)(2,1)} fusion(bf16[512,1152]{1,0:T(8,128)(2,1)} %collective-permute-done.7, bf16[512,1152]{1,0:T(8,128)(2,1)} %copy-done.17, pred[]{:T(512)S(6)} %eq.28), kind=kLoop, calls=%fused_computation.4 | loop fusion | flops 589824 | bytes 3538945 | tf_op jit(solution)/shard_map/jit(_where)/select_n | solution.py:319
  62.1 6.2 %collective-permute-start.14 = (bf16[512,1152]{1,0:T(8,128)(2,1)}, bf16[512,1152]{1,0:T(8,128)(2,1)}, u32[]{:S(2)}, u32[]{:S(2)}) collective-permute-start(bf16[512,1152]{1,0:T(8,128)(2,1)} %broadcast_select_fusion.1.refs_6_), channel_id=1, source_target_pairs={{0,8},{1,121},{2,10},{3,123},{4,12},{5,125},{6,14},{7,127},{8,16},... | collective-permute-start | bytes 3538952 | tf_op jit(solution)/shard_map/ppermute | solution.py:34
  68.4 7.1 %sums.3.refs_6_ = f32[512,1152]{1,0:T(8,128)S(1)} custom-call(f32[1]{0:T(128)S(6)} %copy.21.refs_0_, f32[1]{0:T(128)S(6)} %copy.22.refs_1_, s32[1]{0:T(128)} %bitcast.refs_2_, bf16[512,1152]{1,0:T(8,128)(2,1)S(1)} %get-tuple-element.40.refs_3_, bf16[512,1152]{1,0:T(8,128)(2,1)S(1)} %collective-permute-done.4.refs_4_, ...), custom_call_target="tpu_custom_call" | custom-call | flops 300000000 | bytes 1048576 | tf_op jit(solution)/shard_map/sums/pallas_call | solution.py:233
  79.8 2.0 %collective-permute-done.14.refs_4_ = bf16[512,1152]{1,0:T(8,128)(2,1)} collective-permute-done((bf16[512,1152]{1,0:T(8,128)(2,1)}, bf16[512,1152]{1,0:T(8,128)(2,1)}, u32[]{:S(2)}, u32[]{:S(2)}) %collective-permute-start.14) | collective-permute-done | bytes 1179680 | tf_op jit(solution)/shard_map/ppermute | solution.py:34
  83.7 5.2 %sums.4.refs_5_ = f32[512,1152]{1,0:T(8,128)S(1)} custom-call(f32[1]{0:T(128)S(6)} %copy.21.refs_0_, f32[1]{0:T(128)S(6)} %copy.22.refs_1_, s32[1]{0:T(128)} %bitcast.refs_2_, bf16[512,1152]{1,0:T(8,128)(2,1)S(1)} %get-tuple-element.40.refs_3_, bf16[512,1152]{1,0:T(8,128)(2,1)} %collective-permute-done.14.refs_4_, ...), custom_call_target="tpu_custom_call" | custom-call | flops 300000000 | bytes 1048576 | tf_op jit(solution)/shard_map/sums/pallas_call | solution.py:233
  89.0 5.4 %collective-permute-done.13.refs_4_ = bf16[512,1152]{1,0:T(8,128)(2,1)} collective-permute-done((bf16[512,1152]{1,0:T(8,128)(2,1)S(1)}, bf16[512,1152]{1,0:T(8,128)(2,1)}, u32[]{:S(2)}, u32[]{:S(2)}) %collective-permute-start.13) | collective-permute-done | bytes 1179680 | tf_op jit(solution)/shard_map/ppermute | solution.py:34
  94.4 3.4 %collective-permute-start.15 = (bf16[512,1152]{1,0:T(8,128)(2,1)}, bf16[512,1152]{1,0:T(8,128)(2,1)}, u32[]{:S(2)}, u32[]{:S(2)}) collective-permute-start(bf16[512,1152]{1,0:T(8,128)(2,1)} %collective-permute-done.13.refs_4_), channel_id=1, source_target_pairs={{1,7},{3,5},{4,2},{6,0},{9,15},{11,13},{12,10},{14,8},{17,23},{19,... | collective-permute-start | bytes 3538952 | tf_op jit(solution)/shard_map/ppermute | solution.py:34
  104.2 3.6 %sums.5.refs_8_ = f32[512,1152]{1,0:T(8,128)S(1)} custom-call(f32[1]{0:T(128)S(6)} %copy.21.refs_0_, f32[1]{0:T(128)S(6)} %copy.22.refs_1_, s32[1]{0:T(128)} %bitcast.refs_2_, bf16[512,1152]{1,0:T(8,128)(2,1)S(1)} %get-tuple-element.40.refs_3_, bf16[512,1152]{1,0:T(8,128)(2,1)} %collective-permute-done.13.refs_4_, f32[512,1152]{1,0:T(8,128)S(1)} %sums.4.refs_5_), custom_call_target="tpu_custom_call" | custom-call | flops 300000000 | bytes 1048576 | tf_op jit(solution)/shard_map/sums/pallas_call | solution.py:233
  107.9 2.3 %collective-permute-done.15.refs_5_ = bf16[512,1152]{1,0:T(8,128)(2,1)} collective-permute-done((bf16[512,1152]{1,0:T(8,128)(2,1)}, bf16[512,1152]{1,0:T(8,128)(2,1)}, u32[]{:S(2)}, u32[]{:S(2)}) %collective-permute-start.15) | collective-permute-done | bytes 1179680 | tf_op jit(solution)/shard_map/ppermute | solution.py:34
  110.1 7.5 %finish.1 = (bf16[512,1152]{1,0:T(8,128)(2,1)S(1)}, bf16[288,512]{1,0:T(8,128)(2,1)S(1)}, bf16[288,512]{1,0:T(8,128)(2,1)S(1)}, bf16[288,512]{1,0:T(8,128)(2,1)S(1)}, bf16[288,512]{1,0:T(8,128)(2,1)S(1)}) custom-call(f32[1]{0:T(128)S(6)} %copy.21.refs_0_, f32[1]{0:T(128)S(6)} %copy.22.refs_1_, s32[1]{0:T(128)} %bitcast.refs_2_, ...), custom_call_target="tpu_custom_call" | custom-call | flops 300000000 | bytes 1048576 | tf_op jit(solution)/shard_map/finish/pallas_call | solution.py:233
  118.6 1.9 %collective-permute-start.19 = (bf16[288,512]{1,0:T(8,128)(2,1)S(1)}, bf16[288,512]{1,0:T(8,128)(2,1)S(1)}, u32[]{:S(2)}, u32[]{:S(2)}) collective-permute-start(bf16[288,512]{1,0:T(8,128)(2,1)S(1)} %get-tuple-element.51), channel_id=1, source_target_pairs={{0,96},{1,97},{2,98},{3,99},{4,100},{5,101},{6,102},{7,103},{8,104... | collective-permute-start | bytes 884744 | tf_op jit(solution)/shard_map/ppermute | solution.py:34
  122.4 2.5 %collective-permute-done.20.refs_3_ = bf16[288,512]{1,0:T(8,128)(2,1)S(1)} collective-permute-done((bf16[288,512]{1,0:T(8,128)(2,1)S(1)}, bf16[288,512]{1,0:T(8,128)(2,1)S(1)}, u32[]{:S(2)}, u32[]{:S(2)}) %collective-permute-start.20) | collective-permute-done | bytes 294944 | tf_op jit(solution)/shard_map/ppermute | solution.py:34
  124.9 2.9 %collective-permute-done.18.refs_1_ = bf16[288,512]{1,0:T(8,128)(2,1)S(1)} collective-permute-done((bf16[288,512]{1,0:T(8,128)(2,1)S(1)}, bf16[288,512]{1,0:T(8,128)(2,1)S(1)}, u32[]{:S(2)}, u32[]{:S(2)}) %collective-permute-start.18) | collective-permute-done | bytes 294944 | tf_op jit(solution)/shard_map/ppermute | solution.py:34
  129.6 11.3 %collective-permute-start.23 = (bf16[72,1152]{1,0:T(8,128)(2,1)S(1)}, bf16[72,1152]{1,0:T(8,128)(2,1)S(1)}, u32[]{:S(2)}, u32[]{:S(2)}) collective-permute-start(bf16[72,1152]{1,0:T(8,128)(2,1)S(1)} %get-tuple-element.58), channel_id=1, source_target_pairs={{0,4},{1,5},{2,6},{3,7},{4,0},{5,1},{6,2},{7,3},{8,12},{9,13},{10,... | collective-permute-start | bytes 497672 | tf_op jit(solution)/shard_map/ppermute | solution.py:34
  140.9 2.4 %collective-permute-start.24 = (bf16[72,1152]{1,0:T(8,128)(2,1)S(1)}, bf16[72,1152]{1,0:T(8,128)(2,1)S(1)}, u32[]{:S(2)}, u32[]{:S(2)}) collective-permute-start(bf16[72,1152]{1,0:T(8,128)(2,1)S(1)} %get-tuple-element.59), channel_id=1, source_target_pairs={{0,2},{1,3},{2,0},{3,1},{4,6},{5,7},{6,4},{7,5},{8,10},{9,11},{10,... | collective-permute-start | bytes 497672 | tf_op jit(solution)/shard_map/ppermute | solution.py:34
  145.2 5.5 %collective-permute-done.24 = bf16[72,1152]{1,0:T(8,128)(2,1)S(1)} collective-permute-done((bf16[72,1152]{1,0:T(8,128)(2,1)S(1)}, bf16[72,1152]{1,0:T(8,128)(2,1)S(1)}, u32[]{:S(2)}, u32[]{:S(2)}) %collective-permute-start.24) | collective-permute-done | bytes 165920 | tf_op jit(solution)/shard_map/ppermute | solution.py:34
  151.0 2.7 %collective-permute-start.29 = (bf16[72,1152]{1,0:T(8,128)(2,1)S(1)}, bf16[72,1152]{1,0:T(8,128)(2,1)S(1)}, u32[]{:S(2)}, u32[]{:S(2)}) collective-permute-start(bf16[72,1152]{1,0:T(8,128)(2,1)S(1)} %fusion.2), channel_id=1, source_target_pairs={{0,24},{1,25},{2,26},{3,27},{4,28},{5,29},{6,30},{7,31},{8,0},{9,1... | collective-permute-start | bytes 497672 | tf_op jit(solution)/shard_map/ppermute | solution.py:34
  153.6 3.0 %collective-permute-done.27 = bf16[72,1152]{1,0:T(8,128)(2,1)S(1)} collective-permute-done((bf16[72,1152]{1,0:T(8,128)(2,1)S(1)}, bf16[72,1152]{1,0:T(8,128)(2,1)S(1)}, u32[]{:S(2)}, u32[]{:S(2)}) %collective-permute-start.27) | collective-permute-done | bytes 165920 | tf_op jit(solution)/shard_map/ppermute | solution.py:34
  156.7 5.0 %collective-permute-done.28 = bf16[72,1152]{1,0:T(8,128)(2,1)S(1)} collective-permute-done((bf16[72,1152]{1,0:T(8,128)(2,1)S(1)}, bf16[72,1152]{1,0:T(8,128)(2,1)S(1)}, u32[]{:S(2)}, u32[]{:S(2)}) %collective-permute-start.28) | collective-permute-done | bytes 165920 | tf_op jit(solution)/shard_map/ppermute | solution.py:34
  162.6 3.2 %collective-permute-start.31 = (bf16[72,1152]{1,0:T(8,128)(2,1)S(1)}, bf16[72,1152]{1,0:T(8,128)(2,1)S(1)}, u32[]{:S(2)}, u32[]{:S(2)}) collective-permute-start(bf16[72,1152]{1,0:T(8,128)(2,1)S(1)} %add_convert_fusion), channel_id=1, source_target_pairs={{1,4},{3,6},{4,1},{6,3},{9,12},{11,14},{12,9},{14,11},{17,20},{19,... | collective-permute-start | bytes 497672 | tf_op jit(solution)/shard_map/ppermute | solution.py:34
  167.6 3.2 %collective-permute-done.31 = bf16[72,1152]{1,0:T(8,128)(2,1)S(1)} collective-permute-done((bf16[72,1152]{1,0:T(8,128)(2,1)S(1)}, bf16[72,1152]{1,0:T(8,128)(2,1)S(1)}, u32[]{:S(2)}, u32[]{:S(2)}) %collective-permute-start.31) | collective-permute-done | bytes 165920 | tf_op jit(solution)/shard_map/ppermute | solution.py:34
  172.4 7.5 %collective-permute-done.33 = bf16[2,72,1152]{2,1,0:T(8,128)(2,1)S(1)} collective-permute-done((bf16[2,72,1152]{2,1,0:T(8,128)(2,1)S(1)}, bf16[2,72,1152]{2,1,0:T(8,128)(2,1)S(1)}, u32[]{:S(2)}, u32[]{:S(2)}) %collective-permute-start.33) | collective-permute-done | bytes 331808 | tf_op jit(solution)/shard_map/ppermute | solution.py:34
  180.1 2.7 %collective-permute-start.35 = (bf16[72,1152]{1,0:T(8,128)(2,1)S(1)}, bf16[72,1152]{1,0:T(8,128)(2,1)S(1)}, u32[]{:S(2)}, u32[]{:S(2)}) collective-permute-start(bf16[72,1152]{1,0:T(8,128)(2,1)S(1)} %slice_bitcast_fusion), channel_id=1, source_target_pairs={{0,96},{1,97},{2,98},{3,99},{4,100},{5,101},{6,102},{7,103},{8,104... | collective-permute-start | bytes 497672 | tf_op jit(solution)/shard_map/ppermute | solution.py:34
  182.8 3.2 %collective-permute-done.34 = bf16[72,1152]{1,0:T(8,128)(2,1)S(1)} collective-permute-done((bf16[72,1152]{1,0:T(8,128)(2,1)S(1)}, bf16[72,1152]{1,0:T(8,128)(2,1)S(1)}, u32[]{:S(2)}, u32[]{:S(2)}) %collective-permute-start.34) | collective-permute-done | bytes 165920 | tf_op jit(solution)/shard_map/ppermute | solution.py:34
  (119 shorter events, 44.1 us)
Async XLA Ops:
  4.6 18.0 %collective-permute-start.2 = (bf16[288,1152]{1,0:T(8,128)(2,1)S(1)}, bf16[288,1152]{1,0:T(8,128)(2,1)S(1)}, u32[]{:S(2)}, u32[]{:S(2)}) collective-permute-start(bf16[288,1152]{1,0:T(8,128)(2,1)S(1)} %get-tuple-element.35.refs_0_), channel_id=1, source_target_pairs={{0,2},{1,3},{2,4},{3,5},{4,6},{5,7},{6,0},{7,1},{8,10},{9,11},{10,... | collective-permute-start | bytes 1990664 | tf_op jit(solution)/shard_map/ppermute | solution.py:34
  6.0 17.4 %collective-permute-start.3 = (bf16[288,1152]{1,0:T(8,128)(2,1)}, bf16[288,1152]{1,0:T(8,128)(2,1)S(1)}, u32[]{:S(2)}, u32[]{:S(2)}) collective-permute-start(bf16[288,1152]{1,0:T(8,128)(2,1)} %get-tuple-element.37), channel_id=1, source_target_pairs={{0,7},{1,6},{2,1},{3,0},{4,3},{5,2},{6,5},{7,4},{8,15},{9,14},{10,... | collective-permute-start | bytes 1990664 | tf_op jit(solution)/shard_map/ppermute | solution.py:34
  7.5 15.9 %collective-permute-start.1 = (bf16[288,1152]{1,0:T(8,128)(2,1)}, bf16[288,1152]{1,0:T(8,128)(2,1)}, u32[]{:S(2)}, u32[]{:S(2)}) collective-permute-start(bf16[288,1152]{1,0:T(8,128)(2,1)} %get-tuple-element.37), channel_id=1, source_target_pairs={{0,1},{1,0},{2,3},{3,2},{4,5},{5,4},{6,7},{7,6},{8,9},{9,8},{10,11... | collective-permute-start | bytes 1990664 | tf_op jit(solution)/shard_map/ppermute | solution.py:34
  9.1 30.0 %collective-permute-start.5 = (bf16[512,1152]{1,0:T(8,128)(2,1)S(1)}, bf16[512,1152]{1,0:T(8,128)(2,1)S(1)}, u32[]{:S(2)}, u32[]{:S(2)}) collective-permute-start(bf16[512,1152]{1,0:T(8,128)(2,1)S(1)} %pad_maximum_fusion.refs_4_), channel_id=1, source_target_pairs={{0,32},{1,33},{2,34},{3,35},{4,36},{5,37},{6,38},{7,39},{8,40},{9,... | collective-permute-start | bytes 3538952 | tf_op jit(solution)/shard_map/ppermute | solution.py:34
  10.8 28.3 %collective-permute-start.6 = (bf16[512,1152]{1,0:T(8,128)(2,1)S(1)}, bf16[512,1152]{1,0:T(8,128)(2,1)S(1)}, u32[]{:S(2)}, u32[]{:S(2)}) collective-permute-start(bf16[512,1152]{1,0:T(8,128)(2,1)S(1)} %pad_maximum_fusion.refs_4_), channel_id=1, source_target_pairs={{0,96},{1,97},{2,98},{3,99},{4,100},{5,101},{6,102},{7,103},{8,104... | collective-permute-start | bytes 3538952 | tf_op jit(solution)/shard_map/ppermute | solution.py:34
  32.7 6.4 %collective-permute-start.4 = (bf16[512,1152]{1,0:T(8,128)(2,1)S(1)}, bf16[512,1152]{1,0:T(8,128)(2,1)S(1)}, u32[]{:S(2)}, u32[]{:S(2)}) collective-permute-start(bf16[512,1152]{1,0:T(8,128)(2,1)S(1)} %get-tuple-element.40.refs_3_), channel_id=1, source_target_pairs={{0,1},{1,0},{2,3},{3,2},{4,5},{5,4},{6,7},{7,6},{8,9},{9,8},{10,11... | collective-permute-start | bytes 3538952 | tf_op jit(solution)/shard_map/ppermute | solution.py:34
  33.4 16.0 %collective-permute-start.8 = (bf16[512,1152]{1,0:T(8,128)(2,1)S(1)}, bf16[512,1152]{1,0:T(8,128)(2,1)S(1)}, u32[]{:S(2)}, u32[]{:S(2)}) collective-permute-start(bf16[512,1152]{1,0:T(8,128)(2,1)S(1)} %get-tuple-element.40.refs_3_), channel_id=1, source_target_pairs={{1,2},{3,0},{4,7},{6,5},{9,10},{11,8},{12,15},{14,13},{17,18},{19,... | collective-permute-start | bytes 3538952 | tf_op jit(solution)/shard_map/ppermute | solution.py:34
  36.3 16.1 %collective-permute-start.10 = (bf16[512,1152]{1,0:T(8,128)(2,1)S(1)}, bf16[512,1152]{1,0:T(8,128)(2,1)}, u32[]{:S(2)}, u32[]{:S(2)}) collective-permute-start(bf16[512,1152]{1,0:T(8,128)(2,1)S(1)} %get-tuple-element.40.refs_3_), channel_id=1, source_target_pairs={{0,121},{1,8},{2,123},{3,10},{4,125},{5,12},{6,127},{7,14},{8,1},{... | collective-permute-start | bytes 3538952 | tf_op jit(solution)/shard_map/ppermute | solution.py:34
  39.0 20.7 %collective-permute-start.7 = (bf16[512,1152]{1,0:T(8,128)(2,1)S(1)}, bf16[512,1152]{1,0:T(8,128)(2,1)}, u32[]{:S(2)}, u32[]{:S(2)}) collective-permute-start(bf16[512,1152]{1,0:T(8,128)(2,1)S(1)} %get-tuple-element.40.refs_3_), channel_id=1, source_target_pairs={{1,6},{3,4},{4,3},{6,1},{9,14},{11,12},{12,11},{14,9},{17,22},{19,... | collective-permute-start | bytes 3538952 | tf_op jit(solution)/shard_map/ppermute | solution.py:34
  49.3 26.2 %collective-permute-start.9 = (bf16[512,1152]{1,0:T(8,128)(2,1)S(1)}, bf16[512,1152]{1,0:T(8,128)(2,1)}, u32[]{:S(2)}, u32[]{:S(2)}) collective-permute-start(bf16[512,1152]{1,0:T(8,128)(2,1)S(1)} %get-tuple-element.40.refs_3_), channel_id=1, source_target_pairs={{0,3},{2,1},{5,6},{7,4},{8,11},{10,9},{13,14},{15,12},{16,19},{18,... | collective-permute-start | bytes 3538952 | tf_op jit(solution)/shard_map/ppermute | solution.py:34
  52.4 23.1 %collective-permute-start.11 = (bf16[512,1152]{1,0:T(8,128)(2,1)}, bf16[512,1152]{1,0:T(8,128)(2,1)}, u32[]{:S(2)}, u32[]{:S(2)}) collective-permute-start(bf16[512,1152]{1,0:T(8,128)(2,1)} %collective-permute-done.10.refs_5_), channel_id=1, source_target_pairs={{1,7},{3,5},{4,2},{6,0},{9,15},{11,13},{12,10},{14,8},{17,23},{19,... | collective-permute-start | bytes 3538952 | tf_op jit(solution)/shard_map/ppermute | solution.py:34
  62.1 19.7 %collective-permute-start.14 = (bf16[512,1152]{1,0:T(8,128)(2,1)}, bf16[512,1152]{1,0:T(8,128)(2,1)}, u32[]{:S(2)}, u32[]{:S(2)}) collective-permute-start(bf16[512,1152]{1,0:T(8,128)(2,1)} %broadcast_select_fusion.1.refs_6_), channel_id=1, source_target_pairs={{0,8},{1,121},{2,10},{3,123},{4,12},{5,125},{6,14},{7,127},{8,16},... | collective-permute-start | bytes 3538952 | tf_op jit(solution)/shard_map/ppermute | solution.py:34
  76.9 17.4 %collective-permute-start.13 = (bf16[512,1152]{1,0:T(8,128)(2,1)S(1)}, bf16[512,1152]{1,0:T(8,128)(2,1)}, u32[]{:S(2)}, u32[]{:S(2)}) collective-permute-start(bf16[512,1152]{1,0:T(8,128)(2,1)S(1)} %broadcast_select_fusion.refs_5_), channel_id=1, source_target_pairs={{0,8},{1,121},{2,10},{3,123},{4,12},{5,125},{6,14},{7,127},{8,16},... | collective-permute-start | bytes 3538952 | tf_op jit(solution)/shard_map/ppermute | solution.py:34
  78.5 24.0 %collective-permute-start.12 = (bf16[512,1152]{1,0:T(8,128)(2,1)}, bf16[512,1152]{1,0:T(8,128)(2,1)}, u32[]{:S(2)}, u32[]{:S(2)}) collective-permute-start(bf16[512,1152]{1,0:T(8,128)(2,1)} %broadcast_select_fusion.1.refs_6_), channel_id=1, source_target_pairs={{0,6},{2,4},{5,3},{7,1},{8,14},{10,12},{13,11},{15,9},{16,22},{18,... | collective-permute-start | bytes 3538952 | tf_op jit(solution)/shard_map/ppermute | solution.py:34
  81.8 20.8 %collective-permute-start.16 = (bf16[512,1152]{1,0:T(8,128)(2,1)}, bf16[512,1152]{1,0:T(8,128)(2,1)}, u32[]{:S(2)}, u32[]{:S(2)}) collective-permute-start(bf16[512,1152]{1,0:T(8,128)(2,1)} %collective-permute-done.14.refs_4_), channel_id=1, source_target_pairs={{1,3},{3,1},{4,6},{6,4},{9,11},{11,9},{12,14},{14,12},{17,19},{19,... | collective-permute-start | bytes 3538952 | tf_op jit(solution)/shard_map/ppermute | solution.py:34
  94.4 15.8 %collective-permute-start.15 = (bf16[512,1152]{1,0:T(8,128)(2,1)}, bf16[512,1152]{1,0:T(8,128)(2,1)}, u32[]{:S(2)}, u32[]{:S(2)}) collective-permute-start(bf16[512,1152]{1,0:T(8,128)(2,1)} %collective-permute-done.13.refs_4_), channel_id=1, source_target_pairs={{1,7},{3,5},{4,2},{6,0},{9,15},{11,13},{12,10},{14,8},{17,23},{19,... | collective-permute-start | bytes 3538952 | tf_op jit(solution)/shard_map/ppermute | solution.py:34
  97.8 12.4 %collective-permute-start.17 = (bf16[512,1152]{1,0:T(8,128)(2,1)}, bf16[512,1152]{1,0:T(8,128)(2,1)}, u32[]{:S(2)}, u32[]{:S(2)}) collective-permute-start(bf16[512,1152]{1,0:T(8,128)(2,1)} %collective-permute-done.13.refs_4_), channel_id=1, source_target_pairs={{0,2},{2,0},{5,7},{7,5},{8,10},{10,8},{13,15},{15,13},{16,18},{18,... | collective-permute-start | bytes 3538952 | tf_op jit(solution)/shard_map/ppermute | solution.py:34
  102.6 25.3 %collective-permute-start.22 = (bf16[256,1152]{1,0:T(8,128)(2,1)S(1)}, bf16[256,1152]{1,0:T(8,128)(2,1)S(1)}, u32[]{:S(2)}, u32[]{:S(2)}) collective-permute-start(bf16[256,1152]{1,0:T(8,128)(2,1)S(1)} %slice.36), channel_id=1, source_target_pairs={{0,96},{1,97},{2,98},{3,99},{4,100},{5,101},{6,102},{7,103},{8,104... | collective-permute-start | bytes 1769480 | tf_op jit(solution)/shard_map/ppermute | solution.py:34
  103.0 24.9 %collective-permute-start.21 = (bf16[256,1152]{1,0:T(8,128)(2,1)S(1)}, bf16[256,1152]{1,0:T(8,128)(2,1)S(1)}, u32[]{:S(2)}, u32[]{:S(2)}) collective-permute-start(bf16[256,1152]{1,0:T(8,128)(2,1)S(1)} %slice.35), channel_id=1, source_target_pairs={{0,32},{1,33},{2,34},{3,35},{4,36},{5,37},{6,38},{7,39},{8,40},{9,... | collective-permute-start | bytes 1769480 | tf_op jit(solution)/shard_map/ppermute | solution.py:34
  117.7 7.3 %collective-permute-start.20 = (bf16[288,512]{1,0:T(8,128)(2,1)S(1)}, bf16[288,512]{1,0:T(8,128)(2,1)S(1)}, u32[]{:S(2)}, u32[]{:S(2)}) collective-permute-start(bf16[288,512]{1,0:T(8,128)(2,1)S(1)} %get-tuple-element.52), channel_id=1, source_target_pairs={{0,64},{1,65},{2,66},{3,67},{4,68},{5,69},{6,70},{7,71},{8,72},{9,... | collective-permute-start | bytes 884744 | tf_op jit(solution)/shard_map/ppermute | solution.py:34
  117.9 9.9 %collective-permute-start.18 = (bf16[288,512]{1,0:T(8,128)(2,1)S(1)}, bf16[288,512]{1,0:T(8,128)(2,1)S(1)}, u32[]{:S(2)}, u32[]{:S(2)}) collective-permute-start(bf16[288,512]{1,0:T(8,128)(2,1)S(1)} %get-tuple-element.50), channel_id=1, source_target_pairs={{0,32},{1,33},{2,34},{3,35},{4,36},{5,37},{6,38},{7,39},{8,40},{9,... | collective-permute-start | bytes 884744 | tf_op jit(solution)/shard_map/ppermute | solution.py:34
  118.6 9.2 %collective-permute-start.19 = (bf16[288,512]{1,0:T(8,128)(2,1)S(1)}, bf16[288,512]{1,0:T(8,128)(2,1)S(1)}, u32[]{:S(2)}, u32[]{:S(2)}) collective-permute-start(bf16[288,512]{1,0:T(8,128)(2,1)S(1)} %get-tuple-element.51), channel_id=1, source_target_pairs={{0,96},{1,97},{2,98},{3,99},{4,100},{5,101},{6,102},{7,103},{8,104... | collective-permute-start | bytes 884744 | tf_op jit(solution)/shard_map/ppermute | solution.py:34
  129.6 15.6 %collective-permute-start.23 = (bf16[72,1152]{1,0:T(8,128)(2,1)S(1)}, bf16[72,1152]{1,0:T(8,128)(2,1)S(1)}, u32[]{:S(2)}, u32[]{:S(2)}) collective-permute-start(bf16[72,1152]{1,0:T(8,128)(2,1)S(1)} %get-tuple-element.58), channel_id=1, source_target_pairs={{0,4},{1,5},{2,6},{3,7},{4,0},{5,1},{6,2},{7,3},{8,12},{9,13},{10,... | collective-permute-start | bytes 497672 | tf_op jit(solution)/shard_map/ppermute | solution.py:34
  140.9 9.8 %collective-permute-start.24 = (bf16[72,1152]{1,0:T(8,128)(2,1)S(1)}, bf16[72,1152]{1,0:T(8,128)(2,1)S(1)}, u32[]{:S(2)}, u32[]{:S(2)}) collective-permute-start(bf16[72,1152]{1,0:T(8,128)(2,1)S(1)} %get-tuple-element.59), channel_id=1, source_target_pairs={{0,2},{1,3},{2,0},{3,1},{4,6},{5,7},{6,4},{7,5},{8,10},{9,11},{10,... | collective-permute-start | bytes 497672 | tf_op jit(solution)/shard_map/ppermute | solution.py:34
  143.2 7.5 %collective-permute-start.25 = (bf16[72,1152]{1,0:T(8,128)(2,1)S(1)}, bf16[72,1152]{1,0:T(8,128)(2,1)S(1)}, u32[]{:S(2)}, u32[]{:S(2)}) collective-permute-start(bf16[72,1152]{1,0:T(8,128)(2,1)S(1)} %get-tuple-element.60), channel_id=1, source_target_pairs={{0,6},{1,7},{2,4},{3,5},{4,2},{5,3},{6,0},{7,1},{8,14},{9,15},{10,... | collective-permute-start | bytes 497672 | tf_op jit(solution)/shard_map/ppermute | solution.py:34
  143.3 7.5 %collective-permute-start.26 = (bf16[256,1152]{1,0:T(8,128)(2,1)S(1)}, bf16[256,1152]{1,0:T(8,128)(2,1)S(1)}, u32[]{:S(2)}, u32[]{:S(2)}) collective-permute-start(bf16[256,1152]{1,0:T(8,128)(2,1)S(1)} %slice.29), channel_id=1, source_target_pairs={{0,1},{1,0},{2,3},{3,2},{4,5},{5,4},{6,7},{7,6},{8,9},{9,8},{10,11... | collective-permute-start | bytes 1769480 | tf_op jit(solution)/shard_map/ppermute | solution.py:34
  150.9 10.8 %collective-permute-start.28 = (bf16[72,1152]{1,0:T(8,128)(2,1)S(1)}, bf16[72,1152]{1,0:T(8,128)(2,1)S(1)}, u32[]{:S(2)}, u32[]{:S(2)}) collective-permute-start(bf16[72,1152]{1,0:T(8,128)(2,1)S(1)} %fusion.2), channel_id=1, source_target_pairs={{0,8},{1,9},{2,10},{3,11},{4,12},{5,13},{6,14},{7,15},{8,16},{9,17... | collective-permute-start | bytes 497672 | tf_op jit(solution)/shard_map/ppermute | solution.py:34
  151.0 10.7 %collective-permute-start.29 = (bf16[72,1152]{1,0:T(8,128)(2,1)S(1)}, bf16[72,1152]{1,0:T(8,128)(2,1)S(1)}, u32[]{:S(2)}, u32[]{:S(2)}) collective-permute-start(bf16[72,1152]{1,0:T(8,128)(2,1)S(1)} %fusion.2), channel_id=1, source_target_pairs={{0,24},{1,25},{2,26},{3,27},{4,28},{5,29},{6,30},{7,31},{8,0},{9,1... | collective-permute-start | bytes 497672 | tf_op jit(solution)/shard_map/ppermute | solution.py:34
  162.6 8.2 %collective-permute-start.31 = (bf16[72,1152]{1,0:T(8,128)(2,1)S(1)}, bf16[72,1152]{1,0:T(8,128)(2,1)S(1)}, u32[]{:S(2)}, u32[]{:S(2)}) collective-permute-start(bf16[72,1152]{1,0:T(8,128)(2,1)S(1)} %add_convert_fusion), channel_id=1, source_target_pairs={{1,4},{3,6},{4,1},{6,3},{9,12},{11,14},{12,9},{14,11},{17,20},{19,... | collective-permute-start | bytes 497672 | tf_op jit(solution)/shard_map/ppermute | solution.py:34
  170.9 9.2 %collective-permute-start.32 = (bf16[2,72,1152]{2,1,0:T(8,128)(2,1)S(1)}, bf16[2,72,1152]{2,1,0:T(8,128)(2,1)S(1)}, u32[]{:S(2)}, u32[]{:S(2)}) collective-permute-start(bf16[2,72,1152]{2,1,0:T(8,128)(2,1)S(1)} %pad_maximum_fusion.1), channel_id=1, source_target_pairs={{0,96},{1,97},{2,98},{3,99},{4,100},{5,101},{6,102},{7,103},{8,104... | collective-permute-start | bytes 995336 | tf_op jit(solution)/shard_map/ppermute | solution.py:34
  171.5 8.5 %collective-permute-start.33 = (bf16[2,72,1152]{2,1,0:T(8,128)(2,1)S(1)}, bf16[2,72,1152]{2,1,0:T(8,128)(2,1)S(1)}, u32[]{:S(2)}, u32[]{:S(2)}) collective-permute-start(bf16[2,72,1152]{2,1,0:T(8,128)(2,1)S(1)} %pad_maximum_fusion.1), channel_id=1, source_target_pairs={{0,32},{1,33},{2,34},{3,35},{4,36},{5,37},{6,38},{7,39},{8,40},{9,... | collective-permute-start | bytes 995336 | tf_op jit(solution)/shard_map/ppermute | solution.py:34
  180.0 6.1 %collective-permute-start.34 = (bf16[72,1152]{1,0:T(8,128)(2,1)S(1)}, bf16[72,1152]{1,0:T(8,128)(2,1)S(1)}, u32[]{:S(2)}, u32[]{:S(2)}) collective-permute-start(bf16[72,1152]{1,0:T(8,128)(2,1)S(1)} %slice_bitcast_fusion.1), channel_id=1, source_target_pairs={{0,32},{1,33},{2,34},{3,35},{4,36},{5,37},{6,38},{7,39},{8,40},{9,... | collective-permute-start | bytes 497672 | tf_op jit(solution)/shard_map/ppermute | solution.py:34
  (24 other events, 200.7 us)

commit v6 on v4

--- a/solution.py
+++ b/solution.py
@@ -187,7 +187,7 @@
 
 def sums(emb, units, scale, bias, odd, total=None, label=False, finish=None):
     count, width = emb.shape
-    block = 256
+    block = 512
     smem = pl.BlockSpec(memory_space=pltpu.SMEM)
     rows = pl.BlockSpec((block, width), lambda i: (i, 0))
     whole = pl.BlockSpec((count, width), lambda i: (0, 0))

time: 190 us -> 190 us (level)
  Pallas kernels: 31 us -> 29 us
    pallas_call x4, Pallas kernels: 23.5 us -> 21.5 us  [sums(): pl.pallas_call(functools.partial(sums_kernel, (tuple(names), tuple(plan),...]
  transfers between devices with their start and end apart: 35 -> 35, of which waited for: 18 -> 18; matrix products, arithmetic and copies ran while one was open for 6% -> 6% of each run, Pallas kernels for 15% -> 14%
where the time goes in v6:
time: 190 us; the launch traced here: 189 us
  starting transfers between devices  69.6 us (37%)
  waiting for transfers between devices  67.5 us (36%)
  Pallas kernels  29 us (15%)
  local copies, waits for them, and re-layouts  9.4 us (5%)
  other arithmetic  9.16 us (5%)
  between operations  2.39 us (1%)
    ppermute x35, starting transfers between devices, moved(): return lax.ppermute(block, AXES, pairs)  69.6 us
    ppermute x35, waiting for transfers between devices, moved(): return lax.ppermute(block, AXES, pairs)  67.5 us
    pallas_call x4, Pallas kernels, sums(): pl.pallas_call(functools.partial(sums_kernel, (tuple(names), tuple(plan),...  21.5 us
    pallas_call x1, Pallas kernels, embed(): pl.pallas_call(embed_kernel, in_specs=[pl.BlockSpec(memory_space=pltpu.SM...  5.79 us
    unnamed x47, local copies, waits for them, and re-layouts  5.7 us
  transfers between devices with their start and end apart: 35, of which 18 were waited for; matrix products, arithmetic and copies ran while one was open for 6% of the time, Pallas kernels for 14%

profile of v6, /device:TPU:1, one launch (start us, length us, event | category | flops | bytes accessed | tf_op | source)
XLA Modules:
  0.0 188.9 jit_solution(1425050888385239565)
XLA Ops:
  10.8 2.2 %collective-permute-start.6 = (bf16[512,1152]{1,0:T(8,128)(2,1)S(1)}, bf16[512,1152]{1,0:T(8,128)(2,1)S(1)}, u32[]{:S(2)}, u32[]{:S(2)}) collective-permute-start(bf16[512,1152]{1,0:T(8,128)(2,1)S(1)} %pad_maximum_fusion.refs_4_), channel_id=1, source_target_pairs={{0,96},{1,97},{2,98},{3,99},{4,100},{5,101},{6,102},{7,103},{8,104... | collective-permute-start | bytes 3538952 | tf_op jit(solution)/shard_map/ppermute | solution.py:34
  13.0 9.6 %collective-permute-done.2.refs_2_ = bf16[288,1152]{1,0:T(8,128)(2,1)S(1)} collective-permute-done((bf16[288,1152]{1,0:T(8,128)(2,1)S(1)}, bf16[288,1152]{1,0:T(8,128)(2,1)S(1)}, u32[]{:S(2)}, u32[]{:S(2)}) %collective-permute-start.2) | collective-permute-done | bytes 663584 | tf_op jit(solution)/shard_map/ppermute | solution.py:34
  24.8 5.8 %embed.1 = (f32[512,1152]{1,0:T(8,128)S(1)}, bf16[512,1152]{1,0:T(8,128)(2,1)S(1)}, f32[512,128]{1,0:T(8,128)S(1)}) custom-call(s32[4]{0:T(128)S(1)} %pad_add_fusion.place, bf16[256,1152]{1,0:T(8,128)(2,1)S(1)} %get-tuple-element.73.own, bf16[256,1152]{1,0:T(8,128)(2,1)} %collective-permute-done.mate, bf16[288,1152]{1,0:T(8,128)(2,1)S(1)} %get-tuple-element.35.refs_0_, ...), custom_call_target="tpu_custom_call" | custom-call | flops 300000000 | bytes 1048576 | tf_op jit(solution)/shard_map/embed/pallas_call | solution.py:114
  33.4 2.9 %collective-permute-start.8 = (bf16[512,1152]{1,0:T(8,128)(2,1)S(1)}, bf16[512,1152]{1,0:T(8,128)(2,1)S(1)}, u32[]{:S(2)}, u32[]{:S(2)}) collective-permute-start(bf16[512,1152]{1,0:T(8,128)(2,1)S(1)} %get-tuple-element.40.refs_3_), channel_id=1, source_target_pairs={{1,2},{3,0},{4,7},{6,5},{9,10},{11,8},{12,15},{14,13},{17,18},{19,... | collective-permute-start | bytes 3538952 | tf_op jit(solution)/shard_map/ppermute | solution.py:34
  36.4 2.7 %collective-permute-done.5.refs_5_ = bf16[512,1152]{1,0:T(8,128)(2,1)S(1)} collective-permute-done((bf16[512,1152]{1,0:T(8,128)(2,1)S(1)}, bf16[512,1152]{1,0:T(8,128)(2,1)S(1)}, u32[]{:S(2)}, u32[]{:S(2)}) %collective-permute-start.5) | collective-permute-done | bytes 1179680 | tf_op jit(solution)/shard_map/ppermute | solution.py:34
  39.0 5.8 %collective-permute-start.7 = (bf16[512,1152]{1,0:T(8,128)(2,1)S(1)}, bf16[512,1152]{1,0:T(8,128)(2,1)}, u32[]{:S(2)}, u32[]{:S(2)}) collective-permute-start(bf16[512,1152]{1,0:T(8,128)(2,1)S(1)} %get-tuple-element.40.refs_3_), channel_id=1, source_target_pairs={{1,6},{3,4},{4,3},{6,1},{9,14},{11,12},{12,11},{14,9},{17,22},{19,... | collective-permute-start | bytes 3538952 | tf_op jit(solution)/shard_map/ppermute | solution.py:34
  44.8 4.5 %collective-permute-done.8 = bf16[512,1152]{1,0:T(8,128)(2,1)S(1)} collective-permute-done((bf16[512,1152]{1,0:T(8,128)(2,1)S(1)}, bf16[512,1152]{1,0:T(8,128)(2,1)S(1)}, u32[]{:S(2)}, u32[]{:S(2)}) %collective-permute-start.8) | collective-permute-done | bytes 1179680 | tf_op jit(solution)/shard_map/ppermute | solution.py:34
  52.4 6.0 %collective-permute-start.11 = (bf16[512,1152]{1,0:T(8,128)(2,1)}, bf16[512,1152]{1,0:T(8,128)(2,1)}, u32[]{:S(2)}, u32[]{:S(2)}) collective-permute-start(bf16[512,1152]{1,0:T(8,128)(2,1)} %collective-permute-done.10.refs_5_), channel_id=1, source_target_pairs={{1,7},{3,5},{4,2},{6,0},{9,15},{11,13},{12,10},{14,8},{17,23},{19,... | collective-permute-start | bytes 3538952 | tf_op jit(solution)/shard_map/ppermute | solution.py:34
  59.7 2.4 %broadcast_select_fusion.1.refs_6_ = bf16[512,1152]{1,0:T(8,128)(2,1)} fusion(bf16[512,1152]{1,0:T(8,128)(2,1)} %collective-permute-done.7, bf16[512,1152]{1,0:T(8,128)(2,1)} %copy-done.17, pred[]{:T(512)S(6)} %eq.28), kind=kLoop, calls=%fused_computation.4 | loop fusion | flops 589824 | bytes 3538945 | tf_op jit(solution)/shard_map/jit(_where)/select_n | solution.py:319
  62.1 6.2 %collective-permute-start.14 = (bf16[512,1152]{1,0:T(8,128)(2,1)}, bf16[512,1152]{1,0:T(8,128)(2,1)}, u32[]{:S(2)}, u32[]{:S(2)}) collective-permute-start(bf16[512,1152]{1,0:T(8,128)(2,1)} %broadcast_select_fusion.1.refs_6_), channel_id=1, source_target_pairs={{0,8},{1,121},{2,10},{3,123},{4,12},{5,125},{6,14},{7,127},{8,16},... | collective-permute-start | bytes 3538952 | tf_op jit(solution)/shard_map/ppermute | solution.py:34
  68.3 6.8 %sums.3.refs_6_ = f32[512,1152]{1,0:T(8,128)S(1)} custom-call(f32[1]{0:T(128)S(6)} %copy.21.refs_0_, f32[1]{0:T(128)S(6)} %copy.22.refs_1_, s32[1]{0:T(128)} %bitcast.refs_2_, bf16[512,1152]{1,0:T(8,128)(2,1)S(1)} %get-tuple-element.40.refs_3_, bf16[512,1152]{1,0:T(8,128)(2,1)S(1)} %collective-permute-done.4.refs_4_, ...), custom_call_target="tpu_custom_call" | custom-call | flops 300000000 | bytes 1048576 | tf_op jit(solution)/shard_map/sums/pallas_call | solution.py:233
  79.8 2.0 %collective-permute-done.14.refs_4_ = bf16[512,1152]{1,0:T(8,128)(2,1)} collective-permute-done((bf16[512,1152]{1,0:T(8,128)(2,1)}, bf16[512,1152]{1,0:T(8,128)(2,1)}, u32[]{:S(2)}, u32[]{:S(2)}) %collective-permute-start.14) | collective-permute-done | bytes 1179680 | tf_op jit(solution)/shard_map/ppermute | solution.py:34
  81.8 2.1 %collective-permute-start.16 = (bf16[512,1152]{1,0:T(8,128)(2,1)}, bf16[512,1152]{1,0:T(8,128)(2,1)}, u32[]{:S(2)}, u32[]{:S(2)}) collective-permute-start(bf16[512,1152]{1,0:T(8,128)(2,1)} %collective-permute-done.14.refs_4_), channel_id=1, source_target_pairs={{1,3},{3,1},{4,6},{6,4},{9,11},{11,9},{12,14},{14,12},{17,19},{19,... | collective-permute-start | bytes 3538952 | tf_op jit(solution)/shard_map/ppermute | solution.py:34
  83.9 4.7 %sums.4.refs_5_ = f32[512,1152]{1,0:T(8,128)S(1)} custom-call(f32[1]{0:T(128)S(6)} %copy.21.refs_0_, f32[1]{0:T(128)S(6)} %copy.22.refs_1_, s32[1]{0:T(128)} %bitcast.refs_2_, bf16[512,1152]{1,0:T(8,128)(2,1)S(1)} %get-tuple-element.40.refs_3_, bf16[512,1152]{1,0:T(8,128)(2,1)} %collective-permute-done.14.refs_4_, ...), custom_call_target="tpu_custom_call" | custom-call | flops 300000000 | bytes 1048576 | tf_op jit(solution)/shard_map/sums/pallas_call | solution.py:233
  88.6 5.7 %collective-permute-done.13.refs_4_ = bf16[512,1152]{1,0:T(8,128)(2,1)} collective-permute-done((bf16[512,1152]{1,0:T(8,128)(2,1)S(1)}, bf16[512,1152]{1,0:T(8,128)(2,1)}, u32[]{:S(2)}, u32[]{:S(2)}) %collective-permute-start.13) | collective-permute-done | bytes 1179680 | tf_op jit(solution)/shard_map/ppermute | solution.py:34
  94.3 3.4 %collective-permute-start.15 = (bf16[512,1152]{1,0:T(8,128)(2,1)}, bf16[512,1152]{1,0:T(8,128)(2,1)}, u32[]{:S(2)}, u32[]{:S(2)}) collective-permute-start(bf16[512,1152]{1,0:T(8,128)(2,1)} %collective-permute-done.13.refs_4_), channel_id=1, source_target_pairs={{1,7},{3,5},{4,2},{6,0},{9,15},{11,13},{12,10},{14,8},{17,23},{19,... | collective-permute-start | bytes 3538952 | tf_op jit(solution)/shard_map/ppermute | solution.py:34
  104.2 3.2 %sums.5.refs_8_ = f32[512,1152]{1,0:T(8,128)S(1)} custom-call(f32[1]{0:T(128)S(6)} %copy.21.refs_0_, f32[1]{0:T(128)S(6)} %copy.22.refs_1_, s32[1]{0:T(128)} %bitcast.refs_2_, bf16[512,1152]{1,0:T(8,128)(2,1)S(1)} %get-tuple-element.40.refs_3_, bf16[512,1152]{1,0:T(8,128)(2,1)} %collective-permute-done.13.refs_4_, f32[512,1152]{1,0:T(8,128)S(1)} %sums.4.refs_5_), custom_call_target="tpu_custom_call" | custom-call | flops 300000000 | bytes 1048576 | tf_op jit(solution)/shard_map/sums/pallas_call | solution.py:233
  107.5 2.7 %collective-permute-done.15.refs_5_ = bf16[512,1152]{1,0:T(8,128)(2,1)} collective-permute-done((bf16[512,1152]{1,0:T(8,128)(2,1)}, bf16[512,1152]{1,0:T(8,128)(2,1)}, u32[]{:S(2)}, u32[]{:S(2)}) %collective-permute-start.15) | collective-permute-done | bytes 1179680 | tf_op jit(solution)/shard_map/ppermute | solution.py:34
  110.1 6.8 %finish.1 = (bf16[512,1152]{1,0:T(8,128)(2,1)S(1)}, bf16[288,512]{1,0:T(8,128)(2,1)S(1)}, bf16[288,512]{1,0:T(8,128)(2,1)S(1)}, bf16[288,512]{1,0:T(8,128)(2,1)S(1)}, bf16[288,512]{1,0:T(8,128)(2,1)S(1)}) custom-call(f32[1]{0:T(128)S(6)} %copy.21.refs_0_, f32[1]{0:T(128)S(6)} %copy.22.refs_1_, s32[1]{0:T(128)} %bitcast.refs_2_, ...), custom_call_target="tpu_custom_call" | custom-call | flops 300000000 | bytes 1048576 | tf_op jit(solution)/shard_map/finish/pallas_call | solution.py:233
  117.9 1.9 %collective-permute-start.19 = (bf16[288,512]{1,0:T(8,128)(2,1)S(1)}, bf16[288,512]{1,0:T(8,128)(2,1)S(1)}, u32[]{:S(2)}, u32[]{:S(2)}) collective-permute-start(bf16[288,512]{1,0:T(8,128)(2,1)S(1)} %get-tuple-element.51), channel_id=1, source_target_pairs={{0,96},{1,97},{2,98},{3,99},{4,100},{5,101},{6,102},{7,103},{8,104... | collective-permute-start | bytes 884744 | tf_op jit(solution)/shard_map/ppermute | solution.py:34
  121.7 2.5 %collective-permute-done.20.refs_3_ = bf16[288,512]{1,0:T(8,128)(2,1)S(1)} collective-permute-done((bf16[288,512]{1,0:T(8,128)(2,1)S(1)}, bf16[288,512]{1,0:T(8,128)(2,1)S(1)}, u32[]{:S(2)}, u32[]{:S(2)}) %collective-permute-start.20) | collective-permute-done | bytes 294944 | tf_op jit(solution)/shard_map/ppermute | solution.py:34
  124.2 2.9 %collective-permute-done.18.refs_1_ = bf16[288,512]{1,0:T(8,128)(2,1)S(1)} collective-permute-done((bf16[288,512]{1,0:T(8,128)(2,1)S(1)}, bf16[288,512]{1,0:T(8,128)(2,1)S(1)}, u32[]{:S(2)}, u32[]{:S(2)}) %collective-permute-start.18) | collective-permute-done | bytes 294944 | tf_op jit(solution)/shard_map/ppermute | solution.py:34
  128.9 11.3 %collective-permute-start.23 = (bf16[72,1152]{1,0:T(8,128)(2,1)S(1)}, bf16[72,1152]{1,0:T(8,128)(2,1)S(1)}, u32[]{:S(2)}, u32[]{:S(2)}) collective-permute-start(bf16[72,1152]{1,0:T(8,128)(2,1)S(1)} %get-tuple-element.58), channel_id=1, source_target_pairs={{0,4},{1,5},{2,6},{3,7},{4,0},{5,1},{6,2},{7,3},{8,12},{9,13},{10,... | collective-permute-start | bytes 497672 | tf_op jit(solution)/shard_map/ppermute | solution.py:34
  140.2 2.4 %collective-permute-start.24 = (bf16[72,1152]{1,0:T(8,128)(2,1)S(1)}, bf16[72,1152]{1,0:T(8,128)(2,1)S(1)}, u32[]{:S(2)}, u32[]{:S(2)}) collective-permute-start(bf16[72,1152]{1,0:T(8,128)(2,1)S(1)} %get-tuple-element.59), channel_id=1, source_target_pairs={{0,2},{1,3},{2,0},{3,1},{4,6},{5,7},{6,4},{7,5},{8,10},{9,11},{10,... | collective-permute-start | bytes 497672 | tf_op jit(solution)/shard_map/ppermute | solution.py:34
  144.5 5.6 %collective-permute-done.24 = bf16[72,1152]{1,0:T(8,128)(2,1)S(1)} collective-permute-done((bf16[72,1152]{1,0:T(8,128)(2,1)S(1)}, bf16[72,1152]{1,0:T(8,128)(2,1)S(1)}, u32[]{:S(2)}, u32[]{:S(2)}) %collective-permute-start.24) | collective-permute-done | bytes 165920 | tf_op jit(solution)/shard_map/ppermute | solution.py:34
  150.3 2.7 %collective-permute-start.29 = (bf16[72,1152]{1,0:T(8,128)(2,1)S(1)}, bf16[72,1152]{1,0:T(8,128)(2,1)S(1)}, u32[]{:S(2)}, u32[]{:S(2)}) collective-permute-start(bf16[72,1152]{1,0:T(8,128)(2,1)S(1)} %fusion), channel_id=1, source_target_pairs={{0,24},{1,25},{2,26},{3,27},{4,28},{5,29},{6,30},{7,31},{8,0},{9,1... | collective-permute-start | bytes 497672 | tf_op jit(solution)/shard_map/ppermute | solution.py:34
  153.0 3.0 %collective-permute-done.27 = bf16[72,1152]{1,0:T(8,128)(2,1)S(1)} collective-permute-done((bf16[72,1152]{1,0:T(8,128)(2,1)S(1)}, bf16[72,1152]{1,0:T(8,128)(2,1)S(1)}, u32[]{:S(2)}, u32[]{:S(2)}) %collective-permute-start.27) | collective-permute-done | bytes 165920 | tf_op jit(solution)/shard_map/ppermute | solution.py:34
  156.0 5.0 %collective-permute-done.28 = bf16[72,1152]{1,0:T(8,128)(2,1)S(1)} collective-permute-done((bf16[72,1152]{1,0:T(8,128)(2,1)S(1)}, bf16[72,1152]{1,0:T(8,128)(2,1)S(1)}, u32[]{:S(2)}, u32[]{:S(2)}) %collective-permute-start.28) | collective-permute-done | bytes 165920 | tf_op jit(solution)/shard_map/ppermute | solution.py:34
  162.0 3.2 %collective-permute-start.31 = (bf16[72,1152]{1,0:T(8,128)(2,1)S(1)}, bf16[72,1152]{1,0:T(8,128)(2,1)S(1)}, u32[]{:S(2)}, u32[]{:S(2)}) collective-permute-start(bf16[72,1152]{1,0:T(8,128)(2,1)S(1)} %add_convert_fusion), channel_id=1, source_target_pairs={{1,4},{3,6},{4,1},{6,3},{9,12},{11,14},{12,9},{14,11},{17,20},{19,... | collective-permute-start | bytes 497672 | tf_op jit(solution)/shard_map/ppermute | solution.py:34
  167.0 3.2 %collective-permute-done.31 = bf16[72,1152]{1,0:T(8,128)(2,1)S(1)} collective-permute-done((bf16[72,1152]{1,0:T(8,128)(2,1)S(1)}, bf16[72,1152]{1,0:T(8,128)(2,1)S(1)}, u32[]{:S(2)}, u32[]{:S(2)}) %collective-permute-start.31) | collective-permute-done | bytes 165920 | tf_op jit(solution)/shard_map/ppermute | solution.py:34
  171.8 8.4 %collective-permute-done.32 = bf16[2,72,1152]{2,1,0:T(8,128)(2,1)S(1)} collective-permute-done((bf16[2,72,1152]{2,1,0:T(8,128)(2,1)S(1)}, bf16[2,72,1152]{2,1,0:T(8,128)(2,1)S(1)}, u32[]{:S(2)}, u32[]{:S(2)}) %collective-permute-start.32) | collective-permute-done | bytes 331808 | tf_op jit(solution)/shard_map/ppermute | solution.py:34
  182.0 4.9 %collective-permute-done.34 = bf16[2,72,1152]{2,1,0:T(8,128)(2,1)S(1)} collective-permute-done((bf16[2,72,1152]{2,1,0:T(8,128)(2,1)S(1)}, bf16[2,72,1152]{2,1,0:T(8,128)(2,1)S(1)}, u32[]{:S(2)}, u32[]{:S(2)}) %collective-permute-start.34) | collective-permute-done | bytes 331808 | tf_op jit(solution)/shard_map/ppermute | solution.py:34
  (115 shorter events, 44.1 us)
Async XLA Ops:
  4.6 18.0 %collective-permute-start.2 = (bf16[288,1152]{1,0:T(8,128)(2,1)S(1)}, bf16[288,1152]{1,0:T(8,128)(2,1)S(1)}, u32[]{:S(2)}, u32[]{:S(2)}) collective-permute-start(bf16[288,1152]{1,0:T(8,128)(2,1)S(1)} %get-tuple-element.35.refs_0_), channel_id=1, source_target_pairs={{0,2},{1,3},{2,4},{3,5},{4,6},{5,7},{6,0},{7,1},{8,10},{9,11},{10,... | collective-permute-start | bytes 1990664 | tf_op jit(solution)/shard_map/ppermute | solution.py:34
  6.0 17.4 %collective-permute-start.3 = (bf16[288,1152]{1,0:T(8,128)(2,1)}, bf16[288,1152]{1,0:T(8,128)(2,1)S(1)}, u32[]{:S(2)}, u32[]{:S(2)}) collective-permute-start(bf16[288,1152]{1,0:T(8,128)(2,1)} %get-tuple-element.37), channel_id=1, source_target_pairs={{0,7},{1,6},{2,1},{3,0},{4,3},{5,2},{6,5},{7,4},{8,15},{9,14},{10,... | collective-permute-start | bytes 1990664 | tf_op jit(solution)/shard_map/ppermute | solution.py:34
  7.5 15.9 %collective-permute-start.1 = (bf16[288,1152]{1,0:T(8,128)(2,1)}, bf16[288,1152]{1,0:T(8,128)(2,1)}, u32[]{:S(2)}, u32[]{:S(2)}) collective-permute-start(bf16[288,1152]{1,0:T(8,128)(2,1)} %get-tuple-element.37), channel_id=1, source_target_pairs={{0,1},{1,0},{2,3},{3,2},{4,5},{5,4},{6,7},{7,6},{8,9},{9,8},{10,11... | collective-permute-start | bytes 1990664 | tf_op jit(solution)/shard_map/ppermute | solution.py:34
  9.1 30.0 %collective-permute-start.5 = (bf16[512,1152]{1,0:T(8,128)(2,1)S(1)}, bf16[512,1152]{1,0:T(8,128)(2,1)S(1)}, u32[]{:S(2)}, u32[]{:S(2)}) collective-permute-start(bf16[512,1152]{1,0:T(8,128)(2,1)S(1)} %pad_maximum_fusion.refs_4_), channel_id=1, source_target_pairs={{0,32},{1,33},{2,34},{3,35},{4,36},{5,37},{6,38},{7,39},{8,40},{9,... | collective-permute-start | bytes 3538952 | tf_op jit(solution)/shard_map/ppermute | solution.py:34
  10.8 28.3 %collective-permute-start.6 = (bf16[512,1152]{1,0:T(8,128)(2,1)S(1)}, bf16[512,1152]{1,0:T(8,128)(2,1)S(1)}, u32[]{:S(2)}, u32[]{:S(2)}) collective-permute-start(bf16[512,1152]{1,0:T(8,128)(2,1)S(1)} %pad_maximum_fusion.refs_4_), channel_id=1, source_target_pairs={{0,96},{1,97},{2,98},{3,99},{4,100},{5,101},{6,102},{7,103},{8,104... | collective-permute-start | bytes 3538952 | tf_op jit(solution)/shard_map/ppermute | solution.py:34
  32.7 6.4 %collective-permute-start.4 = (bf16[512,1152]{1,0:T(8,128)(2,1)S(1)}, bf16[512,1152]{1,0:T(8,128)(2,1)S(1)}, u32[]{:S(2)}, u32[]{:S(2)}) collective-permute-start(bf16[512,1152]{1,0:T(8,128)(2,1)S(1)} %get-tuple-element.40.refs_3_), channel_id=1, source_target_pairs={{0,1},{1,0},{2,3},{3,2},{4,5},{5,4},{6,7},{7,6},{8,9},{9,8},{10,11... | collective-permute-start | bytes 3538952 | tf_op jit(solution)/shard_map/ppermute | solution.py:34
  33.4 16.0 %collective-permute-start.8 = (bf16[512,1152]{1,0:T(8,128)(2,1)S(1)}, bf16[512,1152]{1,0:T(8,128)(2,1)S(1)}, u32[]{:S(2)}, u32[]{:S(2)}) collective-permute-start(bf16[512,1152]{1,0:T(8,128)(2,1)S(1)} %get-tuple-element.40.refs_3_), channel_id=1, source_target_pairs={{1,2},{3,0},{4,7},{6,5},{9,10},{11,8},{12,15},{14,13},{17,18},{19,... | collective-permute-start | bytes 3538952 | tf_op jit(solution)/shard_map/ppermute | solution.py:34
  36.3 16.1 %collective-permute-start.10 = (bf16[512,1152]{1,0:T(8,128)(2,1)S(1)}, bf16[512,1152]{1,0:T(8,128)(2,1)}, u32[]{:S(2)}, u32[]{:S(2)}) collective-permute-start(bf16[512,1152]{1,0:T(8,128)(2,1)S(1)} %get-tuple-element.40.refs_3_), channel_id=1, source_target_pairs={{0,121},{1,8},{2,123},{3,10},{4,125},{5,12},{6,127},{7,14},{8,1},{... | collective-permute-start | bytes 3538952 | tf_op jit(solution)/shard_map/ppermute | solution.py:34
  39.0 20.7 %collective-permute-start.7 = (bf16[512,1152]{1,0:T(8,128)(2,1)S(1)}, bf16[512,1152]{1,0:T(8,128)(2,1)}, u32[]{:S(2)}, u32[]{:S(2)}) collective-permute-start(bf16[512,1152]{1,0:T(8,128)(2,1)S(1)} %get-tuple-element.40.refs_3_), channel_id=1, source_target_pairs={{1,6},{3,4},{4,3},{6,1},{9,14},{11,12},{12,11},{14,9},{17,22},{19,... | collective-permute-start | bytes 3538952 | tf_op jit(solution)/shard_map/ppermute | solution.py:34
  49.3 25.8 %collective-permute-start.9 = (bf16[512,1152]{1,0:T(8,128)(2,1)S(1)}, bf16[512,1152]{1,0:T(8,128)(2,1)}, u32[]{:S(2)}, u32[]{:S(2)}) collective-permute-start(bf16[512,1152]{1,0:T(8,128)(2,1)S(1)} %get-tuple-element.40.refs_3_), channel_id=1, source_target_pairs={{0,3},{2,1},{5,6},{7,4},{8,11},{10,9},{13,14},{15,12},{16,19},{18,... | collective-permute-start | bytes 3538952 | tf_op jit(solution)/shard_map/ppermute | solution.py:34
  52.4 22.7 %collective-permute-start.11 = (bf16[512,1152]{1,0:T(8,128)(2,1)}, bf16[512,1152]{1,0:T(8,128)(2,1)}, u32[]{:S(2)}, u32[]{:S(2)}) collective-permute-start(bf16[512,1152]{1,0:T(8,128)(2,1)} %collective-permute-done.10.refs_5_), channel_id=1, source_target_pairs={{1,7},{3,5},{4,2},{6,0},{9,15},{11,13},{12,10},{14,8},{17,23},{19,... | collective-permute-start | bytes 3538952 | tf_op jit(solution)/shard_map/ppermute | solution.py:34
  62.1 19.7 %collective-permute-start.14 = (bf16[512,1152]{1,0:T(8,128)(2,1)}, bf16[512,1152]{1,0:T(8,128)(2,1)}, u32[]{:S(2)}, u32[]{:S(2)}) collective-permute-start(bf16[512,1152]{1,0:T(8,128)(2,1)} %broadcast_select_fusion.1.refs_6_), channel_id=1, source_target_pairs={{0,8},{1,121},{2,10},{3,123},{4,12},{5,125},{6,14},{7,127},{8,16},... | collective-permute-start | bytes 3538952 | tf_op jit(solution)/shard_map/ppermute | solution.py:34
  76.6 17.8 %collective-permute-start.13 = (bf16[512,1152]{1,0:T(8,128)(2,1)S(1)}, bf16[512,1152]{1,0:T(8,128)(2,1)}, u32[]{:S(2)}, u32[]{:S(2)}) collective-permute-start(bf16[512,1152]{1,0:T(8,128)(2,1)S(1)} %broadcast_select_fusion.refs_5_), channel_id=1, source_target_pairs={{0,8},{1,121},{2,10},{3,123},{4,12},{5,125},{6,14},{7,127},{8,16},... | collective-permute-start | bytes 3538952 | tf_op jit(solution)/shard_map/ppermute | solution.py:34
  78.5 24.0 %collective-permute-start.12 = (bf16[512,1152]{1,0:T(8,128)(2,1)}, bf16[512,1152]{1,0:T(8,128)(2,1)}, u32[]{:S(2)}, u32[]{:S(2)}) collective-permute-start(bf16[512,1152]{1,0:T(8,128)(2,1)} %broadcast_select_fusion.1.refs_6_), channel_id=1, source_target_pairs={{0,6},{2,4},{5,3},{7,1},{8,14},{10,12},{13,11},{15,9},{16,22},{18,... | collective-permute-start | bytes 3538952 | tf_op jit(solution)/shard_map/ppermute | solution.py:34
  81.8 20.7 %collective-permute-start.16 = (bf16[512,1152]{1,0:T(8,128)(2,1)}, bf16[512,1152]{1,0:T(8,128)(2,1)}, u32[]{:S(2)}, u32[]{:S(2)}) collective-permute-start(bf16[512,1152]{1,0:T(8,128)(2,1)} %collective-permute-done.14.refs_4_), channel_id=1, source_target_pairs={{1,3},{3,1},{4,6},{6,4},{9,11},{11,9},{12,14},{14,12},{17,19},{19,... | collective-permute-start | bytes 3538952 | tf_op jit(solution)/shard_map/ppermute | solution.py:34
  94.3 15.8 %collective-permute-start.15 = (bf16[512,1152]{1,0:T(8,128)(2,1)}, bf16[512,1152]{1,0:T(8,128)(2,1)}, u32[]{:S(2)}, u32[]{:S(2)}) collective-permute-start(bf16[512,1152]{1,0:T(8,128)(2,1)} %collective-permute-done.13.refs_4_), channel_id=1, source_target_pairs={{1,7},{3,5},{4,2},{6,0},{9,15},{11,13},{12,10},{14,8},{17,23},{19,... | collective-permute-start | bytes 3538952 | tf_op jit(solution)/shard_map/ppermute | solution.py:34
  97.8 12.4 %collective-permute-start.17 = (bf16[512,1152]{1,0:T(8,128)(2,1)}, bf16[512,1152]{1,0:T(8,128)(2,1)}, u32[]{:S(2)}, u32[]{:S(2)}) collective-permute-start(bf16[512,1152]{1,0:T(8,128)(2,1)} %collective-permute-done.13.refs_4_), channel_id=1, source_target_pairs={{0,2},{2,0},{5,7},{7,5},{8,10},{10,8},{13,15},{15,13},{16,18},{18,... | collective-permute-start | bytes 3538952 | tf_op jit(solution)/shard_map/ppermute | solution.py:34
  102.6 24.6 %collective-permute-start.22 = (bf16[256,1152]{1,0:T(8,128)(2,1)S(1)}, bf16[256,1152]{1,0:T(8,128)(2,1)S(1)}, u32[]{:S(2)}, u32[]{:S(2)}) collective-permute-start(bf16[256,1152]{1,0:T(8,128)(2,1)S(1)} %slice.28), channel_id=1, source_target_pairs={{0,96},{1,97},{2,98},{3,99},{4,100},{5,101},{6,102},{7,103},{8,104... | collective-permute-start | bytes 1769480 | tf_op jit(solution)/shard_map/ppermute | solution.py:34
  103.0 24.2 %collective-permute-start.21 = (bf16[256,1152]{1,0:T(8,128)(2,1)S(1)}, bf16[256,1152]{1,0:T(8,128)(2,1)S(1)}, u32[]{:S(2)}, u32[]{:S(2)}) collective-permute-start(bf16[256,1152]{1,0:T(8,128)(2,1)S(1)} %slice.27), channel_id=1, source_target_pairs={{0,32},{1,33},{2,34},{3,35},{4,36},{5,37},{6,38},{7,39},{8,40},{9,... | collective-permute-start | bytes 1769480 | tf_op jit(solution)/shard_map/ppermute | solution.py:34
  116.9 7.3 %collective-permute-start.20 = (bf16[288,512]{1,0:T(8,128)(2,1)S(1)}, bf16[288,512]{1,0:T(8,128)(2,1)S(1)}, u32[]{:S(2)}, u32[]{:S(2)}) collective-permute-start(bf16[288,512]{1,0:T(8,128)(2,1)S(1)} %get-tuple-element.52), channel_id=1, source_target_pairs={{0,64},{1,65},{2,66},{3,67},{4,68},{5,69},{6,70},{7,71},{8,72},{9,... | collective-permute-start | bytes 884744 | tf_op jit(solution)/shard_map/ppermute | solution.py:34
  117.2 9.9 %collective-permute-start.18 = (bf16[288,512]{1,0:T(8,128)(2,1)S(1)}, bf16[288,512]{1,0:T(8,128)(2,1)S(1)}, u32[]{:S(2)}, u32[]{:S(2)}) collective-permute-start(bf16[288,512]{1,0:T(8,128)(2,1)S(1)} %get-tuple-element.50), channel_id=1, source_target_pairs={{0,32},{1,33},{2,34},{3,35},{4,36},{5,37},{6,38},{7,39},{8,40},{9,... | collective-permute-start | bytes 884744 | tf_op jit(solution)/shard_map/ppermute | solution.py:34
  117.9 9.2 %collective-permute-start.19 = (bf16[288,512]{1,0:T(8,128)(2,1)S(1)}, bf16[288,512]{1,0:T(8,128)(2,1)S(1)}, u32[]{:S(2)}, u32[]{:S(2)}) collective-permute-start(bf16[288,512]{1,0:T(8,128)(2,1)S(1)} %get-tuple-element.51), channel_id=1, source_target_pairs={{0,96},{1,97},{2,98},{3,99},{4,100},{5,101},{6,102},{7,103},{8,104... | collective-permute-start | bytes 884744 | tf_op jit(solution)/shard_map/ppermute | solution.py:34
  128.9 15.6 %collective-permute-start.23 = (bf16[72,1152]{1,0:T(8,128)(2,1)S(1)}, bf16[72,1152]{1,0:T(8,128)(2,1)S(1)}, u32[]{:S(2)}, u32[]{:S(2)}) collective-permute-start(bf16[72,1152]{1,0:T(8,128)(2,1)S(1)} %get-tuple-element.58), channel_id=1, source_target_pairs={{0,4},{1,5},{2,6},{3,7},{4,0},{5,1},{6,2},{7,3},{8,12},{9,13},{10,... | collective-permute-start | bytes 497672 | tf_op jit(solution)/shard_map/ppermute | solution.py:34
  140.2 9.9 %collective-permute-start.24 = (bf16[72,1152]{1,0:T(8,128)(2,1)S(1)}, bf16[72,1152]{1,0:T(8,128)(2,1)S(1)}, u32[]{:S(2)}, u32[]{:S(2)}) collective-permute-start(bf16[72,1152]{1,0:T(8,128)(2,1)S(1)} %get-tuple-element.59), channel_id=1, source_target_pairs={{0,2},{1,3},{2,0},{3,1},{4,6},{5,7},{6,4},{7,5},{8,10},{9,11},{10,... | collective-permute-start | bytes 497672 | tf_op jit(solution)/shard_map/ppermute | solution.py:34
  142.6 7.5 %collective-permute-start.25 = (bf16[72,1152]{1,0:T(8,128)(2,1)S(1)}, bf16[72,1152]{1,0:T(8,128)(2,1)S(1)}, u32[]{:S(2)}, u32[]{:S(2)}) collective-permute-start(bf16[72,1152]{1,0:T(8,128)(2,1)S(1)} %get-tuple-element.60), channel_id=1, source_target_pairs={{0,6},{1,7},{2,4},{3,5},{4,2},{5,3},{6,0},{7,1},{8,14},{9,15},{10,... | collective-permute-start | bytes 497672 | tf_op jit(solution)/shard_map/ppermute | solution.py:34
  142.6 7.5 %collective-permute-start.26 = (bf16[256,1152]{1,0:T(8,128)(2,1)S(1)}, bf16[256,1152]{1,0:T(8,128)(2,1)S(1)}, u32[]{:S(2)}, u32[]{:S(2)}) collective-permute-start(bf16[256,1152]{1,0:T(8,128)(2,1)S(1)} %slice.23), channel_id=1, source_target_pairs={{0,1},{1,0},{2,3},{3,2},{4,5},{5,4},{6,7},{7,6},{8,9},{9,8},{10,11... | collective-permute-start | bytes 1769480 | tf_op jit(solution)/shard_map/ppermute | solution.py:34
  150.2 10.8 %collective-permute-start.28 = (bf16[72,1152]{1,0:T(8,128)(2,1)S(1)}, bf16[72,1152]{1,0:T(8,128)(2,1)S(1)}, u32[]{:S(2)}, u32[]{:S(2)}) collective-permute-start(bf16[72,1152]{1,0:T(8,128)(2,1)S(1)} %fusion), channel_id=1, source_target_pairs={{0,8},{1,9},{2,10},{3,11},{4,12},{5,13},{6,14},{7,15},{8,16},{9,17... | collective-permute-start | bytes 497672 | tf_op jit(solution)/shard_map/ppermute | solution.py:34
  150.3 10.7 %collective-permute-start.29 = (bf16[72,1152]{1,0:T(8,128)(2,1)S(1)}, bf16[72,1152]{1,0:T(8,128)(2,1)S(1)}, u32[]{:S(2)}, u32[]{:S(2)}) collective-permute-start(bf16[72,1152]{1,0:T(8,128)(2,1)S(1)} %fusion), channel_id=1, source_target_pairs={{0,24},{1,25},{2,26},{3,27},{4,28},{5,29},{6,30},{7,31},{8,0},{9,1... | collective-permute-start | bytes 497672 | tf_op jit(solution)/shard_map/ppermute | solution.py:34
  162.0 8.2 %collective-permute-start.31 = (bf16[72,1152]{1,0:T(8,128)(2,1)S(1)}, bf16[72,1152]{1,0:T(8,128)(2,1)S(1)}, u32[]{:S(2)}, u32[]{:S(2)}) collective-permute-start(bf16[72,1152]{1,0:T(8,128)(2,1)S(1)} %add_convert_fusion), channel_id=1, source_target_pairs={{1,4},{3,6},{4,1},{6,3},{9,12},{11,14},{12,9},{14,11},{17,20},{19,... | collective-permute-start | bytes 497672 | tf_op jit(solution)/shard_map/ppermute | solution.py:34
  170.2 10.0 %collective-permute-start.32 = (bf16[2,72,1152]{2,1,0:T(8,128)(2,1)S(1)}, bf16[2,72,1152]{2,1,0:T(8,128)(2,1)S(1)}, u32[]{:S(2)}, u32[]{:S(2)}) collective-permute-start(bf16[2,72,1152]{2,1,0:T(8,128)(2,1)S(1)} %pad_maximum_fusion.1), channel_id=1, source_target_pairs={{0,96},{1,97},{2,98},{3,99},{4,100},{5,101},{6,102},{7,103},{8,104... | collective-permute-start | bytes 995336 | tf_op jit(solution)/shard_map/ppermute | solution.py:34
  170.8 11.1 %collective-permute-start.33 = (bf16[2,72,1152]{2,1,0:T(8,128)(2,1)S(1)}, bf16[2,72,1152]{2,1,0:T(8,128)(2,1)S(1)}, u32[]{:S(2)}, u32[]{:S(2)}) collective-permute-start(bf16[2,72,1152]{2,1,0:T(8,128)(2,1)S(1)} %pad_maximum_fusion.1), channel_id=1, source_target_pairs={{0,64},{1,65},{2,66},{3,67},{4,68},{5,69},{6,70},{7,71},{8,72},{9,... | collective-permute-start | bytes 995336 | tf_op jit(solution)/shard_map/ppermute | solution.py:34
  170.8 16.0 %collective-permute-start.34 = (bf16[2,72,1152]{2,1,0:T(8,128)(2,1)S(1)}, bf16[2,72,1152]{2,1,0:T(8,128)(2,1)S(1)}, u32[]{:S(2)}, u32[]{:S(2)}) collective-permute-start(bf16[2,72,1152]{2,1,0:T(8,128)(2,1)S(1)} %pad_maximum_fusion.1), channel_id=1, source_target_pairs={{0,32},{1,33},{2,34},{3,35},{4,36},{5,37},{6,38},{7,39},{8,40},{9,... | collective-permute-start | bytes 995336 | tf_op jit(solution)/shard_map/ppermute | solution.py:34
  (23 other events, 194.7 us)
